TPU v7x, 32 devices: a whole 2x2x4 slice. The times are simulated.
32 devices in a mesh: section: 2 (over core), dp: 4 (over z), seq: 4 (over y, x).
Axes of the slice: x: 2, y: 2, z: 4, core: 2. Of those that a mesh axis runs over, the one named last changes fastest.
Arguments:
- section_input: bfloat16 [8, 640, 768], P('dp', 'seq'), may hold values from -6 to 6
- out_cotangent: bfloat16 [8, 640, 768], P('dp', 'seq'), may hold values from -6 to 6
- lengths: int32 [8], P('dp'), may hold values from 481 to 577
- attn_gain: bfloat16 [2, 768], P('section'), may hold values from 0.25 to 1.75
- w_query: bfloat16 [2, 768, 768], P('section'), may hold values from -0.21875 to 0.21875
- w_key: bfloat16 [2, 768, 768], P('section'), may hold values from -0.21875 to 0.21875
- w_value: bfloat16 [2, 768, 768], P('section'), may hold values from -0.21875 to 0.21875
- w_output: bfloat16 [2, 768, 768], P('section'), may hold values from -3.5 to 3.5
- ffn_gain: bfloat16 [2, 768], P('section'), may hold values from 0.25 to 1.75
- w_gate: bfloat16 [2, 768, 2048], P('section'), may hold values from -0.21875 to 0.21875
- w_up: bfloat16 [2, 768, 2048], P('section'), may hold values from -0.21875 to 0.21875
- w_down: bfloat16 [2, 2048, 768], P('section'), may hold values from -0.125 to 0.125
Outputs:
- section_outputs: bfloat16 [2, 8, 640, 768], P('section', 'dp', 'seq')
- input_grads: bfloat16 [2, 8, 640, 768], P('section', 'dp', 'seq')
- grad_attn_gain: float32 [2, 768], P('section', ('dp', 'seq'))
- grad_query: float32 [2, 768, 768], P('section', 'dp', 'seq')
- grad_key: float32 [2, 768, 768], P('section', 'dp', 'seq')
- grad_value: float32 [2, 768, 768], P('section', 'dp', 'seq')
- grad_output: float32 [2, 768, 768], P('section', 'dp', 'seq')
- grad_ffn_gain: float32 [2, 768], P('section', ('dp', 'seq'))
- grad_gate: float32 [2, 768, 2048], P('section', 'dp', 'seq')
- grad_up: float32 [2, 768, 2048], P('section', 'dp', 'seq')
- grad_down: float32 [2, 2048, 768], P('section', 'dp', 'seq')
All inputs are finite; a program needn't handle non-finite values.
Results may differ from a plain program's by a relative error of at most 0.025.
Values may be sent and summed in bfloat16 or wider, within the bound.
No kernel may reach another device: no remote copies, remote signals or barrier semaphores. Data moves between devices by JAX's collectives and lax.ppermute only.
A program may use at most 192 MiB of HBM per device.

v0:
```python
import jax
import jax.numpy as jnp
from jax import lax
from jax.sharding import PartitionSpec as P

HEADS = 12
HEAD_DIM = 64


epsilon = 1e-05
masked_score = -1e30


def shifted(value, axis, steps):
    count = lax.axis_size(axis)
    leading, last = (max(0, -steps), min(count, count - steps))
    return lax.ppermute(value, axis, [(source, source + steps) for source in range(leading, last)])


def rms_scale(inputs):
    return lax.rsqrt(jnp.mean(inputs * inputs, axis=-1, keepdims=True) + epsilon)


def rotary_tables(count_rows, first_slot, head_dim):
    half_dim = head_dim // 2
    frequency = 10000.0 ** (-2.0 * jnp.arange(half_dim, dtype=jnp.float32) / head_dim)
    places = (first_slot + jnp.arange(count_rows, dtype=jnp.int32)).astype(jnp.float32)
    angles = places[:, None] * frequency[None, :]
    return (jnp.cos(angles), jnp.sin(angles))


def rotate(inputs, cosine, sine_table, direction):
    half_dim = inputs.shape[-1] // 2
    first_half = inputs[..., :half_dim]
    second_half = inputs[..., half_dim:]
    cos_wide = cosine[None, :, None, :]
    sin_wide = direction * sine_table[None, :, None, :]
    return jnp.concatenate(
        [
            first_half * cos_wide - second_half * sin_wide,
            first_half * sin_wide + second_half * cos_wide,
        ],
        axis=-1,
    )


def linear(inputs, matrix):
    return jnp.einsum("bsd,de->bse", inputs, matrix, preferred_element_type=jnp.float32)


def linear_back(inputs, matrix):
    return jnp.einsum("bse,de->bsd", inputs, matrix, preferred_element_type=jnp.float32)


def outer_sum(inputs, others):
    return jnp.einsum("bsd,bse->de", inputs, others, preferred_element_type=jnp.float32)


def norm_back(grad_normed, gain_row, normed, scale_rows):
    scaled = grad_normed * gain_row
    return scale_rows * (scaled - normed * jnp.mean(scaled * normed, axis=-1, keepdims=True))


def query_key_value(inputs, params, cosine, sine_table):
    attn_gain, w_query, w_key, w_value = params[:4]
    batch_size, slot_count = (inputs.shape[0], inputs.shape[1])
    heads_shape = (batch_size, slot_count, HEADS, HEAD_DIM)
    scale_one = rms_scale(inputs)
    normed = inputs * scale_one
    normed_low = (normed * attn_gain).astype(jnp.bfloat16)
    queries = rotate(
        linear(normed_low, w_query).reshape(heads_shape), cosine, sine_table, 1.0
    ).astype(jnp.bfloat16)
    key_rot = rotate(linear(normed_low, w_key).reshape(heads_shape), cosine, sine_table, 1.0)
    key_low = key_rot.reshape(batch_size, slot_count, -1).astype(jnp.bfloat16)
    value_low = linear(normed_low, w_value).astype(jnp.bfloat16)
    return (scale_one, normed, normed_low, queries, key_low, value_low)


def attention_weights(queries, keys_all, length, first_slot):
    batch_size, slot_count = (queries.shape[0], queries.shape[1])
    key_count = keys_all.shape[1]
    key_heads = keys_all.reshape(batch_size, key_count, HEADS, HEAD_DIM)
    scores = jnp.einsum(
        "bqhd,bkhd->bhqk", queries, key_heads, preferred_element_type=jnp.float32
    ) * HEAD_DIM ** (-0.5)
    query_places = first_slot + jnp.arange(slot_count, dtype=jnp.int32)
    key_places = jnp.arange(key_count, dtype=jnp.int32)
    allowed = (key_places[None, :] <= query_places[:, None]) & (key_places[None, :] < length)
    scores = jnp.where(allowed[None, None], scores, masked_score)
    row_max = jnp.max(scores, axis=-1, keepdims=True)
    exponent = jnp.exp(scores - row_max)
    return exponent / jnp.sum(exponent, axis=-1, keepdims=True)


def layer_rest(inputs, params, attention, values_all):
    w_output, ffn_gain, w_gate, w_up, w_down = params[4:]
    batch_size, slot_count = (inputs.shape[0], inputs.shape[1])
    value_heads = values_all.reshape(batch_size, values_all.shape[1], HEADS, HEAD_DIM)
    attention_low = attention.astype(jnp.bfloat16)
    mixed = jnp.einsum(
        "bhqk,bkhd->bqhd", attention_low, value_heads, preferred_element_type=jnp.float32
    )
    mixed_low = mixed.reshape(batch_size, slot_count, -1).astype(jnp.bfloat16)
    after_attn = inputs + linear(mixed_low, w_output)
    scale_two = rms_scale(after_attn)
    normed_two = after_attn * scale_two
    normed_two_low = (normed_two * ffn_gain).astype(jnp.bfloat16)
    gate_proj = linear(normed_two_low, w_gate)
    up_proj = linear(normed_two_low, w_up)
    sigmoid_gate = jax.nn.sigmoid(gate_proj)
    hidden_low = (gate_proj * sigmoid_gate * up_proj).astype(jnp.bfloat16)
    result = after_attn + linear(hidden_low, w_down)
    return (
        result,
        (
            attention_low,
            value_heads,
            mixed_low,
            scale_two,
            normed_two,
            normed_two_low,
            gate_proj,
            up_proj,
            sigmoid_gate,
            hidden_low,
        ),
    )


def ffn_backward(inputs, grad_out, params, length, first_slot, projected, keys_all, values_all):
    w_output, ffn_gain, w_gate, w_up, w_down = params[4:]
    queries = projected[3]
    attention = attention_weights(queries, keys_all, length, first_slot)
    result, kept = layer_rest(inputs, params, attention, values_all)
    (
        attention_low,
        value_heads,
        mixed_low,
        scale_two,
        normed_two,
        normed_two_low,
        gate_proj,
        up_proj,
        sigmoid_gate,
        hidden_low,
    ) = kept
    grad_ffn_out = grad_out.astype(jnp.bfloat16)
    grad_hidden = linear_back(grad_ffn_out, w_down)
    grad_gate = (
        grad_hidden * up_proj * sigmoid_gate * (1.0 + gate_proj * (1.0 - sigmoid_gate))
    ).astype(jnp.bfloat16)
    grad_up = (grad_hidden * gate_proj * sigmoid_gate).astype(jnp.bfloat16)
    grad_norm_two = linear_back(grad_gate, w_gate) + linear_back(grad_up, w_up)
    g_ffn_gain = jnp.sum(grad_norm_two * normed_two, axis=(0, 1))
    grad_mid = grad_out + norm_back(grad_norm_two, ffn_gain, normed_two, scale_two)
    grad_branch = grad_mid.astype(jnp.bfloat16)
    rows_all = (
        lax.all_gather(mixed_low, "seq", axis=1, tiled=True),
        lax.all_gather(normed_two_low, "seq", axis=1, tiled=True),
        lax.all_gather(hidden_low, "seq", axis=1, tiled=True),
    )
    cols_all = (
        lax.all_to_all(grad_branch, "seq", split_axis=2, concat_axis=1, tiled=True),
        lax.all_to_all(grad_gate, "seq", split_axis=2, concat_axis=1, tiled=True),
        lax.all_to_all(grad_up, "seq", split_axis=2, concat_axis=1, tiled=True),
        lax.all_to_all(grad_ffn_out, "seq", split_axis=2, concat_axis=1, tiled=True),
    )
    g_output = outer_sum(rows_all[0], cols_all[0])
    g_gate = outer_sum(rows_all[1], cols_all[1])
    g_up = outer_sum(rows_all[1], cols_all[2])
    g_down = outer_sum(rows_all[2], cols_all[3])
    context = (attention, attention_low, value_heads, grad_branch)
    return (grad_mid, (g_output, g_ffn_gain, g_gate, g_up, g_down), context)


def attn_backward(grad_mid, params, cosine, sine_table, projected, keys_all, context):
    attn_gain, w_query, w_key, w_value, w_output = params[:5]
    scale_one, normed, normed_low, queries = projected[:4]
    attention, attention_low, value_heads, grad_branch = context
    batch_size, slot_count = (grad_mid.shape[0], grad_mid.shape[1])
    key_count = keys_all.shape[1]
    grad_mixed = (
        linear_back(grad_branch, w_output)
        .astype(jnp.bfloat16)
        .reshape(batch_size, slot_count, HEADS, HEAD_DIM)
    )
    grad_attention = jnp.einsum(
        "bqhd,bkhd->bhqk", grad_mixed, value_heads, preferred_element_type=jnp.float32
    )
    row_total = jnp.sum(attention * grad_attention, axis=-1, keepdims=True)
    grad_scores = (attention * (grad_attention - row_total)).astype(jnp.bfloat16)
    key_heads = keys_all.reshape(batch_size, key_count, HEADS, HEAD_DIM)
    grad_queries = jnp.einsum(
        "bhqk,bkhd->bqhd", grad_scores, key_heads, preferred_element_type=jnp.float32
    ) * HEAD_DIM ** (-0.5)
    key_terms = jnp.einsum(
        "bhqk,bqhd->bkhd", grad_scores, queries, preferred_element_type=jnp.float32
    ) * HEAD_DIM ** (-0.5)
    value_terms = jnp.einsum(
        "bhqk,bqhd->bkhd", attention_low, grad_mixed, preferred_element_type=jnp.float32
    )
    grad_keys, grad_values = (
        lax.psum_scatter(
            key_terms.reshape(batch_size, key_count, -1).astype(jnp.bfloat16),
            "seq",
            scatter_dimension=1,
            tiled=True,
        ).astype(jnp.float32),
        lax.psum_scatter(
            value_terms.reshape(batch_size, key_count, -1).astype(jnp.bfloat16),
            "seq",
            scatter_dimension=1,
            tiled=True,
        ).astype(jnp.float32),
    )
    grad_query_low = (
        rotate(grad_queries, cosine, sine_table, -1.0)
        .reshape(batch_size, slot_count, -1)
        .astype(jnp.bfloat16)
    )
    grad_key_low = (
        rotate(grad_keys.reshape(batch_size, slot_count, HEADS, HEAD_DIM), cosine, sine_table, -1.0)
        .reshape(batch_size, slot_count, -1)
        .astype(jnp.bfloat16)
    )
    grad_value_low = grad_values.astype(jnp.bfloat16)
    normed_all = lax.all_gather(normed_low, "seq", axis=1, tiled=True)
    cols_all = (
        lax.all_to_all(grad_query_low, "seq", split_axis=2, concat_axis=1, tiled=True),
        lax.all_to_all(grad_key_low, "seq", split_axis=2, concat_axis=1, tiled=True),
        lax.all_to_all(grad_value_low, "seq", split_axis=2, concat_axis=1, tiled=True),
    )
    g_query = outer_sum(normed_all, cols_all[0])
    g_key = outer_sum(normed_all, cols_all[1])
    g_value = outer_sum(normed_all, cols_all[2])
    grad_norm_one = (
        linear_back(grad_query_low, w_query)
        + linear_back(grad_key_low, w_key)
        + linear_back(grad_value_low, w_value)
    )
    g_attn_gain = jnp.sum(grad_norm_one * normed, axis=(0, 1))
    grad_in = grad_mid + norm_back(grad_norm_one, attn_gain, normed, scale_one)
    return (grad_in, (g_attn_gain, g_query, g_key, g_value))


def on_device(
    section_input,
    out_cotangent,
    lengths,
    attn_gain,
    w_query,
    w_key,
    w_value,
    w_output,
    ffn_gain,
    w_gate,
    w_up,
    w_down,
):
    stacked = (attn_gain, w_query, w_key, w_value, w_output, ffn_gain, w_gate, w_up, w_down)
    params = tuple((weight[0] for weight in stacked))
    section_index = lax.axis_index("section")
    is_first = section_index == 0
    micro = section_input.shape[0]
    slot_count = section_input.shape[1]
    seq_count = lax.axis_size("seq")
    first_slot = lax.axis_index("seq") * slot_count
    cosine, sine_table = rotary_tables(slot_count, first_slot, HEAD_DIM)
    inputs_wide = section_input.astype(jnp.float32)
    received = jnp.zeros((1, slot_count, section_input.shape[2]), jnp.float32)
    saved_inputs = []
    results = []
    for tick_index in range(micro + 1):
        own_input = inputs_wide[min(tick_index, micro - 1)][None]
        block_in = jnp.where(is_first, own_input, received)
        item_index = jnp.clip(tick_index - section_index, 0, micro - 1)
        projected = query_key_value(block_in, params, cosine, sine_table)
        keys_all, values_all = (
            lax.all_gather(projected[4], "seq", axis=1, tiled=True),
            lax.all_gather(projected[5], "seq", axis=1, tiled=True),
        )
        attention = attention_weights(projected[3], keys_all, lengths[item_index], first_slot)
        result, unused = layer_rest(block_in, params, attention, values_all)
        result_low = result.astype(jnp.bfloat16)
        received = shifted(result_low, "section", 1).astype(jnp.float32)
        saved_inputs.append(block_in)
        results.append(result_low)
    running = tuple(
        (
            (
                jnp.zeros(weight.shape, jnp.float32)
                if weight.ndim == 1
                else jnp.zeros((weight.shape[0], weight.shape[1] // seq_count), jnp.float32)
            )
            for weight in params
        )
    )
    matrix_shares = None
    back_received = jnp.zeros_like(received)
    grad_inputs = []
    for tick_index in range(micro + 1):
        item_raw = tick_index - 1 + section_index
        valid_scale = ((item_raw >= 0) & (item_raw < micro)).astype(jnp.float32)
        item_index = jnp.clip(item_raw, 0, micro - 1)
        low_tick = max(tick_index - 1, 0)
        high_tick = min(tick_index + 1, micro)
        block_in = jnp.where(is_first, saved_inputs[low_tick], saved_inputs[high_tick])
        own_grad = out_cotangent[min(tick_index, micro - 1)][None].astype(jnp.float32)
        grad_out = jnp.where(is_first, back_received, own_grad)
        projected = query_key_value(block_in, params, cosine, sine_table)
        keys_all, values_all = (
            lax.all_gather(projected[4], "seq", axis=1, tiled=True),
            lax.all_gather(projected[5], "seq", axis=1, tiled=True),
        )
        grad_mid, ffn_terms, context = ffn_backward(
            block_in,
            grad_out,
            params,
            lengths[item_index],
            first_slot,
            projected,
            keys_all,
            values_all,
        )
        ffn_terms = tuple((term * valid_scale for term in ffn_terms))
        ffn_totals = tuple(
            (left_part + right_part for left_part, right_part in zip(running[4:], ffn_terms))
        )
        grad_in, attn_terms = attn_backward(
            grad_mid, params, cosine, sine_table, projected, keys_all, context
        )
        grad_low = grad_in.astype(jnp.bfloat16)
        back_received = shifted(grad_low, "section", -1).astype(jnp.float32)
        grad_inputs.append(grad_low)
        attn_terms = tuple((term * valid_scale for term in attn_terms))
        attn_totals = tuple(
            (left_part + right_part for left_part, right_part in zip(running[:4], attn_terms))
        )
        running = attn_totals + ffn_totals
    matrix_shares = (
        lax.psum_scatter(
            running[1].astype(jnp.bfloat16), "dp", scatter_dimension=0, tiled=True
        ).astype(jnp.float32),
        lax.psum_scatter(
            running[2].astype(jnp.bfloat16), "dp", scatter_dimension=0, tiled=True
        ).astype(jnp.float32),
        lax.psum_scatter(
            running[3].astype(jnp.bfloat16), "dp", scatter_dimension=0, tiled=True
        ).astype(jnp.float32),
        lax.psum_scatter(
            running[4].astype(jnp.bfloat16), "dp", scatter_dimension=0, tiled=True
        ).astype(jnp.float32),
        lax.psum_scatter(
            running[6].astype(jnp.bfloat16), "dp", scatter_dimension=0, tiled=True
        ).astype(jnp.float32),
        lax.psum_scatter(
            running[7].astype(jnp.bfloat16), "dp", scatter_dimension=0, tiled=True
        ).astype(jnp.float32),
        lax.psum_scatter(
            running[8].astype(jnp.bfloat16), "dp", scatter_dimension=0, tiled=True
        ).astype(jnp.float32),
    )
    gain_shares = (
        lax.psum_scatter(running[0], ("dp", "seq"), scatter_dimension=0, tiled=True),
        lax.psum_scatter(running[5], ("dp", "seq"), scatter_dimension=0, tiled=True),
    )
    section_outputs = jnp.concatenate(
        [
            jnp.where(is_first, results[index_mb], results[index_mb + 1])
            for index_mb in range(micro)
        ],
        axis=0,
    )[None]
    input_grads = jnp.concatenate(
        [
            jnp.where(is_first, grad_inputs[index_mb + 1], grad_inputs[index_mb])
            for index_mb in range(micro)
        ],
        axis=0,
    )[None]
    return (
        section_outputs,
        input_grads,
        gain_shares[0][None],
        matrix_shares[0][None],
        matrix_shares[1][None],
        matrix_shares[2][None],
        matrix_shares[3][None],
        gain_shares[1][None],
        matrix_shares[4][None],
        matrix_shares[5][None],
        matrix_shares[6][None],
    )


def solution(mesh):
    return jax.shard_map(
        on_device,
        mesh=mesh,
        in_specs=(
            P("dp", "seq", None),
            P("dp", "seq", None),
            P("dp"),
            P("section", None),
            P("section", None, None),
            P("section", None, None),
            P("section", None, None),
            P("section", None, None),
            P("section", None),
            P("section", None, None),
            P("section", None, None),
            P("section", None, None),
        ),
        out_specs=(
            P("section", "dp", "seq", None),
            P("section", "dp", "seq", None),
            P("section", ("dp", "seq")),
            P("section", "dp", "seq"),
            P("section", "dp", "seq"),
            P("section", "dp", "seq"),
            P("section", "dp", "seq"),
            P("section", ("dp", "seq")),
            P("section", "dp", "seq"),
            P("section", "dp", "seq"),
            P("section", "dp", "seq"),
        ),
        check_vma=False,
    )
```

profile of v0, /device:TPU:0, one launch (start us, length us, event | category | flops | bytes accessed | tf_op | source)
XLA Modules:
  0.0 1423.5 jit_solution(5181154661690189075)
XLA Ops:
  9.5 15.8 %all-gather = bf16[640,768]{1,0:T(8,128)(2,1)} all-gather(bf16[160,768]{1,0:T(8,128)(2,1)S(1)} %convolution_convert_fusion.14), channel_id=2, replica_groups=mesh['section'=2,'dp'=4,'seq'=4] {'seq'}, dimensions={0}, use_global_device_ids=true | all-gather | bytes 1228800 | tf_op jit(solution)/shard_map/all_gather | solution.py:281
  86.0 14.8 %all-gather.1 = bf16[640,768]{1,0:T(8,128)(2,1)} all-gather(bf16[160,768]{1,0:T(8,128)(2,1)S(1)} %convolution_convert_fusion.13), channel_id=3, replica_groups=mesh['section'=2,'dp'=4,'seq'=4] {'seq'}, dimensions={0}, use_global_device_ids=true | all-gather | bytes 1228800 | tf_op jit(solution)/shard_map/all_gather | solution.py:281
  108.1 12.8 all_gather.75
  162.2 13.3 all_gather.79
  177.7 14.4 %all-gather.3 = bf16[640,768]{1,0:T(8,128)(2,1)} all-gather(bf16[160,768]{1,0:T(8,128)(2,1)} %convolution_convert_fusion.11), channel_id=5, replica_groups=mesh['section'=2,'dp'=4,'seq'=4] {'seq'}, dimensions={0}, use_global_device_ids=true | all-gather | bytes 1228800 | tf_op jit(solution)/shard_map/all_gather | solution.py:314
  247.2 13.1 all_gather.83
  275.5 16.5 %all-gather.4 = bf16[640,768]{1,0:T(8,128)(2,1)} all-gather(bf16[160,768]{1,0:T(8,128)(2,1)} %convolution_convert_fusion.9), channel_id=6, replica_groups=mesh['section'=2,'dp'=4,'seq'=4] {'seq'}, dimensions={0}, use_global_device_ids=true | all-gather | bytes 1228800 | tf_op jit(solution)/shard_map/all_gather | solution.py:314
  421.1 18.6 %all_gather.87 = bf16[1,640,768]{2,1,0:T(8,128)(2,1)} all-gather(bf16[1,160,768]{2,1,0:T(8,128)(2,1)} %copy.238), channel_id=1, replica_groups=mesh['section'=2,'dp'=4,'seq'=4] {'seq'}, dimensions={1}, use_global_device_ids=true | all-gather | bytes 1228800 | tf_op jit(solution)/shard_map/all_gather | solution.py:159
  439.8 17.1 %all_gather.88 = bf16[1,640,768]{2,1,0:T(8,128)(2,1)} all-gather(bf16[1,160,768]{2,1,0:T(8,128)(2,1)} %copy.242), channel_id=1, replica_groups=mesh['section'=2,'dp'=4,'seq'=4] {'seq'}, dimensions={1}, use_global_device_ids=true | all-gather | bytes 1228800 | tf_op jit(solution)/shard_map/all_gather | solution.py:159
  614.7 21.6 %all-gather.2 = bf16[640,768]{1,0:T(8,128)(2,1)} all-gather(bf16[160,768]{1,0:T(8,128)(2,1)S(1)} %convolution_convert_fusion.12), channel_id=4, replica_groups=mesh['section'=2,'dp'=4,'seq'=4] {'seq'}, dimensions={0}, use_global_device_ids=true | all-gather | bytes 1228800 | tf_op jit(solution)/shard_map/all_gather | solution.py:281
  642.2 17.6 %all_gather.77 = bf16[1,640,768]{2,1,0:T(8,128)(2,1)} all-gather(bf16[1,160,768]{2,1,0:T(8,128)(2,1)} %copy.194), channel_id=1, replica_groups=mesh['section'=2,'dp'=4,'seq'=4] {'seq'}, dimensions={1}, use_global_device_ids=true | all-gather | bytes 1228800 | tf_op jit(solution)/shard_map/all_gather | solution.py:280
  667.9 13.7 reduce.65
  695.3 13.7 reduce.68
  742.7 18.7 %all_gather.84 = bf16[1,640,768]{2,1,0:T(8,128)(2,1)} all-gather(bf16[1,160,768]{2,1,0:T(8,128)(2,1)} %copy-done.55), channel_id=1, replica_groups=mesh['section'=2,'dp'=4,'seq'=4] {'seq'}, dimensions={1}, use_global_device_ids=true | all-gather | bytes 1228800 | tf_op jit(solution)/shard_map/all_gather | solution.py:228
  761.5 17.9 %all_gather.85 = bf16[1,640,768]{2,1,0:T(8,128)(2,1)} all-gather(bf16[1,160,768]{2,1,0:T(8,128)(2,1)S(1)} %multiply_convert_fusion.18), channel_id=1, replica_groups=mesh['section'=2,'dp'=4,'seq'=4] {'seq'}, dimensions={1}, use_global_device_ids=true | all-gather | bytes 1228800 | tf_op jit(solution)/shard_map/all_gather | solution.py:228
  792.0 20.3 %all_gather.86 = bf16[1,640,768]{2,1,0:T(8,128)(2,1)} all-gather(bf16[1,160,768]{2,1,0:T(8,128)(2,1)S(1)} %copy-done.54), channel_id=1, replica_groups=mesh['section'=2,'dp'=4,'seq'=4] {'seq'}, dimensions={1}, use_global_device_ids=true | all-gather | bytes 1228800 | tf_op jit(solution)/shard_map/all_gather | solution.py:228
  825.9 14.4 %all_gather.90 = bf16[1,640,768]{2,1,0:T(8,128)(2,1)} all-gather(bf16[1,160,768]{2,1,0:T(8,128)(2,1)S(1)} %copy-done.77), channel_id=1, replica_groups=mesh['section'=2,'dp'=4,'seq'=4] {'seq'}, dimensions={1}, use_global_device_ids=true | all-gather | bytes 1228800 | tf_op jit(solution)/shard_map/all_gather | solution.py:160
  905.0 13.7 reduce.64
  926.3 17.4 %all_gather.91 = bf16[1,640,768]{2,1,0:T(8,128)(2,1)} all-gather(bf16[1,160,768]{2,1,0:T(8,128)(2,1)} %copy-done.88), channel_id=1, replica_groups=mesh['section'=2,'dp'=4,'seq'=4] {'seq'}, dimensions={1}, use_global_device_ids=true | all-gather | bytes 1228800 | tf_op jit(solution)/shard_map/all_gather | solution.py:160
  986.4 13.7 reduce.67
  1069.0 13.6 reduce.66
  1187.5 13.6 reduce.69
  1320.9 42.8 %all-reduce.2 = (f32[768]{0:T(1024)S(1)}, f32[768]{0:T(1024)S(1)}) all-reduce(f32[768]{0:T(1024)S(1)} %multiply_add_fusion.7, f32[768]{0:T(1024)S(1)} %copy-done.127), channel_id=17, replica_groups=mesh['section'=2,'dp'=4,'seq'=4] {'dp','seq'}, use_global_device_ids=true, to_apply=%region_42.43.clone | all-reduce | flops 1536 | bytes 12288
  1392.7 22.3 %reduce-scatter.38.cloned.1.call-done = bf16[512,192]{0,1:T(8,128)(2,1)} async-done(((bf16[2048,192]{0,1:T(8,128)(2,1)}), bf16[512,192]{0,1:T(8,128)(2,1)}) %reduce-scatter.38.cloned.1.call-update) | async-done | bytes 196624 | tf_op jit(solution)/shard_map/reduce_scatter | solution.py:360
  (745 shorter events, 995.3 us)
Async XLA Ops:
  7.2 337.3 %reduce-scatter.40.cloned.1.call-start = ((), (), s32[]{:S(2)}) async-start(), calls=%async_computation.47 | async-start | bytes 1228800
  275.5 82.7 %reduce-scatter.20.cloned.1.call-start = ((), (), s32[]{:S(2)}) async-start(), calls=%async_computation.34 | async-start | bytes 1228800 | tf_op jit(solution)/shard_map/reduce_scatter | solution.py:210
  330.6 166.9 %reduce-scatter.42.cloned.1.call-start = ((), (), s32[]{:S(2)}) async-start(), calls=%async_computation.48 | async-start | bytes 1228800
  394.5 112.6 %reduce-scatter.22.cloned.1.call-start = ((), (), s32[]{:S(2)}) async-start(), calls=%async_computation.35 | async-start | bytes 1228800 | tf_op jit(solution)/shard_map/reduce_scatter | solution.py:210
  411.5 58.0 %all-to-all-start.9 = ((bf16[4,2,15360]{2,1,0:T(2,128)(2,1)}), bf16[4,2,15360]{2,1,0:T(2,128)(2,1)}, u32[]{:S(2)}, u32[]{:S(2)}) async-start(bf16[4,2,15360]{2,1,0:T(2,128)(2,1)} %reshape.2118), calls=%async_computation.15 | async-start | bytes 491520 | tf_op jit(solution)/shard_map/all_to_all | solution.py:164
  415.6 678.4 %all-gather.13.cloned.1.call-start = ((), (), s32[]{:S(2)}) async-start(), calls=%async_computation.44 | async-start | bytes 3276800 | tf_op jit(solution)/shard_map/all_gather | solution.py:161
  551.0 686.8 %reduce-scatter.32.cloned.1.call-start = ((), (), s32[]{:S(2)}) async-start(), calls=%async_computation.40 | async-start | bytes 491520 | tf_op jit(solution)/shard_map/reduce_scatter | solution.py:351
  567.5 672.0 %all-gather.15.cloned.1.call-start = ((), (), s32[]{:S(2)}) async-start(), calls=%async_computation.45 | async-start | bytes 3276800 | tf_op jit(solution)/shard_map/all_gather | solution.py:161
  582.2 661.4 %reduce-scatter.44.cloned.1.call-start = ((), (), s32[]{:S(2)}) async-start(), calls=%async_computation.49 | async-start | bytes 1228800
  685.0 51.6 %all-to-all-start.12 = ((bf16[4,2,40960]{2,1,0:T(2,128)(2,1)}), bf16[4,2,40960]{2,1,0:T(2,128)(2,1)}, u32[]{:S(2)}, u32[]{:S(2)}) async-start(bf16[4,2,40960]{2,1,0:T(2,128)(2,1)} %reshape.2126), calls=%async_computation.19 | async-start | bytes 1310720 | tf_op jit(solution)/shard_map/all_to_all | solution.py:165
  689.4 602.5 %reduce-scatter.24.cloned.1.call-start = ((), (), s32[]{:S(2)}) async-start(), calls=%async_computation.36 | async-start | bytes 1228800 | tf_op jit(solution)/shard_map/reduce_scatter | solution.py:210
  724.5 650.7 %all-gather.17.cloned.1.call-start = ((), (), s32[]{:S(2)}) async-start(), calls=%async_computation.46 | async-start | bytes 3276800 | tf_op jit(solution)/shard_map/all_gather | solution.py:161
  736.6 51.3 %all-to-all-start.15 = ((bf16[4,2,40960]{2,1,0:T(2,128)(2,1)}), bf16[4,2,40960]{2,1,0:T(2,128)(2,1)}, u32[]{:S(2)}, u32[]{:S(2)}) async-start(bf16[4,2,40960]{2,1,0:T(2,128)(2,1)} %reshape.2132), calls=%async_computation.23 | async-start | bytes 1310720 | tf_op jit(solution)/shard_map/all_to_all | solution.py:166
  787.9 33.9 %all-to-all-start = ((bf16[4,2,15360]{2,1,0:T(2,128)(2,1)}), bf16[4,2,15360]{2,1,0:T(2,128)(2,1)}, u32[]{:S(2)}, u32[]{:S(2)}) async-start(bf16[4,2,15360]{2,1,0:T(2,128)(2,1)} %reshape.2100), calls=%async_computation.3 | async-start | bytes 491520 | tf_op jit(solution)/shard_map/all_to_all | solution.py:230
  821.8 54.9 %all-to-all-start.3 = ((bf16[4,2,15360]{2,1,0:T(2,128)(2,1)}), bf16[4,2,15360]{2,1,0:T(2,128)(2,1)}, u32[]{:S(2)}, u32[]{:S(2)}) async-start(bf16[4,2,15360]{2,1,0:T(2,128)(2,1)} %reshape.2106), calls=%async_computation.7 | async-start | bytes 491520 | tf_op jit(solution)/shard_map/all_to_all | solution.py:231
  922.1 81.4 %all-to-all-start.13 = ((bf16[4,2,40960]{2,1,0:T(2,128)(2,1)}), bf16[4,2,40960]{2,1,0:T(2,128)(2,1)}, u32[]{:S(2)}, u32[]{:S(2)}) async-start(bf16[4,2,40960]{2,1,0:T(2,128)(2,1)} %reshape.2124), calls=%async_computation.20 | async-start | bytes 1310720 | tf_op jit(solution)/shard_map/all_to_all | solution.py:165
  1086.0 33.2 %all-to-all-start.14 = ((bf16[4,2,40960]{2,1,0:T(2,128)(2,1)}), bf16[4,2,40960]{2,1,0:T(2,128)(2,1)}, u32[]{:S(2)}, u32[]{:S(2)}) async-start(bf16[4,2,40960]{2,1,0:T(2,128)(2,1)} %reshape.2128), calls=%async_computation.21 | async-start | bytes 1310720 | tf_op jit(solution)/shard_map/all_to_all | solution.py:165
  1123.4 258.7 %reduce-scatter.34.cloned.1.call-start = ((), (), s32[]{:S(2)}) async-start(), calls=%async_computation.41 | async-start | bytes 983040 | tf_op jit(solution)/shard_map/reduce_scatter | solution.py:354
  1208.7 175.2 %reduce-scatter.36.cloned.1.call-start = ((), (), s32[]{:S(2)}) async-start(), calls=%async_computation.42 | async-start | bytes 983040 | tf_op jit(solution)/shard_map/reduce_scatter | solution.py:357
  1263.6 122.0 %reduce-scatter.26.cloned.1.call-start = ((), (), s32[]{:S(2)}) async-start(), calls=%async_computation.37 | async-start | bytes 491520 | tf_op jit(solution)/shard_map/reduce_scatter | solution.py:342
  1304.6 59.1 %all-to-all-start.8 = ((bf16[4,2,15360]{2,1,0:T(2,128)(2,1)}), bf16[4,2,15360]{2,1,0:T(2,128)(2,1)}, u32[]{:S(2)}, u32[]{:S(2)}) async-start(bf16[4,2,15360]{2,1,0:T(2,128)(2,1)} %reshape.2116), calls=%async_computation.13 | async-start | bytes 491520 | tf_op jit(solution)/shard_map/all_to_all | solution.py:232
  1308.7 78.5 %reduce-scatter.28.cloned.1.call-start = ((), (), s32[]{:S(2)}) async-start(), calls=%async_computation.38 | async-start | bytes 491520 | tf_op jit(solution)/shard_map/reduce_scatter | solution.py:345
  1317.9 73.2 %reduce-scatter.30.cloned.1.call-start = ((), (), s32[]{:S(2)}) async-start(), calls=%async_computation.39 | async-start | bytes 491520 | tf_op jit(solution)/shard_map/reduce_scatter | solution.py:348
  1374.6 40.5 %reduce-scatter.38.cloned.1.call-start = ((), (), s32[]{:S(2)}) async-start(), calls=%async_computation.43 | async-start | bytes 983040 | tf_op jit(solution)/shard_map/reduce_scatter | solution.py:360
  (152 other events, 1896.0 us)
Sparse Core Ops, SparseCore 0:
  275.6 28.8 reduce-scatter.39
  330.8 27.4 reduce-scatter.19
  394.6 29.8 reduce-scatter.41
  427.3 30.2 reduce-scatter.21
  459.3 40.9 all-gather.12
  567.6 21.0 reduce-scatter.31
  590.6 43.1 all-gather.14
  637.1 30.3 reduce-scatter.43
  724.6 31.0 reduce-scatter.23
  757.5 50.5 all-gather.16
  1141.4 24.6 reduce-scatter.33
  1237.9 24.5 reduce-scatter.35
  1278.2 20.1 reduce-scatter.25
  1318.0 22.0 reduce-scatter.27
  1374.7 16.4 reduce-scatter.29
  1393.3 21.6 reduce-scatter.37
where the time goes:
time: 1440 us; the launch traced here: 1420 us
  local copies, waits for them, and re-layouts  432 us (30%)
  blocking collectives  369 us (26%)
  matrix products  257 us (18%)
  other arithmetic  216 us (15%)
  starting transfers between devices  95.3 us (7%)
  waiting for transfers between devices  36.7 us (3%)
  between operations  16.7 us (1%)
    unnamed x328, local copies, waits for them, and re-layouts  167 us
    unnamed x23, other arithmetic  149 us
    all_gather x6, blocking collectives, on_device(): lax.all_gather(projected[5], 'seq', axis=1, tiled=True)  95.3 us
    all_gather x6, blocking collectives, on_device(): lax.all_gather(projected[4], 'seq', axis=1, tiled=True)  81.4 us
    dot_general x21, matrix products, outer_sum(): jnp.einsum('bsd,bse->de', inputs, others, preferred_element_type=jnp.floa...  65.4 us
    all_gather x3, blocking collectives, attn_backward(): normed_all = lax.all_gather(normed_low, 'seq', axis=1, tiled=True)  56.9 us
    dot_general x36, matrix products, linear(): jnp.einsum('bsd,de->bse', inputs, matrix, preferred_element_type=jnp.floa...  54.1 us
    all_gather x3, blocking collectives, ffn_backward(): lax.all_gather(mixed_low, 'seq', axis=1, tiled=True)  48.4 us
  transfers between devices with their start and end apart: 41, of which 7 were waited for; matrix products, arithmetic and copies ran while one was open for 47% of the time, Pallas kernels for 0%

commit v1 on v0

v1 whole, which is shorter than its diff:
```python
import functools

import jax
import jax.numpy as jnp
import numpy as np
from jax import lax
from jax.experimental import pallas as pl
from jax.experimental.pallas import tpu as pltpu
from jax.sharding import PartitionSpec as P

DIM = 768
HEAD_DIM = 64
FF = 2048
ROWS = 160
PARTS = 4
SLOTS = ROWS * PARTS
SHARE_HEADS = 3
SHARE = SHARE_HEADS * HEAD_DIM
FF_SHARE = FF // PARTS
PACKED = SLOTS * 3 // 2
PACKED_ROWS = ROWS * 3 // 2
WINDOW = 256
QUERY_BLOCKS = ((0, 256), (256, 256), (512, 128))
HALVES = ((0, 320), (320, 320))

epsilon = 1e-05
masked_score = -1e30
bf16 = jnp.bfloat16
f32 = jnp.float32
MIB = 1 << 20


def nn(left, right):
    return lax.dot_general(left, right, (((1,), (0,)), ((), ())), preferred_element_type=f32)


def nt(left, right):
    return lax.dot_general(left, right, (((1,), (1,)), ((), ())), preferred_element_type=f32)


def tn(left, right):
    return lax.dot_general(left, right, (((0,), (0,)), ((), ())), preferred_element_type=f32)


def rms_scale(values):
    return lax.rsqrt(jnp.mean(values * values, axis=-1, keepdims=True) + epsilon)


def rotate(values, cosine, signed_sine):
    width = values.shape[-1]
    lane = lax.broadcasted_iota(jnp.int32, values.shape, 1)
    ahead = pltpu.roll(values, width - 32, 1)
    behind = pltpu.roll(values, 32, 1)
    partner = jnp.where(lane % HEAD_DIM < 32, ahead, behind)
    return values * cosine + partner * signed_sine


def wide(table):
    return jnp.concatenate([table, table], axis=1)


def unpack(packed, count):
    tail = packed[count:]
    third = jnp.concatenate([tail[:, :HEAD_DIM], tail[:, HEAD_DIM:]], axis=0)
    return jnp.concatenate([packed[:count], third], axis=1)


def place():
    return lax.axis_index("section"), lax.axis_index("seq")


def block_rows(index, size=ROWS):
    return pl.ds(pl.multiple_of(index * size, size), size)


def window_start(seq):
    return pl.multiple_of(((3 * seq) >> 1) * 128, 128)


class Loader:
    def __init__(self, sems, core):
        self.sems = sems
        self.core = core
        self.count = 0

    def start(self, layer, own, other, target):
        sem = self.sems.at[self.count]
        self.count += 1

        @pl.when(self.core == layer)
        def _():
            pltpu.make_async_copy(own, target, sem).start()

        @pl.when(self.core != layer)
        def _():
            pltpu.make_async_copy(other, target, sem).start()

        return pltpu.make_async_copy(own, target, sem)


def project(normed, windows, odd, cos, sin, queries, keys, values, value_t):
    for first, count in QUERY_BLOCKS:
        rows = slice(first, first + count)
        block = normed[rows, :]
        cosine, sine = wide(cos[rows, :]), wide(sin[rows, :])
        for kind, (window, target) in enumerate(zip(windows, (queries, keys, values))):
            result = nn(block, window[...])
            if kind < 2:
                result = rotate(result, cosine, sine)
            if kind == 0:
                result = result * HEAD_DIM ** (-0.5)
            result = jnp.where(odd, pltpu.roll(result, WINDOW - HEAD_DIM, 1), result)
            low = result.astype(bf16)
            for head in range(SHARE_HEADS):
                target[head, rows, :] = low[:, head * HEAD_DIM : (head + 1) * HEAD_DIM]
            if kind == 2:
                turned = jnp.transpose(result).astype(bf16)
                for head in range(SHARE_HEADS):
                    value_t[head, :, rows] = turned[head * HEAD_DIM : (head + 1) * HEAD_DIM, :]


def masked(scores_t, first, length):
    spots = lax.broadcasted_iota(jnp.int32, scores_t.shape, 0)
    query = first + lax.broadcasted_iota(jnp.int32, (1, scores_t.shape[1]), 1)
    bound = jnp.minimum(query + 1, length)
    return jnp.where(spots < bound, scores_t, masked_score)


def attend(queries, keys, value_t, length, mixed_t):
    @pl.loop(0, SHARE_HEADS)
    def _(head):
        for first, count in QUERY_BLOCKS:
            last = first + count
            scores = nt(keys[head, :last, :], queries[head, first:last, :])
            scores = masked(scores, first, length)
            exponent = jnp.exp(scores - jnp.max(scores, axis=0, keepdims=True))
            total = jnp.sum(exponent, axis=0, keepdims=True)
            mixed = nn(value_t[head, :, :last], exponent.astype(bf16))
            mixed_t[head, :, first:last] = mixed * (1.0 / total)


def untranspose(mixed_t, pair, single):
    both = jnp.concatenate([mixed_t[0], mixed_t[1]], axis=0)
    pair[...] = jnp.transpose(both).astype(bf16)
    last = jnp.concatenate([mixed_t[2], mixed_t[2]], axis=0)
    single[...] = jnp.transpose(last).astype(bf16)


def pack_all(pair, single, target):
    half = SLOTS // 2
    target[:SLOTS, :] = pair[...]
    target[SLOTS:, :] = jnp.concatenate(
        [single[:half, :HEAD_DIM], single[half:, :HEAD_DIM]], axis=1
    )


def pack_block(pair, single, index, target):
    half = ROWS // 2
    rows = block_rows(index)
    target[:ROWS, :] = pair[rows, :]
    tail = single[rows, :]
    target[ROWS:, :] = jnp.concatenate([tail[:half, :HEAD_DIM], tail[half:, :HEAD_DIM]], axis=1)


def norm_back(grad_normed, gain, normed, scale):
    scaled = grad_normed * gain
    return scale * (scaled - normed * jnp.mean(scaled * normed, axis=-1, keepdims=True))


def ffn_back_chunk(gate, up, grad_hidden):
    sigmoid = jax.nn.sigmoid(gate)
    grad_gate = grad_hidden * up * sigmoid * (1.0 + gate * (1.0 - sigmoid))
    grad_up = grad_hidden * gate * sigmoid
    return grad_gate.astype(bf16), grad_up.astype(bf16)


def first_attention(
    x_0, x_1, x_2, x_3, length, gain_own, gain_other, cos, sin,
    q_own, q_other, k_own, k_other, v_own, v_other,
    normed, queries, keys, values, packed,
    w_q, w_k, w_v, value_t, mixed_t, pair, single, sems,
):
    core, seq = place()
    odd = seq % 2 == 1
    loader = Loader(sems, core)
    span = pl.ds(window_start(seq), WINDOW)
    copies = [
        loader.start(0, own.at[0, :, span], other.at[0, :, span], target)
        for own, other, target in ((q_own, q_other, w_q), (k_own, k_other, w_k), (v_own, v_other, w_v))
    ]
    gain = jnp.where(core == 0, gain_own[0:1, :], gain_other[0:1, :])
    for offset, block in enumerate((x_0, x_1, x_2, x_3)):
        wide_block = block[...].astype(f32)
        normed[block_rows(seq ^ offset), :] = (wide_block * rms_scale(wide_block) * gain).astype(bf16)
    for copy in copies:
        copy.wait()
    project(normed, (w_q, w_k, w_v), odd, cos, sin, queries, keys, values, value_t)
    attend(queries, keys, value_t, length[0], mixed_t)
    untranspose(mixed_t, pair, single)
    pack_all(pair, single, packed)


def middle(
    x_0, x_1, x_2, x_3, o_0, o_1, o_2, o_3, length, gain_own, gain_other, cos, sin,
    o_own, o_other, g_own, g_other, u_own, u_other, d_own, d_other,
    q_own, q_other, k_own, k_other, v_own, v_other,
    after_own, normed_two, hidden, mid_own, normed, queries, keys, values, packed,
    b_0, b_1, b_2, b_3,
    w_o, w_g, w_u, w_d, w_q, w_k, w_v, after, total, value_t, mixed_t, pair, single, sems,
):
    core, seq = place()
    odd = seq % 2 == 1
    loader = Loader(sems, core)
    copy_o = loader.start(0, o_own.at[0], o_other.at[0], w_o)
    copies = []
    for part in range(PARTS):
        span = slice(part * FF_SHARE, (part + 1) * FF_SHARE)
        copies.append(
            (
                loader.start(0, g_own.at[0, :, span], g_other.at[0, :, span], w_g.at[part]),
                loader.start(0, u_own.at[0, :, span], u_other.at[0, :, span], w_u.at[part]),
                loader.start(0, d_own.at[0, span, :], d_other.at[0, span, :], w_d.at[span, :]),
            )
        )
    span = pl.ds(window_start(seq), WINDOW)
    copies_qkv = [
        loader.start(1, own.at[0, :, span], other.at[0, :, span], target)
        for own, other, target in ((q_own, q_other, w_q), (k_own, k_other, w_k), (v_own, v_other, w_v))
    ]
    gain_ffn = jnp.where(core == 0, gain_own[1:2, :], gain_other[1:2, :])
    gain_attn = jnp.where(core == 1, gain_own[0:1, :], gain_other[0:1, :])
    for offset, block in enumerate((x_0, x_1, x_2, x_3)):
        after[block_rows(seq ^ offset), :] = block[...].astype(f32)
    copy_o.wait()
    for offset, block in enumerate((o_0, o_1, o_2, o_3)):
        share = w_o[block_rows(seq ^ offset, SHARE), :]
        whole = unpack(block[...], SLOTS)
        for first, count in HALVES:
            rows = slice(first, first + count)
            after[rows, :] += nn(whole[rows], share)
    for first, count in HALVES:
        rows = slice(first, first + count)
        block = after[rows, :]
        normed_two[rows, :] = (block * rms_scale(block) * gain_ffn).astype(bf16)
        total[rows, :] = block
    after_own[...] = after[block_rows(seq), :]
    for part in range(PARTS):
        for copy in copies[part]:
            copy.wait()
        for first, count in HALVES:
            rows = slice(first, first + count)
            block = normed_two[rows, :]
            gate = nn(block, w_g[part])
            up = nn(block, w_u[part])
            low = (gate * jax.nn.sigmoid(gate) * up).astype(bf16)
            hidden[rows, part * FF_SHARE : (part + 1) * FF_SHARE] = low
            total[rows, :] += nn(low, w_d[part * FF_SHARE : (part + 1) * FF_SHARE, :])
    for first, count in HALVES:
        rows = slice(first, first + count)
        low = total[rows, :].astype(bf16)
        block = low.astype(f32)
        total[rows, :] = block
        normed[rows, :] = (block * rms_scale(block) * gain_attn).astype(bf16)
    mid_own[...] = total[block_rows(seq), :].astype(bf16)
    for copy in copies_qkv:
        copy.wait()
    project(normed, (w_q, w_k, w_v), odd, cos, sin, queries, keys, values, value_t)
    attend(queries, keys, value_t, length[0], mixed_t)
    untranspose(mixed_t, pair, single)
    pack_all(pair, single, packed)
    for offset, target in enumerate((b_0, b_1, b_2, b_3)):
        pack_block(pair, single, seq ^ offset, target)


def send_blocks(seq, grad_branch, w_o, targets):
    for here in range(PARTS):

        @pl.when(seq == here)
        def _():
            for offset, target in enumerate(targets):
                other = here ^ offset
                span = slice(other * SHARE, (other + 1) * SHARE)
                grad_heads = nt(grad_branch, w_o[span, :]).astype(bf16)
                target[...] = jnp.concatenate([grad_heads, grad_branch[:, span]], axis=1)


def last_rows(
    mid_own, cotangent, o_0, o_1, o_2, o_3, gain_own, gain_other,
    o_own, o_other, g_own, g_other, u_own, u_other, d_own, d_other,
    output, normed_two, grad_after, grad_gain, b_0, b_1, b_2, b_3,
    w_o, w_g, w_u, w_d, branch, hidden, sems,
):
    core, seq = place()
    loader = Loader(sems, core)
    copy_o = loader.start(1, o_own.at[0], o_other.at[0], w_o)
    copies = []
    for part in range(PARTS):
        span = slice(part * FF_SHARE, (part + 1) * FF_SHARE)
        copies.append(
            (
                loader.start(1, g_own.at[0, :, span], g_other.at[0, :, span], w_g.at[part]),
                loader.start(1, u_own.at[0, :, span], u_other.at[0, :, span], w_u.at[part]),
                loader.start(1, d_own.at[0, span, :], d_other.at[0, span, :], w_d.at[span, :]),
            )
        )
    gain = jnp.where(core == 1, gain_own[1:2, :], gain_other[1:2, :])
    copy_o.wait()
    after = mid_own[...].astype(f32)
    for offset, block in enumerate((o_0, o_1, o_2, o_3)):
        after = after + nn(unpack(block[...], ROWS), w_o[block_rows(seq ^ offset, SHARE), :])
    scale = rms_scale(after)
    normed = after * scale
    low = (normed * gain).astype(bf16)
    normed_two[...] = low
    grad_low = cotangent[...]
    grad_normed = jnp.zeros((ROWS, DIM), f32)
    for part in range(PARTS):
        for copy in copies[part]:
            copy.wait()
        gate = nn(low, w_g[part])
        up = nn(low, w_u[part])
        span = slice(part * FF_SHARE, (part + 1) * FF_SHARE)
        hidden[:, span] = (gate * jax.nn.sigmoid(gate) * up).astype(bf16)
        grad_gate, grad_up = ffn_back_chunk(gate, up, nt(grad_low, w_d[span, :]))
        grad_normed = grad_normed + nt(grad_gate, w_g[part]) + nt(grad_up, w_u[part])
    output[...] = (after + nn(hidden[...], w_d[...])).astype(bf16)
    grad_gain[...] = jnp.sum(grad_normed * normed, axis=0, keepdims=True)
    total = grad_low.astype(f32) + norm_back(grad_normed, gain, normed, scale)
    grad_after[...] = total
    branch[...] = total.astype(bf16)
    send_blocks(seq, branch[...], w_o, (b_0, b_1, b_2, b_3))


def first_rows_back(
    after_own, grad_in, gain_own, gain_other,
    o_own, o_other, g_own, g_other, u_own, u_other, d_own, d_other,
    grad_after, grad_gain, b_0, b_1, b_2, b_3,
    w_o, w_g, w_u, w_d, branch, sems,
):
    core, seq = place()
    loader = Loader(sems, core)
    copies = []
    for part in range(PARTS):
        span = slice(part * FF_SHARE, (part + 1) * FF_SHARE)
        copies.append(
            (
                loader.start(0, g_own.at[0, :, span], g_other.at[0, :, span], w_g.at[part]),
                loader.start(0, u_own.at[0, :, span], u_other.at[0, :, span], w_u.at[part]),
                loader.start(0, d_own.at[0, span, :], d_other.at[0, span, :], w_d.at[span, :]),
            )
        )
    copy_o = loader.start(0, o_own.at[0], o_other.at[0], w_o)
    gain = jnp.where(core == 0, gain_own[1:2, :], gain_other[1:2, :])
    after = after_own[...]
    scale = rms_scale(after)
    normed = after * scale
    low = (normed * gain).astype(bf16)
    grad_low = grad_in[...]
    grad_normed = jnp.zeros((ROWS, DIM), f32)
    for part in range(PARTS):
        for copy in copies[part]:
            copy.wait()
        gate = nn(low, w_g[part])
        up = nn(low, w_u[part])
        grad_gate, grad_up = ffn_back_chunk(gate, up, nt(grad_low, w_d[part * FF_SHARE : (part + 1) * FF_SHARE, :]))
        grad_normed = grad_normed + nt(grad_gate, w_g[part]) + nt(grad_up, w_u[part])
    grad_gain[...] = jnp.sum(grad_normed * normed, axis=0, keepdims=True)
    total = grad_low.astype(f32) + norm_back(grad_normed, gain, normed, scale)
    grad_after[...] = total
    branch[...] = total.astype(bf16)
    copy_o.wait()
    send_blocks(seq, branch[...], w_o, (b_0, b_1, b_2, b_3))


def attention_back(
    g_0, g_1, g_2, g_3, length, cos, sin, queries, keys, values,
    b_0, b_1, b_2, b_3,
    grad_mixed, key_t, query_grad_t, key_grad, value_grad, whole,
):
    _, seq = place()
    for offset, block in enumerate((g_0, g_1, g_2, g_3)):
        low = block[:, :SHARE]
        for head in range(SHARE_HEADS):
            grad_mixed[head, block_rows(seq ^ offset), :] = low[:, head * HEAD_DIM : (head + 1) * HEAD_DIM]
    key_grad[...] = jnp.zeros_like(key_grad)
    value_grad[...] = jnp.zeros_like(value_grad)

    @pl.loop(0, SHARE_HEADS)
    def _(head):
        key_wide = keys[head].astype(f32)
        key_t[...] = jnp.transpose(jnp.concatenate([key_wide, key_wide], axis=1))[:HEAD_DIM].astype(bf16)
        for first, count in QUERY_BLOCKS:
            last = first + count
            query = queries[head, first:last, :]
            grad = grad_mixed[head, first:last, :]
            scores = nt(keys[head, :last, :], query)
            scores = masked(scores, first, length[0])
            exponent = jnp.exp(scores - jnp.max(scores, axis=0, keepdims=True))
            weights = exponent * (1.0 / jnp.sum(exponent, axis=0, keepdims=True))
            grad_weights = nt(values[head, :last, :], grad)
            row_total = jnp.sum(weights * grad_weights, axis=0, keepdims=True)
            grad_scores = (weights * (grad_weights - row_total)).astype(bf16)
            value_grad[head, :last, :] += nn(weights.astype(bf16), grad)
            key_grad[head, :last, :] += nn(grad_scores, query)
            query_grad_t[head, :, first:last] = nn(key_t[:, :last], grad_scores) * HEAD_DIM ** (-0.5)

    turned = jnp.concatenate([query_grad_t[0], query_grad_t[1], query_grad_t[2], query_grad_t[2]], axis=0)
    query_side = jnp.transpose(turned)
    key_side = jnp.concatenate([key_grad[0], key_grad[1], key_grad[2], key_grad[2]], axis=1)
    value_side = jnp.concatenate([value_grad[0], value_grad[1], value_grad[2]], axis=1)
    cosine, sine = wide(cos[...]), wide(sin[...])
    query_side = rotate(query_side, cosine, -sine)[:, :SHARE]
    key_side = rotate(key_side, cosine, -sine)[:, :SHARE]
    whole[...] = jnp.concatenate([query_side, key_side, value_side], axis=1).astype(bf16)
    for offset, target in enumerate((b_0, b_1, b_2, b_3)):
        target[...] = whole[block_rows(seq ^ offset), :]


def input_back(
    layer, b_0, b_1, b_2, b_3, inputs, grad_after, gain_own, gain_other,
    q_own, q_other, k_own, k_other, v_own, v_other,
    grad_in, grad_gain,
    w_q, w_k, w_v, sides, sems,
):
    core, seq = place()
    loader = Loader(sems, core)
    copies = [
        loader.start(layer, own.at[0], other.at[0], target)
        for own, other, target in ((q_own, q_other, w_q), (k_own, k_other, w_k), (v_own, v_other, w_v))
    ]
    gain = jnp.where(core == layer, gain_own[0:1, :], gain_other[0:1, :])
    blocks = (b_0, b_1, b_2, b_3)
    for here in range(PARTS):

        @pl.when(seq == here)
        def _():
            for kind in range(3):
                span = slice(kind * SHARE, (kind + 1) * SHARE)
                sides[kind] = jnp.concatenate(
                    [blocks[here ^ part][:, span] for part in range(PARTS)], axis=1
                )

    wide_inputs = inputs[...].astype(f32)
    scale = rms_scale(wide_inputs)
    normed = wide_inputs * scale
    grad_normed = jnp.zeros((ROWS, DIM), f32)
    for kind, weight in enumerate((w_q, w_k, w_v)):
        copies[kind].wait()
        grad_normed = grad_normed + nt(sides[kind], weight[...])
    grad_gain[...] = jnp.sum(grad_normed * normed, axis=0, keepdims=True)
    grad_in[...] = (grad_after[...] + norm_back(grad_normed, gain, normed, scale)).astype(bf16)


def attention_weights_grad(
    normed, b_0, b_1, b_2, b_3, o_0, o_1, o_2, o_3, g_0, g_1, g_2, g_3,
    keep, send,
    whole, branch, output_grad,
):
    core, seq = place()
    for offset, (block, grad) in enumerate(zip((b_0, b_1, b_2, b_3), (g_0, g_1, g_2, g_3))):
        rows = block_rows(seq ^ offset)
        whole[rows, :] = block[...]
        branch[rows, :] = grad[:, SHARE:]
    for offset, block in enumerate((o_0, o_1, o_2, o_3)):
        output_grad[block_rows(seq ^ offset, SHARE), :] = tn(unpack(block[...], SLOTS), branch[...])
    result = tn(normed[...], whole[...])
    low = result[:, : 2 * SHARE].astype(bf16)
    high = jnp.concatenate([result[:, 2 * SHARE :], output_grad[...]], axis=1).astype(bf16)

    @pl.when(core == 0)
    def _():
        keep[...] = low
        send[...] = high

    @pl.when(core == 1)
    def _():
        keep[...] = high
        send[...] = low


def ffn_weights_grad(
    layer, groups, *refs
):
    if layer == 0:
        (normed_two, hidden, y_0, y_1, y_2, y_3, g_own, g_other, u_own, u_other, d_own, d_other,
         keep, send, keep_down, send_down,
         w_g, w_u, w_d, grad_out, grad_gate, grad_up, down, sems) = refs
    else:
        (n_0, n_1, n_2, n_3, y_0, y_1, y_2, y_3, g_own, g_other, u_own, u_other, d_own, d_other,
         keep, send, keep_down, send_down,
         w_g, w_u, w_d, normed_two, grad_out, grad_gate, grad_up, down, sems) = refs
    core, seq = place()
    loader = Loader(sems, core)
    span = pl.ds(pl.multiple_of(seq * FF_SHARE, FF_SHARE), FF_SHARE)
    last = PARTS
    copies = [
        (
            loader.start(layer, g_own.at[0, :, span], g_other.at[0, :, span], w_g.at[last]),
            loader.start(layer, u_own.at[0, :, span], u_other.at[0, :, span], w_u.at[last]),
            loader.start(layer, d_own.at[0, span, :], d_other.at[0, span, :], w_d),
        )
    ]
    if layer == 1:
        for part in range(PARTS):
            part_span = slice(part * FF_SHARE, (part + 1) * FF_SHARE)
            copies.append(
                (
                    loader.start(layer, g_own.at[0, :, part_span], g_other.at[0, :, part_span], w_g.at[part]),
                    loader.start(layer, u_own.at[0, :, part_span], u_other.at[0, :, part_span], w_u.at[part]),
                )
            )
        for offset, block in enumerate((n_0, n_1, n_2, n_3)):
            normed_two[block_rows(seq ^ offset), :] = block[...]
    for offset, block in enumerate((y_0, y_1, y_2, y_3)):
        grad_out[block_rows(seq ^ offset), :] = block[...]
    for copy in copies[0]:
        copy.wait()
    for first, count in HALVES:
        rows = slice(first, first + count)
        block = normed_two[rows, :]
        grad_gate[rows, :], grad_up[rows, :] = ffn_back_chunk(
            nn(block, w_g[last]), nn(block, w_u[last]), nt(grad_out[rows, :], w_d[...])
        )
    gate_side = tn(normed_two[...], grad_gate[...]).astype(bf16)

    @pl.when(core == 0)
    def _():
        keep[...] = gate_side

    @pl.when(core == 1)
    def _():
        send[...] = gate_side

    up_side = tn(normed_two[...], grad_up[...]).astype(bf16)

    @pl.when(core == 0)
    def _():
        send[...] = up_side

    @pl.when(core == 1)
    def _():
        keep[...] = up_side

    window = grad_out[:, pl.ds(window_start(seq), WINDOW)].astype(f32)
    columns = jnp.where(seq % 2 == 1, pltpu.roll(window, WINDOW - HEAD_DIM, 1), window)
    columns = columns[:, :SHARE].astype(bf16)
    for part in range(PARTS):
        part_span = slice(part * FF_SHARE, (part + 1) * FF_SHARE)
        if layer == 1:
            for copy in copies[1 + part]:
                copy.wait()
            pieces = []
            for first, count in HALVES:
                rows = slice(first, first + count)
                gate = nn(normed_two[rows, :], w_g[part])
                up = nn(normed_two[rows, :], w_u[part])
                pieces.append((gate * jax.nn.sigmoid(gate) * up).astype(bf16))
            low = jnp.concatenate(pieces, axis=0)
        else:
            low = hidden[:, part_span]
        down[part_span, :] = tn(low, columns)
    quarter = FF // groups // 4
    for target, half in ((keep_down, core), (send_down, 1 - core)):
        for group in range(groups):
            begin = group * 4 * quarter + half * 2 * quarter
            begin = pl.multiple_of(begin, 2 * quarter)
            target[group * quarter : (group + 1) * quarter, :] = jnp.concatenate(
                [down[pl.ds(begin, quarter), :], down[pl.ds(begin + quarter, quarter), :]], axis=1
            ).astype(bf16)


def in_vmem(count):
    return [pl.BlockSpec(memory_space=pltpu.VMEM)] * count


def anywhere(count):
    return [pl.BlockSpec(memory_space=pl.ANY)] * count


def in_smem():
    return [pl.BlockSpec(memory_space=pltpu.SMEM)]


def shape(*dims, dtype=bf16):
    return jax.ShapeDtypeStruct(dims, dtype)


def call(body, in_specs, outs, scratch, flops, vmem, name):
    return pl.pallas_call(
        body,
        out_shape=outs,
        in_specs=in_specs,
        out_specs=in_vmem(len(outs)),
        scratch_shapes=scratch,
        compiler_params=pltpu.CompilerParams(vmem_limit_bytes=vmem * MIB),
        cost_estimate=pl.CostEstimate(flops=flops, bytes_accessed=flops // 400, transcendentals=0),
        name=name,
    )


def weights_scratch():
    return [
        pltpu.VMEM((DIM, DIM), bf16),
        pltpu.VMEM((PARTS, DIM, FF_SHARE), bf16),
        pltpu.VMEM((PARTS, DIM, FF_SHARE), bf16),
        pltpu.VMEM((FF, DIM), bf16),
    ]


def windows_scratch():
    return [pltpu.VMEM((DIM, WINDOW), bf16)] * 3


def attend_scratch():
    return [
        pltpu.VMEM((SHARE_HEADS, HEAD_DIM, SLOTS), bf16),
        pltpu.VMEM((SHARE_HEADS, HEAD_DIM, SLOTS), f32),
        pltpu.VMEM((SLOTS, 128), bf16),
        pltpu.VMEM((SLOTS, 128), bf16),
    ]


def sems(count):
    return [pltpu.SemaphoreType.DMA((count,))]


HEADS_OUT = [shape(SHARE_HEADS, SLOTS, HEAD_DIM)] * 3


def call_first_attention(*args):
    return call(
        first_attention,
        in_vmem(4) + in_smem() + in_vmem(4) + anywhere(6),
        [shape(SLOTS, DIM)] + HEADS_OUT + [shape(PACKED, 128)],
        windows_scratch() + attend_scratch() + sems(3),
        4 * 10**9,
        32,
        "first_attention",
    )(*args)


def call_middle(*args):
    return call(
        middle,
        in_vmem(8) + in_smem() + in_vmem(4) + anywhere(14),
        [shape(ROWS, DIM, dtype=f32), shape(SLOTS, DIM), shape(SLOTS, FF), shape(ROWS, DIM), shape(SLOTS, DIM)]
        + HEADS_OUT
        + [shape(PACKED, 128)]
        + [shape(PACKED_ROWS, 128)] * 4,
        weights_scratch()
        + windows_scratch()
        + [pltpu.VMEM((SLOTS, DIM), f32)] * 2
        + attend_scratch()
        + sems(16),
        12 * 10**9,
        52,
        "middle",
    )(*args)


def call_last_rows(*args):
    return call(
        last_rows,
        in_vmem(8) + anywhere(8),
        [shape(ROWS, DIM), shape(ROWS, DIM), shape(ROWS, DIM, dtype=f32), shape(1, DIM, dtype=f32)]
        + [shape(ROWS, 2 * SHARE)] * 4,
        weights_scratch() + [pltpu.VMEM((ROWS, DIM), bf16), pltpu.VMEM((ROWS, FF), bf16)] + sems(13),
        6 * 10**9,
        40,
        "last_rows",
    )(*args)


def call_first_rows_back(*args):
    return call(
        first_rows_back,
        in_vmem(4) + anywhere(8),
        [shape(ROWS, DIM, dtype=f32), shape(1, DIM, dtype=f32)] + [shape(ROWS, 2 * SHARE)] * 4,
        weights_scratch() + [pltpu.VMEM((ROWS, DIM), bf16)] + sems(13),
        5 * 10**9,
        40,
        "first_rows_back",
    )(*args)


def call_attention_back(*args):
    return call(
        attention_back,
        in_vmem(4) + in_smem() + in_vmem(5),
        [shape(ROWS, 3 * SHARE)] * 4,
        [
            pltpu.VMEM((SHARE_HEADS, SLOTS, HEAD_DIM), bf16),
            pltpu.VMEM((HEAD_DIM, SLOTS), bf16),
            pltpu.VMEM((SHARE_HEADS, HEAD_DIM, SLOTS), f32),
            pltpu.VMEM((SHARE_HEADS, SLOTS, HEAD_DIM), f32),
            pltpu.VMEM((SHARE_HEADS, SLOTS, HEAD_DIM), f32),
            pltpu.VMEM((SLOTS, 3 * SHARE), bf16),
        ],
        5 * 10**9,
        40,
        "attention_back",
    )(*args)


def call_input_back(layer, *args):
    return call(
        functools.partial(input_back, layer),
        in_vmem(8) + anywhere(6),
        [shape(ROWS, DIM), shape(1, DIM, dtype=f32)],
        [pltpu.VMEM((DIM, DIM), bf16)] * 3 + [pltpu.VMEM((3, ROWS, DIM), bf16)] + sems(3),
        2 * 10**9,
        32,
        "input_back",
    )(*args)


def call_attention_weights_grad(*args):
    return call(
        attention_weights_grad,
        in_vmem(13),
        [shape(DIM, 2 * SHARE)] * 2,
        [
            pltpu.VMEM((SLOTS, 3 * SHARE), bf16),
            pltpu.VMEM((SLOTS, SHARE), bf16),
            pltpu.VMEM((DIM, SHARE), f32),
        ],
        2 * 10**9,
        40,
        "attention_weights_grad",
    )(*args)


def call_ffn_weights_grad(layer, groups, *args):
    quarter = FF // groups // 4
    parts = PARTS + 1
    scratch = [
        pltpu.VMEM((parts, DIM, FF_SHARE), bf16),
        pltpu.VMEM((parts, DIM, FF_SHARE), bf16),
        pltpu.VMEM((FF_SHARE, DIM), bf16),
    ]
    if layer == 1:
        scratch += [pltpu.VMEM((SLOTS, DIM), bf16)]
    scratch += [
        pltpu.VMEM((SLOTS, DIM), bf16),
        pltpu.VMEM((SLOTS, FF_SHARE), bf16),
        pltpu.VMEM((SLOTS, FF_SHARE), bf16),
        pltpu.VMEM((FF, SHARE), f32),
    ]
    return call(
        functools.partial(ffn_weights_grad, layer, groups),
        in_vmem(6 if layer == 0 else 8) + anywhere(6),
        [shape(DIM, FF_SHARE)] * 2 + [shape(groups * quarter, 2 * SHARE)] * 2,
        scratch + sems(11),
        5 * 10**9,
        48,
        "ffn_weights_grad",
    )(*args)


def rotary_tables():
    lanes = np.arange(128)
    frequency = (10000.0 ** (-2.0 * (lanes % 32) / HEAD_DIM)).astype(np.float32)
    angles = np.arange(SLOTS, dtype=np.float32)[:, None] * frequency[None, :]
    sign = np.where(lanes % HEAD_DIM < 32, -1.0, 1.0).astype(np.float32)
    return np.cos(angles).astype(np.float32), (np.sin(angles) * sign).astype(np.float32)


def swap(value):
    return lax.ppermute(value, "section", [(0, 1), (1, 0)])


def to_partner(value, offset):
    return lax.ppermute(value, "seq", [(part, part ^ offset) for part in range(PARTS)])


def gathered(value):
    return [value] + [to_partner(value, offset) for offset in range(1, PARTS)]


def exchanged(blocks):
    return [blocks[0]] + [to_partner(blocks[offset], offset) for offset in range(1, PARTS)]


def scatter_sum(keep, received):
    total = (keep.astype(f32) + received.astype(f32)).astype(bf16)
    return lax.psum_scatter(total, "dp", scatter_dimension=0, tiled=True)


def on_device(
    section_input, out_cotangent, lengths, attn_gain, w_query, w_key, w_value, w_output,
    ffn_gain, w_gate, w_up, w_down,
):
    groups = lax.axis_size("dp")
    core = lax.axis_index("section")
    is_first = core == 0
    inputs = lax.dynamic_index_in_dim(section_input, core, 0, keepdims=False)
    cotangent = lax.dynamic_index_in_dim(out_cotangent, core, 0, keepdims=False)
    length = lax.dynamic_slice_in_dim(lengths, core, 1, 0)
    cos, sin = (jnp.asarray(table) for table in rotary_tables())
    x_blocks = gathered(inputs)

    gains = jnp.concatenate([attn_gain, ffn_gain], axis=0).astype(f32)
    gains_pair = (gains, swap(gains))
    q_pair = (w_query, swap(w_query))
    k_pair = (w_key, swap(w_key))
    v_pair = (w_value, swap(w_value))
    o_pair = (w_output, swap(w_output))
    g_pair = (w_gate, swap(w_gate))
    u_pair = (w_up, swap(w_up))
    d_pair = (w_down, swap(w_down))
    qkv = q_pair + k_pair + v_pair
    ffn = g_pair + u_pair + d_pair

    normed_0, queries_0, keys_0, values_0, packed_0 = call_first_attention(
        *x_blocks, length, *gains_pair, cos, sin, *qkv
    )
    mixed_0 = gathered(packed_0)
    (after_0, normed_two_0, hidden_0, mid, normed_1, queries_1, keys_1, values_1, packed_1, *mixed_blocks) = (
        call_middle(*x_blocks, *mixed_0, length, *gains_pair, cos, sin, *o_pair, *ffn, *qkv)
    )
    mixed_rows = exchanged(mixed_blocks)
    output, normed_two_1, grad_after_1, gain_ffn_1, *grad_blocks_1 = call_last_rows(
        mid, cotangent, *mixed_rows, *gains_pair, *o_pair, *ffn
    )
    grad_mixed_1 = exchanged(grad_blocks_1)
    grad_qkv_1 = call_attention_back(*grad_mixed_1, length, cos, sin, queries_1, keys_1, values_1)
    grad_rows_1 = exchanged(grad_qkv_1)
    grad_mid, gain_attn_1 = call_input_back(1, *grad_rows_1, mid, grad_after_1, *gains_pair, *qkv)

    grad_after_0, gain_ffn_0, *grad_blocks_0 = call_first_rows_back(
        after_0, grad_mid, *gains_pair, *o_pair, *ffn
    )
    grad_mixed_0 = exchanged(grad_blocks_0)
    grad_qkv_0 = call_attention_back(*grad_mixed_0, length, cos, sin, queries_0, keys_0, values_0)
    grad_rows_0 = exchanged(grad_qkv_0)
    grad_first, gain_attn_0 = call_input_back(0, *grad_rows_0, inputs, grad_after_0, *gains_pair, *qkv)

    mixed_1 = gathered(packed_1)
    normed_two_all = gathered(normed_two_1)
    cotangent_all = gathered(cotangent)
    keep, send, keep_down, send_down = call_ffn_weights_grad(
        1, groups, *normed_two_all, *cotangent_all, *ffn
    )
    ffn_1 = (scatter_sum(keep, swap(send)), scatter_sum(keep_down, swap(send_down)))
    keep, send = call_attention_weights_grad(normed_1, *grad_qkv_1, *mixed_1, *grad_mixed_1)
    attn_1 = scatter_sum(keep, swap(send))

    grad_mid_all = gathered(grad_mid)
    keep, send, keep_down, send_down = call_ffn_weights_grad(
        0, groups, normed_two_0, hidden_0, *grad_mid_all, *ffn
    )
    ffn_0 = (scatter_sum(keep, swap(send)), scatter_sum(keep_down, swap(send_down)))
    keep, send = call_attention_weights_grad(normed_0, *grad_qkv_0, *mixed_0, *grad_mixed_0)
    attn_0 = scatter_sum(keep, swap(send))

    def sort(of_first, of_second):
        mine = jnp.where(is_first, of_first, of_second)
        other = swap(jnp.where(is_first, of_second, of_first))
        return jnp.where(is_first, mine, other), jnp.where(is_first, other, mine)

    section_outputs = jnp.stack(sort(mid, output))[None]
    input_grads = jnp.stack(sort(grad_first, grad_mid))[None]
    attn_low, attn_high = sort(attn_0, attn_1)
    gate, up = sort(ffn_0[0], ffn_1[0])
    down_low, down_high = sort(ffn_0[1], ffn_1[1])
    down = jnp.concatenate(
        [down_low[:, :SHARE], down_low[:, SHARE:], down_high[:, :SHARE], down_high[:, SHARE:]], axis=0
    )
    gains_0 = jnp.concatenate([gain_attn_0, gain_ffn_0], axis=0)
    gains_1 = jnp.concatenate([gain_attn_1, gain_ffn_1], axis=0)
    gain_total = jnp.where(is_first, gains_0, gains_1) + swap(jnp.where(is_first, gains_1, gains_0))
    gain_shares = lax.psum_scatter(gain_total, ("dp", "seq"), scatter_dimension=1, tiled=True)

    return (
        section_outputs,
        input_grads,
        gain_shares[0:1],
        attn_low[None, :, :SHARE].astype(f32),
        attn_low[None, :, SHARE:].astype(f32),
        attn_high[None, :, :SHARE].astype(f32),
        attn_high[None, :, SHARE:].astype(f32),
        gain_shares[1:2],
        gate[None].astype(f32),
        up[None].astype(f32),
        down[None].astype(f32),
    )


def solution(mesh):
    return jax.shard_map(
        on_device,
        mesh=mesh,
        in_specs=(
            P("dp", "seq", None),
            P("dp", "seq", None),
            P("dp"),
            P("section", None),
            P("section", None, None),
            P("section", None, None),
            P("section", None, None),
            P("section", None, None),
            P("section", None),
            P("section", None, None),
            P("section", None, None),
            P("section", None, None),
        ),
        out_specs=(
            P("section", "dp", "seq", None),
            P("section", "dp", "seq", None),
            P("section", ("dp", "seq")),
            P("section", "dp", "seq"),
            P("section", "dp", "seq"),
            P("section", "dp", "seq"),
            P("section", "dp", "seq"),
            P("section", ("dp", "seq")),
            P("section", "dp", "seq"),
            P("section", "dp", "seq"),
            P("section", "dp", "seq"),
        ),
        check_vma=False,
    )
```

time: 1440 us -> 504 us (0.35)
  local copies, waits for them, and re-layouts: 432 us -> 50.2 us
  blocking collectives: 369 us -> 0 us
  matrix products: 257 us -> 0 us
  waiting for transfers between devices: 36.7 us -> 268 us
  other arithmetic: 216 us -> 16.5 us
  Pallas kernels: 0 us -> 98.8 us
  starting transfers between devices: 95.3 us -> 49.9 us
    all_gather x21 -> x0, blocking collectives: 327 us -> none  [the longest x6 95.3 us: on_device(): lax.all_gather(projected[5], 'seq', axis=1, tiled=True)]
    dot_general x96 -> x0, matrix products: 224 us -> none  [the longest x21 65.4 us: outer_sum(): jnp.einsum('bsd,bse->de', inputs, others, preferred_element_type=jnp.floa...]
    unnamed x23 -> x0, other arithmetic: 149 us -> none
    all_to_all x63 -> x0, local copies, waits for them, and re-layouts: 140 us -> none  [the longest x9 30.7 us: ffn_backward(): lax.all_to_all(grad_gate, 'seq', split_axis=2, concat_axis=1, tiled=True)]
    unnamed x328 -> x256, local copies, waits for them, and re-layouts: 167 us -> 46.3 us
    reduce_scatter x10 -> x6, waiting for transfers between devices: 29 us -> 129 us  [scatter_sum(): return lax.psum_scatter(total, 'dp', scatter_dimension=0, tiled=True)]
    pallas_call x0 -> x12, Pallas kernels: none -> 98.8 us  [the longest x2 23.4 us: call_ffn_weights_grad(): call(functools.partial(ffn_weights_grad, layer, groups), in_vmem(6 if lay...]
    convert_element_type x33 -> x0, local copies, waits for them, and re-layouts: 88.5 us -> none  [the longest x3 17.6 us: ffn_backward(): grad_up = (grad_hidden * gate_proj * sigmoid_gate).astype(jnp.bfloat16)]
  transfers between devices with their start and end apart: 41 -> 60, of which waited for: 7 -> 33; matrix products, arithmetic and copies ran while one was open for 47% -> 4% of each run, Pallas kernels for 0% -> 12%
where the time goes in v1:
time: 504 us; the launch traced here: 499 us
  waiting for transfers between devices  268 us (53%)
  Pallas kernels  98.8 us (20%)
  local copies, waits for them, and re-layouts  50.2 us (10%)
  starting transfers between devices  49.9 us (10%)
  other arithmetic  16.5 us (3%)
  between operations  15.8 us (3%)
    reduce_scatter x6, waiting for transfers between devices, scatter_sum(): return lax.psum_scatter(total, 'dp', scatter_dimension=0, tiled=True)  129 us
    unnamed x8, waiting for transfers between devices  78.4 us
    ppermute x33, waiting for transfers between devices, to_partner(): lax.ppermute(value, 'seq', [(part, part ^ offset) for part in range(PARTS)])  50.5 us
    unnamed x256, local copies, waits for them, and re-layouts  46.3 us
    ppermute x33, starting transfers between devices, to_partner(): lax.ppermute(value, 'seq', [(part, part ^ offset) for part in range(PARTS)])  44.2 us
    pallas_call x2, Pallas kernels, call_ffn_weights_grad(): call(functools.partial(ffn_weights_grad, layer, groups), in_vmem(6 if lay...  23.4 us
    pallas_call x1, Pallas kernels, call_middle(): call(middle, in_vmem(8) + in_smem() + in_vmem(4) + anywhere(14), [shape(R...  21.2 us
    pallas_call x2, Pallas kernels, call_attention_back(): call(attention_back, in_vmem(4) + in_smem() + in_vmem(5), [shape(ROWS, 3...  16.7 us
  transfers between devices with their start and end apart: 60, of which 33 were waited for; matrix products, arithmetic and copies ran while one was open for 4% of the time, Pallas kernels for 12%

profile of v1, /device:TPU:0, one launch (start us, length us, event | category | flops | bytes accessed | tf_op | source)
XLA Modules:
  0.0 499.4 jit_solution(8396164668352762334)
XLA Ops:
  8.2 3.0 collective-permute-start
  19.0 5.4 %collective-permute-done.1.x_2 = bf16[160,768]{1,0:T(8,128)(2,1)S(1)} collective-permute-done((bf16[160,768]{1,0:T(8,128)(2,1)S(1)}, bf16[160,768]{1,0:T(8,128)(2,1)S(1)}, u32[]{:S(2)}, u32[]{:S(2)}) %collective-permute-start.1) | collective-permute-done | bytes 245792 | tf_op jit(solution)/shard_map/ppermute | solution.py:773
  26.7 4.7 collective-permute-done.2.x_3
  42.0 7.4 %first_attention.1 = (bf16[640,768]{1,0:T(8,128)(2,1)S(1)}, bf16[3,640,64]{2,1,0:T(8,128)(2,1)S(1)}, bf16[3,640,64]{2,1,0:T(8,128)(2,1)S(1)}, bf16[3,640,64]{2,1,0:T(8,128)(2,1)S(1)}, bf16[960,128]{1,0:T(8,128)(2,1)S(1)}) custom-call(bf16[160,768]{1,0:T(8,128)(2,1)S(1)} %dynamic-slice_bitcast_fusion.1.x_0.inputs, ...), custom_call_target="tpu_custom_call" | custom-call | flops 4000000000 | bytes 10000000 | tf_op jit(solution)/shard_map/first_attention/pallas_call | solution.py:631
  55.7 5.1 %collective-permute-done.7.o_1 = bf16[960,128]{1,0:T(8,128)(2,1)S(1)} collective-permute-done((bf16[960,128]{1,0:T(8,128)(2,1)S(1)}, bf16[960,128]{1,0:T(8,128)(2,1)S(1)}, u32[]{:S(2)}, u32[]{:S(2)}) %collective-permute-start.7) | collective-permute-done | bytes 245792 | tf_op jit(solution)/shard_map/ppermute | solution.py:773
  63.2 5.7 %collective-permute-done.9.o_3 = bf16[960,128]{1,0:T(8,128)(2,1)S(1)} collective-permute-done((bf16[960,128]{1,0:T(8,128)(2,1)S(1)}, bf16[960,128]{1,0:T(8,128)(2,1)S(1)}, u32[]{:S(2)}, u32[]{:S(2)}) %collective-permute-start.9) | collective-permute-done | bytes 245792 | tf_op jit(solution)/shard_map/ppermute | solution.py:773
  74.4 21.2 %middle.1 = (f32[160,768]{1,0:T(8,128)}, bf16[640,768]{1,0:T(8,128)(2,1)}, bf16[640,2048]{1,0:T(8,128)(2,1)}, bf16[160,768]{1,0:T(8,128)(2,1)S(1)}, bf16[640,768...) custom-call(bf16[160,768]{1,0:T(8,128)(2,1)S(1)} %dynamic-slice_bitc, ...), custom_call_target="tpu_custom_call" | custom-call | flops 12000000000 | bytes 30000000 | tf_op jit(solution)/shard_map/middle/pallas_call | solution.py:643
  108.9 10.2 %last_rows.1 = (bf16[160,768]{1,0:T(8,128)(2,1)S(1)}, bf16[160,768]{1,0:T(8,128)(2,1)}, f32[160,768]{1,0:T(8,128)S(1)}, f32[1,768]{1,0:T(1,128)S(1)}, bf16[160,3...) custom-call(bf16[160,768]{1,0:T(8,128)(2,1)S(1)} %get-tuple-element., ...), custom_call_target="tpu_custom_call" | custom-call | flops 6000000000 | bytes 15000000 | tf_op jit(solution)/shard_map/last_rows/pallas_call | solution.py:662
  126.8 8.0 %attention_back.2 = (bf16[160,576]{1,0:T(8,128)(2,1)S(1)}, bf16[160,576]{1,0:T(8,128)(2,1)S(1)}, bf16[160,576]{1,0:T(8,128)(2,1)S(1)}, bf16[160,576]{1,0:T(8,128)(2,1)S(1)}) custom-call(bf16[160,384]{1,0:T(8,128)(2,1)S(1)} %get-tuple-element.75.g_0, bf16[160,384]{1,0:T(8,128)(2,1)S(1)} %collective-permute-done.18.g_1, ...), custom_call_target="tpu_custom_call" | custom-call | flops 5000000000 | bytes 12500000 | tf_op jit(solution)/shard_map/attention_back/pallas_call | solution.py:687
  142.9 4.2 collective-permute-done.23.b_3
  150.2 8.3 %first_rows_back.1 = (f32[160,768]{1,0:T(8,128)S(1)}, f32[1,768]{1,0:T(1,128)S(1)}, bf16[160,384]{1,0:T(8,128)(2,1)S(1)}, bf16[160,384]{1,0:T(8,128)(2,1)}, bf16...) custom-call(f32[160,768]{1,0:T(8,128)S(1)} %copy-done.39, bf16[160,768]{1,0:T(8,128)(2,1)S(1)} %get-tuple-element.87.grad_in.refs_2_, ...), custom_call_target="tpu_custom_call" | custom-call | flops 5000000000 | bytes 12500000 | tf_op jit(solution)/shard_map/first_rows_back/pallas_call | solution.py:675
  179.7 8.7 %attention_back.3 = (bf16[160,576]{1,0:T(8,128)(2,1)S(1)}, bf16[160,576]{1,0:T(8,128)(2,1)S(1)}, bf16[160,576]{1,0:T(8,128)(2,1)S(1)}, bf16[160,576]{1,0:T(8,128)(2,1)S(1)}) custom-call(bf16[160,384]{1,0:T(8,128)(2,1)S(1)} %copy-done.91, bf16[160,384]{1,0:T(8,128)(2,1)S(1)} %copy-done.94, bf16[160,384]{1,0:T(8,128)(2,1)S(1)} %copy-done.97, ...), custom_call_target="tpu_custom_call" | custom-call | flops 5000000000 | bytes 12500000 | tf_op jit(solution)/shard_map/attention_back/pallas_call | solution.py:687
  192.2 14.6 %ffn_weights_grad.3 = (bf16[768,512]{1,0:T(8,128)(2,1)S(1)}, bf16[768,512]{1,0:T(8,128)(2,1)S(1)}, bf16[512,384]{1,0:T(8,128)(2,1)S(1)}, bf16[512,384]{1,0:T(8,128)(2,1)}) custom-call(bf16[160,768]{1,0:T(8,128)(2,1)} %get-tuple-element.116.refs_0_, bf16[160,768]{1,0:T(8,128)(2,1)S(1)} %collective-permute-done.42.refs_1_, ...), custom_call_target="tpu_custom_call" | custom-call | flops 5000000000 | bytes 12500000 | tf_op jit(solution)/shard_map/ffn_weights_grad/pallas_call | solution.py:749
  219.8 5.7 %collective-permute-done.38.refs_3_ = bf16[160,768]{1,0:T(8,128)(2,1)S(1)} collective-permute-done((bf16[160,768]{1,0:T(8,128)(2,1)S(1)}, bf16[160,768]{1,0:T(8,128)(2,1)S(1)}, u32[]{:S(2)}, u32[]{:S(2)}) %collective-permute-start.38) | collective-permute-done | bytes 245792 | tf_op jit(solution)/shard_map/ppermute | solution.py:773
  227.0 9.0 %collective-permute-done.39.refs_4_ = bf16[160,768]{1,0:T(8,128)(2,1)S(1)} collective-permute-done((bf16[160,768]{1,0:T(8,128)(2,1)S(1)}, bf16[160,768]{1,0:T(8,128)(2,1)S(1)}, u32[]{:S(2)}, u32[]{:S(2)}) %collective-permute-start.39) | collective-permute-done | bytes 245792 | tf_op jit(solution)/shard_map/ppermute | solution.py:773
  237.7 8.8 %ffn_weights_grad.2 = (bf16[768,512]{1,0:T(8,128)(2,1)S(1)}, bf16[768,512]{1,0:T(8,128)(2,1)S(1)}, bf16[512,384]{1,0:T(8,128)(2,1)S(1)}, bf16[512,384]{1,0:T(8,128)(2,1)S(1)}) custom-call(bf16[640,768]{1,0:T(8,128)(2,1)S(1)} %copy-done.30, bf16[640,2048]{1,0:T(8,128)(2,1)} %get-tuple-element.113.refs_1_, ...), custom_call_target="tpu_custom_call" | custom-call | flops 5000000000 | bytes 12500000 | tf_op jit(solution)/shard_map/ffn_weights_grad/pallas_call | solution.py:749
  246.7 3.2 attention_weights_grad.3
  271.9 78.3 %reduce-scatter.22.cloned.1.call-done = f32[48,2]{1,0:T(8,128)} async-done(((f32[768,2]{1,0:T(8,128)}), f32[48,2]{1,0:T(8,128)}) %reduce-scatter.22.cloned.1.call-update) | async-done | bytes 400
  354.6 18.3 %reduce-scatter.20.cloned.1.call-done = bf16[128,384]{1,0:T(8,128)(2,1)} async-done(((bf16[512,384]{1,0:T(8,128)(2,1)}), bf16[128,384]{1,0:T(8,128)(2,1)}) %reduce-scatter.20.cloned.1.call-update) | async-done | bytes 98320 | tf_op jit(solution)/shard_map/reduce_scatter | solution.py:786
  372.9 21.7 %reduce-scatter.18.cloned.1.call-done = bf16[128,384]{1,0:T(8,128)(2,1)} async-done(((bf16[512,384]{1,0:T(8,128)(2,1)}), bf16[128,384]{1,0:T(8,128)(2,1)}) %reduce-scatter.18.cloned.1.call-update) | async-done | bytes 98320 | tf_op jit(solution)/shard_map/reduce_scatter | solution.py:786
  397.0 20.1 %reduce-scatter.12.cloned.1.call-done = bf16[192,384]{1,0:T(8,128)(2,1)} async-done(((bf16[768,384]{1,0:T(8,128)(2,1)}), bf16[192,384]{1,0:T(8,128)(2,1)}) %reduce-scatter.12.cloned.1.call-update) | async-done | bytes 147472 | tf_op jit(solution)/shard_map/reduce_scatter | solution.py:786
  417.1 22.6 %reduce-scatter.10.cloned.1.call-done = bf16[192,384]{1,0:T(8,128)(2,1)} async-done(((bf16[768,384]{1,0:T(8,128)(2,1)}), bf16[192,384]{1,0:T(8,128)(2,1)}) %reduce-scatter.10.cloned.1.call-update) | async-done | bytes 147472 | tf_op jit(solution)/shard_map/reduce_scatter | solution.py:786
  442.1 21.6 %reduce-scatter.16.cloned.1.call-done = bf16[192,512]{1,0:T(8,128)(2,1)} async-done(((bf16[768,512]{1,0:T(8,128)(2,1)}), bf16[192,512]{1,0:T(8,128)(2,1)}) %reduce-scatter.16.cloned.1.call-update) | async-done | bytes 196624 | tf_op jit(solution)/shard_map/reduce_scatter | solution.py:786
  463.7 25.0 %reduce-scatter.14.cloned.1.call-done = bf16[192,512]{1,0:T(8,128)(2,1)} async-done(((bf16[768,512]{1,0:T(8,128)(2,1)}), bf16[192,512]{1,0:T(8,128)(2,1)}) %reduce-scatter.14.cloned.1.call-update) | async-done | bytes 196624 | tf_op jit(solution)/shard_map/reduce_scatter | solution.py:786
  (399 shorter events, 142.8 us)
Async XLA Ops:
  7.2 343.0 %reduce-scatter.22.cloned.1.call-start = ((), (), s32[]{:S(2)}) async-start(), calls=%async_computation.13 | async-start | bytes 417792
  11.2 20.2 %collective-permute-start.4 = (bf16[1,768,768]{2,1,0:T(8,128)(2,1)}, bf16[1,768,768]{2,1,0:T(8,128)(2,1)S(1)}, u32[]{:S(2)}, u32[]{:S(2)}) collective-permute-start(bf16[1,768,768]{2,1,0:T(8,128)(2,1)} %q_own.7), channel_id=1, source_target_pairs={{0,16},{16,0},{1,17},{17,1},{2,18},{18,2},{3,19},{19,3},{4,20},{20... | collective-permute-start | bytes 3538952 | tf_op jit(solution)/shard_map/ppermute | solution.py:769
  12.5 56.3 %collective-permute-start.11 = (bf16[1,768,2048]{2,1,0:T(8,128)(2,1)}, bf16[1,768,2048]{2,1,0:T(8,128)(2,1)S(1)}, u32[]{:S(2)}, u32[]{:S(2)}) collective-permute-start(bf16[1,768,2048]{2,1,0:T(8,128)(2,1)} %refs_8_.3), channel_id=1, source_target_pairs={{0,16},{16,0},{1,17},{17,1},{2,18},{18,2},{3,19},{19,3},{4,20},{20... | collective-permute-start | bytes 9437192 | tf_op jit(solution)/shard_map/ppermute | solution.py:769
  12.6 56.2 %collective-permute-start.12 = (bf16[1,768,2048]{2,1,0:T(8,128)(2,1)}, bf16[1,768,2048]{2,1,0:T(8,128)(2,1)S(1)}, u32[]{:S(2)}, u32[]{:S(2)}) collective-permute-start(bf16[1,768,2048]{2,1,0:T(8,128)(2,1)} %refs_10_.3), channel_id=1, source_target_pairs={{0,16},{16,0},{1,17},{17,1},{2,18},{18,2},{3,19},{19,3},{4,20},{20... | collective-permute-start | bytes 9437192 | tf_op jit(solution)/shard_map/ppermute | solution.py:769
  14.1 56.4 %collective-permute-start.13 = (bf16[1,2048,768]{2,1,0:T(8,128)(2,1)}, bf16[1,2048,768]{2,1,0:T(8,128)(2,1)}, u32[]{:S(2)}, u32[]{:S(2)}) collective-permute-start(bf16[1,2048,768]{2,1,0:T(8,128)(2,1)} %refs_12_.1), channel_id=1, source_target_pairs={{0,16},{16,0},{1,17},{17,1},{2,18},{18,2},{3,19},{19,3},{4,20},{20... | collective-permute-start | bytes 9437192 | tf_op jit(solution)/shard_map/ppermute | solution.py:769
  140.4 24.5 %collective-permute-start.45 = (bf16[160,768]{1,0:T(8,128)(2,1)}, bf16[160,768]{1,0:T(8,128)(2,1)S(1)}, u32[]{:S(2)}, u32[]{:S(2)}) collective-permute-start(bf16[160,768]{1,0:T(8,128)(2,1)} %dynamic-slice_bitcast_fusion.cotangent.refs_4_), channel_id=1, source_target_pairs={{0,1},{1,0},{2,3},{3,2},{4,5},{5,4},{6,7},{7,6},{8,9},{9,8},{10,11... | collective-permute-start | bytes 737288 | tf_op jit(solution)/shard_map/ppermute | solution.py:773
  164.0 24.5 %collective-permute-start.46 = (bf16[160,768]{1,0:T(8,128)(2,1)}, bf16[160,768]{1,0:T(8,128)(2,1)}, u32[]{:S(2)}, u32[]{:S(2)}) collective-permute-start(bf16[160,768]{1,0:T(8,128)(2,1)} %dynamic-slice_bitcast_fusion.cotangent.refs_4_), channel_id=1, source_target_pairs={{0,2},{1,3},{2,0},{3,1},{4,6},{5,7},{6,4},{7,5},{8,10},{9,11},{10,... | collective-permute-start | bytes 737288 | tf_op jit(solution)/shard_map/ppermute | solution.py:773
  165.6 24.0 %collective-permute-start.47 = (bf16[160,768]{1,0:T(8,128)(2,1)}, bf16[160,768]{1,0:T(8,128)(2,1)S(1)}, u32[]{:S(2)}, u32[]{:S(2)}) collective-permute-start(bf16[160,768]{1,0:T(8,128)(2,1)} %dynamic-slice_bitcast_fusion.cotangent.refs_4_), channel_id=1, source_target_pairs={{0,3},{1,2},{2,1},{3,0},{4,7},{5,6},{6,5},{7,4},{8,11},{9,10},{10,... | collective-permute-start | bytes 737288 | tf_op jit(solution)/shard_map/ppermute | solution.py:773
  167.7 22.9 %collective-permute-start.42 = (bf16[160,768]{1,0:T(8,128)(2,1)}, bf16[160,768]{1,0:T(8,128)(2,1)S(1)}, u32[]{:S(2)}, u32[]{:S(2)}) collective-permute-start(bf16[160,768]{1,0:T(8,128)(2,1)} %get-tuple-element.116.refs_0_), channel_id=1, source_target_pairs={{0,1},{1,0},{2,3},{3,2},{4,5},{5,4},{6,7},{7,6},{8,9},{9,8},{10,11... | collective-permute-start | bytes 737288 | tf_op jit(solution)/shard_map/ppermute | solution.py:773
  169.5 22.7 %collective-permute-start.43 = (bf16[160,768]{1,0:T(8,128)(2,1)}, bf16[160,768]{1,0:T(8,128)(2,1)S(1)}, u32[]{:S(2)}, u32[]{:S(2)}) collective-permute-start(bf16[160,768]{1,0:T(8,128)(2,1)} %get-tuple-element.116.refs_0_), channel_id=1, source_target_pairs={{0,2},{1,3},{2,0},{3,1},{4,6},{5,7},{6,4},{7,5},{8,10},{9,11},{10,... | collective-permute-start | bytes 737288 | tf_op jit(solution)/shard_map/ppermute | solution.py:773
  170.4 21.8 %collective-permute-start.44 = (bf16[160,768]{1,0:T(8,128)(2,1)}, bf16[160,768]{1,0:T(8,128)(2,1)S(1)}, u32[]{:S(2)}, u32[]{:S(2)}) collective-permute-start(bf16[160,768]{1,0:T(8,128)(2,1)} %get-tuple-element.116.refs_0_), channel_id=1, source_target_pairs={{0,3},{1,2},{2,1},{3,0},{4,7},{5,6},{6,5},{7,4},{8,11},{9,10},{10,... | collective-permute-start | bytes 737288 | tf_op jit(solution)/shard_map/ppermute | solution.py:773
  211.2 35.4 %collective-permute-start.33 = (bf16[960,128]{1,0:T(8,128)(2,1)}, bf16[960,128]{1,0:T(8,128)(2,1)}, u32[]{:S(2)}, u32[]{:S(2)}) collective-permute-start(bf16[960,128]{1,0:T(8,128)(2,1)} %get-tuple-element.109.o_0), channel_id=1, source_target_pairs={{0,1},{1,0},{2,3},{3,2},{4,5},{5,4},{6,7},{7,6},{8,9},{9,8},{10,11... | collective-permute-start | bytes 737288 | tf_op jit(solution)/shard_map/ppermute | solution.py:773
  212.2 34.4 %collective-permute-start.34 = (bf16[960,128]{1,0:T(8,128)(2,1)}, bf16[960,128]{1,0:T(8,128)(2,1)}, u32[]{:S(2)}, u32[]{:S(2)}) collective-permute-start(bf16[960,128]{1,0:T(8,128)(2,1)} %get-tuple-element.109.o_0), channel_id=1, source_target_pairs={{0,2},{1,3},{2,0},{3,1},{4,6},{5,7},{6,4},{7,5},{8,10},{9,11},{10,... | collective-permute-start | bytes 737288 | tf_op jit(solution)/shard_map/ppermute | solution.py:773
  214.3 21.7 %collective-permute-start.39 = (bf16[160,768]{1,0:T(8,128)(2,1)S(1)}, bf16[160,768]{1,0:T(8,128)(2,1)S(1)}, u32[]{:S(2)}, u32[]{:S(2)}) collective-permute-start(bf16[160,768]{1,0:T(8,128)(2,1)S(1)} %get-tuple-element.87.grad_in.refs_2_), channel_id=1, source_target_pairs={{0,2},{1,3},{2,0},{3,1},{4,6},{5,7},{6,4},{7,5},{8,10},{9,11},{10,... | collective-permute-start | bytes 737288 | tf_op jit(solution)/shard_map/ppermute | solution.py:773
  216.2 156.6 %reduce-scatter.20.cloned.1.call-start = ((), (), s32[]{:S(2)}) async-start(), calls=%async_computation.12 | async-start | bytes 491520 | tf_op jit(solution)/shard_map/reduce_scatter | solution.py:786
  216.3 19.7 %collective-permute-start.40 = (bf16[160,768]{1,0:T(8,128)(2,1)S(1)}, bf16[160,768]{1,0:T(8,128)(2,1)S(1)}, u32[]{:S(2)}, u32[]{:S(2)}) collective-permute-start(bf16[160,768]{1,0:T(8,128)(2,1)S(1)} %get-tuple-element.87.grad_in.refs_2_), channel_id=1, source_target_pairs={{0,3},{1,2},{2,1},{3,0},{4,7},{5,6},{6,5},{7,4},{8,11},{9,10},{10,... | collective-permute-start | bytes 737288 | tf_op jit(solution)/shard_map/ppermute | solution.py:773
  219.7 174.9 %reduce-scatter.18.cloned.1.call-start = ((), (), s32[]{:S(2)}) async-start(), calls=%async_computation.11 | async-start | bytes 491520 | tf_op jit(solution)/shard_map/reduce_scatter | solution.py:786
  225.5 21.1 %collective-permute-start.35 = (bf16[960,128]{1,0:T(8,128)(2,1)}, bf16[960,128]{1,0:T(8,128)(2,1)S(1)}, u32[]{:S(2)}, u32[]{:S(2)}) collective-permute-start(bf16[960,128]{1,0:T(8,128)(2,1)} %get-tuple-element.109.o_0), channel_id=1, source_target_pairs={{0,3},{1,2},{2,1},{3,0},{4,7},{5,6},{6,5},{7,4},{8,11},{9,10},{10,... | collective-permute-start | bytes 737288 | tf_op jit(solution)/shard_map/ppermute | solution.py:773
  251.2 165.9 %reduce-scatter.12.cloned.1.call-start = ((), (), s32[]{:S(2)}) async-start(), calls=%async_computation.8 | async-start | bytes 737280 | tf_op jit(solution)/shard_map/reduce_scatter | solution.py:786
  254.3 185.3 %reduce-scatter.10.cloned.1.call-start = ((), (), s32[]{:S(2)}) async-start(), calls=%async_computation.7 | async-start | bytes 737280 | tf_op jit(solution)/shard_map/reduce_scatter | solution.py:786
  265.1 198.5 %reduce-scatter.16.cloned.1.call-start = ((), (), s32[]{:S(2)}) async-start(), calls=%async_computation.10 | async-start | bytes 983040 | tf_op jit(solution)/shard_map/reduce_scatter | solution.py:786
  268.8 219.8 %reduce-scatter.14.cloned.1.call-start = ((), (), s32[]{:S(2)}) async-start(), calls=%async_computation.9 | async-start | bytes 983040 | tf_op jit(solution)/shard_map/reduce_scatter | solution.py:786
  270.0 82.3 %collective-permute-start.41 = (bf16[768,512]{1,0:T(8,128)(2,1)S(1)}, bf16[768,512]{1,0:T(8,128)(2,1)}, u32[]{:S(2)}, u32[]{:S(2)}) collective-permute-start(bf16[768,512]{1,0:T(8,128)(2,1)S(1)} %copy-done.57), channel_id=1, source_target_pairs={{0,16},{16,0},{1,17},{17,1},{2,18},{18,2},{3,19},{19,3},{4,20},{20... | collective-permute-start | bytes 2359304 | tf_op jit(solution)/shard_map/ppermute | solution.py:769
  271.4 83.1 %collective-permute-start.30 = (bf16[160,768]{1,0:T(8,128)(2,1)S(1)}, bf16[160,768]{1,0:T(8,128)(2,1)S(1)}, u32[]{:S(2)}, u32[]{:S(2)}) collective-permute-start(bf16[160,768]{1,0:T(8,128)(2,1)S(1)} %broadcast_select_fusion), channel_id=1, source_target_pairs={{0,16},{16,0},{1,17},{17,1},{2,18},{18,2},{3,19},{19,3},{4,20},{20... | collective-permute-start | bytes 737288 | tf_op jit(solution)/shard_map/ppermute | solution.py:769
  (162 other events, 1399.3 us)
Sparse Core Ops, SparseCore 0:
  216.3 133.7 reduce-scatter.21
  353.1 19.6 reduce-scatter.19
  375.7 18.8 reduce-scatter.17
  396.9 20.1 reduce-scatter.11
  419.3 20.2 reduce-scatter.9
  441.9 21.7 reduce-scatter.15
  466.1 22.5 reduce-scatter.13

commit v2 on v1

v2 whole, which is shorter than its diff:
```python
import functools

import jax
import jax.numpy as jnp
import numpy as np
from jax import lax
from jax.experimental import pallas as pl
from jax.experimental.pallas import tpu as pltpu
from jax.sharding import PartitionSpec as P

DIM = 768
HEAD_DIM = 64
FF = 2048
ROWS = 160
PARTS = 4
SLOTS = ROWS * PARTS
SHARE_HEADS = 3
SHARE = SHARE_HEADS * HEAD_DIM
FF_SHARE = FF // PARTS
PACKED = SLOTS * 3 // 2
PACKED_ROWS = ROWS * 3 // 2
WINDOW = 256
QUERY_BLOCKS = ((0, 256), (256, 256), (512, 128))
HALVES = ((0, 320), (320, 320))

epsilon = 1e-05
masked_score = -1e30
bf16 = jnp.bfloat16
f32 = jnp.float32
MIB = 1 << 20
VMEM_MIB = 60
GAIN_ROWS = 16
COST = 10**9


def nn(left, right):
    return lax.dot_general(left, right, (((1,), (0,)), ((), ())), preferred_element_type=f32)


def nt(left, right):
    return lax.dot_general(left, right, (((1,), (1,)), ((), ())), preferred_element_type=f32)


def tn(left, right):
    return lax.dot_general(left, right, (((0,), (0,)), ((), ())), preferred_element_type=f32)


def rms_scale(values):
    return lax.rsqrt(jnp.mean(values * values, axis=-1, keepdims=True) + epsilon)


def rotate(values, cosine, signed_sine):
    width = values.shape[-1]
    lane = lax.broadcasted_iota(jnp.int32, values.shape, 1)
    ahead = pltpu.roll(values, width - 32, 1)
    behind = pltpu.roll(values, 32, 1)
    partner = jnp.where(lane % HEAD_DIM < 32, ahead, behind)
    return values * cosine + partner * signed_sine


def wide(table):
    return jnp.concatenate([table, table], axis=1)


def unpack(packed, count):
    tail = packed[count:]
    third = jnp.concatenate([tail[:, :HEAD_DIM], tail[:, HEAD_DIM:]], axis=0)
    return jnp.concatenate([packed[:count], third], axis=1)


def gain_row(gains, kind):
    rows = gains[...].astype(f32)
    return jnp.concatenate([rows[3 * kind + part : 3 * kind + part + 1, :] for part in range(3)], axis=1)


def place():
    return lax.axis_index("section"), lax.axis_index("seq")


def block_rows(index, size=ROWS):
    return pl.ds(pl.multiple_of(index * size, size), size)


def window_start(seq):
    return pl.multiple_of(((3 * seq) >> 1) * 128, 128)


class Mover:
    def __init__(self, sems, core=None):
        self.sems = sems
        self.core = core
        self.count = 0
        self.sent = []

    def next_sem(self):
        self.count += 1
        return self.sems.at[self.count - 1]

    def fetch(self, source, target):
        copy = pltpu.make_async_copy(source, target, self.next_sem())
        copy.start()
        return copy

    def fetch_all(self, sources, targets):
        return [self.fetch(source, target) for source, target in zip(sources, targets)]

    def fetch_layer(self, layer, own, other, target):
        sem = self.next_sem()

        @pl.when(self.core == layer)
        def _():
            pltpu.make_async_copy(own, target, sem).start()

        @pl.when(self.core != layer)
        def _():
            pltpu.make_async_copy(other, target, sem).start()

        return pltpu.make_async_copy(own, target, sem)

    def fetch_windows(self, layer, pair, targets):
        return [
            self.fetch_layer(layer, pair[0].at[block_rows(kind, DIM), :], pair[1].at[block_rows(kind, DIM), :], target)
            for kind, target in enumerate(targets)
        ]

    def fetch_gains(self, layer, pair, target):
        rows = slice(3 * DIM, 3 * DIM + GAIN_ROWS)
        return self.fetch_layer(layer, pair[0].at[rows, :], pair[1].at[rows, :], target)

    def fetch_ffn(self, layer, pairs, targets):
        copies = []
        for part in range(PARTS):
            span = slice(part * FF_SHARE, (part + 1) * FF_SHARE)
            (g_own, g_other), (u_own, u_other), (d_own, d_other) = pairs
            copies.append(
                (
                    self.fetch_layer(layer, g_own.at[0, :, span], g_other.at[0, :, span], targets[0].at[part]),
                    self.fetch_layer(layer, u_own.at[0, :, span], u_other.at[0, :, span], targets[1].at[part]),
                    self.fetch_layer(layer, d_own.at[0, span, :], d_other.at[0, span, :], targets[2].at[span, :]),
                )
            )
        return copies

    def send(self, source, target):
        copy = pltpu.make_async_copy(source, target, self.next_sem())
        copy.start()
        self.sent.append(copy)

    def finish(self):
        for copy in self.sent:
            copy.wait()


def wait(copies):
    for copy in copies:
        copy.wait()


def project(normed, windows, odd, cos, sin, heads, value_t):
    for first, count in QUERY_BLOCKS:
        rows = slice(first, first + count)
        block = normed[rows, :]
        cosine, sine = wide(cos[rows, :]), wide(sin[rows, :])
        for kind, window in enumerate(windows):
            result = nn(block, window[...])
            if kind < 2:
                result = rotate(result, cosine, sine)
            if kind == 0:
                result = result * HEAD_DIM ** (-0.5)
            result = jnp.where(odd, pltpu.roll(result, WINDOW - HEAD_DIM, 1), result)
            low = result.astype(bf16)
            for head in range(SHARE_HEADS):
                heads[kind, head, rows, :] = low[:, head * HEAD_DIM : (head + 1) * HEAD_DIM]
            if kind == 2:
                turned = jnp.transpose(result).astype(bf16)
                for head in range(SHARE_HEADS):
                    value_t[head, :, rows] = turned[head * HEAD_DIM : (head + 1) * HEAD_DIM, :]


def masked(scores_t, first, length):
    spots = lax.broadcasted_iota(jnp.int32, scores_t.shape, 0)
    query = first + lax.broadcasted_iota(jnp.int32, (1, scores_t.shape[1]), 1)
    bound = jnp.minimum(query + 1, length)
    return jnp.where(spots < bound, scores_t, masked_score)


def attend(heads, value_t, length, mixed_t):
    for head in range(SHARE_HEADS):
        for first, count in QUERY_BLOCKS:
            last = first + count
            scores = nt(heads[1, head, :last, :], heads[0, head, first:last, :])
            scores = masked(scores, first, length)
            exponent = jnp.exp(scores - jnp.max(scores, axis=0, keepdims=True))
            total = jnp.sum(exponent, axis=0, keepdims=True)
            mixed = nn(value_t[head, :, :last], exponent.astype(bf16))
            mixed_t[head, :, first:last] = mixed * (1.0 / total)


def untranspose(mixed_t, pair, single):
    both = jnp.concatenate([mixed_t[0], mixed_t[1]], axis=0)
    pair[...] = jnp.transpose(both).astype(bf16)
    last = jnp.concatenate([mixed_t[2], mixed_t[2]], axis=0)
    single[...] = jnp.transpose(last).astype(bf16)


def pack_all(pair, single, target):
    half = SLOTS // 2
    target[:SLOTS, :] = pair[...]
    target[SLOTS:, :] = jnp.concatenate(
        [single[:half, :HEAD_DIM], single[half:, :HEAD_DIM]], axis=1
    )


def pack_block(pair, single, index, target):
    half = ROWS // 2
    rows = block_rows(index)
    target[:ROWS, :] = pair[rows, :]
    tail = single[rows, :]
    target[ROWS:, :] = jnp.concatenate([tail[:half, :HEAD_DIM], tail[half:, :HEAD_DIM]], axis=1)


def columns_of(array, first, rows=slice(None)):
    return array[rows, first * 128 : (first + 1) * 128]


def norm_back(grad_normed, gain, normed, scale):
    scaled = grad_normed * gain
    return scale * (scaled - normed * jnp.mean(scaled * normed, axis=-1, keepdims=True))


def ffn_back_chunk(gate, up, grad_hidden):
    sigmoid = jax.nn.sigmoid(gate)
    grad_gate = grad_hidden * up * sigmoid * (1.0 + gate * (1.0 - sigmoid))
    grad_up = grad_hidden * gate * sigmoid
    return grad_gate.astype(bf16), grad_up.astype(bf16)


def pack_windows(seq_weights_h, gains_h, packed_h, packed, gains, sems):
    _, seq = place()
    move = Mover(sems)
    span = pl.ds(window_start(seq), WINDOW)
    copies = move.fetch_all(gains_h, gains)
    copies += [
        move.fetch(weight.at[0, :, span], packed.at[block_rows(kind, DIM), :])
        for kind, weight in enumerate(seq_weights_h)
    ]
    wait(copies)
    rows = [gain[:, part * WINDOW : (part + 1) * WINDOW].astype(f32) for gain in gains for part in range(3)]
    rows.append(jnp.zeros((GAIN_ROWS - 6, WINDOW), f32))
    packed[3 * DIM :, :] = jnp.concatenate(rows, axis=0).astype(bf16)
    move.send(packed, packed_h)
    move.finish()


def first_attention(
    x_h, lengths, cos_h, sin_h, windows_h,
    normed_h, heads_h, packed_h,
    x_blocks, gains, cos, sin, windows, normed, heads, packed, value_t, mixed_t, pair, single, sems,
):
    core, seq = place()
    move = Mover(sems, core)
    copies_x = move.fetch_all(x_h, x_blocks)
    copy_gains = move.fetch_gains(0, windows_h, gains)
    copies_qkv = move.fetch_windows(0, windows_h, windows)
    copies_table = move.fetch_all((cos_h, sin_h), (cos, sin))
    copy_gains.wait()
    gain = gain_row(gains, 0)
    for offset, block in enumerate(x_blocks):
        copies_x[offset].wait()
        wide_block = block[...].astype(f32)
        normed[block_rows(seq ^ offset), :] = (wide_block * rms_scale(wide_block) * gain).astype(bf16)
    move.send(normed, normed_h)
    wait(copies_table + copies_qkv)
    project(normed, windows, seq % 2 == 1, cos, sin, heads, value_t)
    move.send(heads, heads_h)
    attend(heads, value_t, lengths[core], mixed_t)
    untranspose(mixed_t, pair, single)
    pack_all(pair, single, packed)
    move.send(packed, packed_h)
    move.finish()


def middle(
    x_h, mixed_h, lengths, cos_h, sin_h, o_h, ffn_h, windows_h,
    after_h, normed_two_h, hidden_h, mid_h, normed_h, heads_h, packed_h, blocks_h,
    x_blocks, mixed, gains, gains_next, cos, sin, w_o, w_g, w_u, w_d, windows,
    after, normed_two, hidden, mid, normed, heads, packed, blocks, total, value_t, mixed_t, pair, single, sems,
):
    core, seq = place()
    move = Mover(sems, core)
    copies_x = move.fetch_all(x_h, x_blocks)
    copy_o = move.fetch_layer(0, o_h[0].at[0], o_h[1].at[0], w_o)
    copies_gain = [move.fetch_gains(0, windows_h, gains), move.fetch_gains(1, windows_h, gains_next)]
    copies_mixed = move.fetch_all(mixed_h, mixed)
    copies_ffn = move.fetch_ffn(0, ffn_h, (w_g, w_u, w_d))
    copies_qkv = move.fetch_windows(1, windows_h, windows)
    copies_table = move.fetch_all((cos_h, sin_h), (cos, sin))
    for offset, block in enumerate(x_blocks):
        copies_x[offset].wait()
        after[block_rows(seq ^ offset), :] = block[...].astype(f32)
    copy_o.wait()
    for offset, block in enumerate(mixed):
        share = w_o[block_rows(seq ^ offset, SHARE), :]
        copies_mixed[offset].wait()
        whole = unpack(block[...], SLOTS)
        for first, count in HALVES:
            rows = slice(first, first + count)
            after[rows, :] += nn(whole[rows], share)
    wait(copies_gain)
    gain_ffn = gain_row(gains, 1)
    gain_attn = gain_row(gains_next, 0)
    for first, count in HALVES:
        rows = slice(first, first + count)
        block = after[rows, :]
        normed_two[rows, :] = (block * rms_scale(block) * gain_ffn).astype(bf16)
        total[rows, :] = block
    move.send(after.at[block_rows(seq), :], after_h)
    move.send(normed_two, normed_two_h)
    for part in range(PARTS):
        wait(copies_ffn[part])
        span = slice(part * FF_SHARE, (part + 1) * FF_SHARE)
        for first, count in HALVES:
            rows = slice(first, first + count)
            block = normed_two[rows, :]
            gate = nn(block, w_g[part])
            up = nn(block, w_u[part])
            low = (gate * jax.nn.sigmoid(gate) * up).astype(bf16)
            hidden[rows, span] = low
            total[rows, :] += nn(low, w_d[span, :])
    move.send(hidden, hidden_h)
    for first, count in HALVES:
        rows = slice(first, first + count)
        low = total[rows, :].astype(bf16)
        mid[rows, :] = low
        block = low.astype(f32)
        normed[rows, :] = (block * rms_scale(block) * gain_attn).astype(bf16)
    move.send(mid.at[block_rows(seq), :], mid_h)
    move.send(normed, normed_h)
    wait(copies_table + copies_qkv)
    project(normed, windows, seq % 2 == 1, cos, sin, heads, value_t)
    move.send(heads, heads_h)
    attend(heads, value_t, lengths[core], mixed_t)
    untranspose(mixed_t, pair, single)
    for offset, (block, target) in enumerate(zip(blocks, blocks_h)):
        pack_block(pair, single, seq ^ offset, block)
        move.send(block, target)
    pack_all(pair, single, packed)
    move.send(packed, packed_h)
    move.finish()


def send_blocks(move, seq, grad_branch, w_o, blocks, blocks_h):
    for here in range(PARTS):

        @pl.when(seq == here)
        def _():
            for offset, block in enumerate(blocks):
                other = here ^ offset
                span = slice(other * SHARE, (other + 1) * SHARE)
                grad_heads = nt(grad_branch[...], w_o[span, :]).astype(bf16)
                block[...] = jnp.concatenate([grad_heads, grad_branch[:, span]], axis=1)

    for block, target in zip(blocks, blocks_h):
        move.send(block, target)


def last_rows(
    mid_h, cotangent_h, mixed_h, windows_h, o_h, ffn_h,
    output_h, normed_two_h, grad_after_h, grad_gain_h, blocks_h,
    mid, cotangent, mixed, gains, w_o, w_g, w_u, w_d,
    output, normed_two, grad_after, grad_gain, blocks, branch, hidden, sems,
):
    core, seq = place()
    move = Mover(sems, core)
    copies = move.fetch_all((mid_h, cotangent_h.at[core]), (mid, cotangent))
    copies.append(move.fetch_gains(1, windows_h, gains))
    copy_o = move.fetch_layer(1, o_h[0].at[0], o_h[1].at[0], w_o)
    copies_mixed = move.fetch_all(mixed_h, mixed)
    copies_ffn = move.fetch_ffn(1, ffn_h, (w_g, w_u, w_d))
    wait(copies)
    gain = gain_row(gains, 1)
    copy_o.wait()
    after = mid[...].astype(f32)
    for offset, block in enumerate(mixed):
        copies_mixed[offset].wait()
        after = after + nn(unpack(block[...], ROWS), w_o[block_rows(seq ^ offset, SHARE), :])
    scale = rms_scale(after)
    normed = after * scale
    low = (normed * gain).astype(bf16)
    normed_two[...] = low
    move.send(normed_two, normed_two_h)
    grad_low = cotangent[...]
    grad_normed = jnp.zeros((ROWS, DIM), f32)
    for part in range(PARTS):
        wait(copies_ffn[part])
        gate = nn(low, w_g[part])
        up = nn(low, w_u[part])
        span = slice(part * FF_SHARE, (part + 1) * FF_SHARE)
        hidden[:, span] = (gate * jax.nn.sigmoid(gate) * up).astype(bf16)
        grad_gate, grad_up = ffn_back_chunk(gate, up, nt(grad_low, w_d[span, :]))
        grad_normed = grad_normed + nt(grad_gate, w_g[part]) + nt(grad_up, w_u[part])
    grad_gain[...] = jnp.sum(grad_normed * normed, axis=0, keepdims=True)
    move.send(grad_gain, grad_gain_h)
    total = grad_low.astype(f32) + norm_back(grad_normed, gain, normed, scale)
    grad_after[...] = total
    move.send(grad_after, grad_after_h)
    branch[...] = total.astype(bf16)
    send_blocks(move, seq, branch, w_o, blocks, blocks_h)
    output[...] = (after + nn(hidden[...], w_d[...])).astype(bf16)
    move.send(output, output_h)
    move.finish()


def first_rows_back(
    after_h, grad_in_h, windows_h, o_h, ffn_h,
    grad_after_h, grad_gain_h, blocks_h,
    after_own, grad_in, gains, w_o, w_g, w_u, w_d, grad_after, grad_gain, blocks, branch, sems,
):
    core, seq = place()
    move = Mover(sems, core)
    copies = move.fetch_all((after_h, grad_in_h), (after_own, grad_in))
    copies.append(move.fetch_gains(0, windows_h, gains))
    copies_ffn = move.fetch_ffn(0, ffn_h, (w_g, w_u, w_d))
    copy_o = move.fetch_layer(0, o_h[0].at[0], o_h[1].at[0], w_o)
    wait(copies)
    gain = gain_row(gains, 1)
    after = after_own[...]
    scale = rms_scale(after)
    normed = after * scale
    low = (normed * gain).astype(bf16)
    grad_low = grad_in[...]
    grad_normed = jnp.zeros((ROWS, DIM), f32)
    for part in range(PARTS):
        wait(copies_ffn[part])
        gate = nn(low, w_g[part])
        up = nn(low, w_u[part])
        span = slice(part * FF_SHARE, (part + 1) * FF_SHARE)
        grad_gate, grad_up = ffn_back_chunk(gate, up, nt(grad_low, w_d[span, :]))
        grad_normed = grad_normed + nt(grad_gate, w_g[part]) + nt(grad_up, w_u[part])
    grad_gain[...] = jnp.sum(grad_normed * normed, axis=0, keepdims=True)
    move.send(grad_gain, grad_gain_h)
    total = grad_low.astype(f32) + norm_back(grad_normed, gain, normed, scale)
    grad_after[...] = total
    move.send(grad_after, grad_after_h)
    branch[...] = total.astype(bf16)
    copy_o.wait()
    send_blocks(move, seq, branch, w_o, blocks, blocks_h)
    move.finish()


def attention_back(
    grads_h, lengths, cos_h, sin_h, heads_h,
    blocks_h,
    grads, cos, sin, heads, grad_mixed, key_t, query_grad_t, key_grad, value_grad, whole, sems,
):
    core, seq = place()
    move = Mover(sems)
    copies_grads = move.fetch_all(grads_h, grads)
    copy_heads = move.fetch(heads_h, heads)
    copies_table = move.fetch_all((cos_h, sin_h), (cos, sin))
    key_grad[...] = jnp.zeros_like(key_grad)
    value_grad[...] = jnp.zeros_like(value_grad)
    for offset, block in enumerate(grads):
        copies_grads[offset].wait()
        low = block[:, :SHARE]
        for head in range(SHARE_HEADS):
            grad_mixed[head, block_rows(seq ^ offset), :] = low[:, head * HEAD_DIM : (head + 1) * HEAD_DIM]
    copy_heads.wait()
    length = lengths[core]

    for head in range(SHARE_HEADS):
        key_wide = heads[1, head].astype(f32)
        key_t[...] = jnp.transpose(jnp.concatenate([key_wide, key_wide], axis=1))[:HEAD_DIM].astype(bf16)
        for first, count in QUERY_BLOCKS:
            last = first + count
            query = heads[0, head, first:last, :]
            grad = grad_mixed[head, first:last, :]
            scores = nt(heads[1, head, :last, :], query)
            scores = masked(scores, first, length)
            exponent = jnp.exp(scores - jnp.max(scores, axis=0, keepdims=True))
            weights = exponent * (1.0 / jnp.sum(exponent, axis=0, keepdims=True))
            grad_weights = nt(heads[2, head, :last, :], grad)
            row_total = jnp.sum(weights * grad_weights, axis=0, keepdims=True)
            grad_scores = (weights * (grad_weights - row_total)).astype(bf16)
            value_grad[head, :last, :] += nn(weights.astype(bf16), grad)
            key_grad[head, :last, :] += nn(grad_scores, query)
            query_grad_t[head, :, first:last] = nn(key_t[:, :last], grad_scores) * HEAD_DIM ** (-0.5)

    turned = jnp.concatenate([query_grad_t[0], query_grad_t[1], query_grad_t[2], query_grad_t[2]], axis=0)
    query_side = jnp.transpose(turned)
    key_side = jnp.concatenate([key_grad[0], key_grad[1], key_grad[2], key_grad[2]], axis=1)
    value_side = jnp.concatenate([value_grad[0], value_grad[1], value_grad[2]], axis=1)
    wait(copies_table)
    cosine, sine = wide(cos[...]), wide(sin[...])
    query_side = rotate(query_side, cosine, -sine)[:, :SHARE]
    key_side = rotate(key_side, cosine, -sine)[:, :SHARE]
    whole[...] = jnp.concatenate([query_side, key_side, value_side], axis=1).astype(bf16)
    for offset, target in enumerate(blocks_h):
        move.send(whole.at[block_rows(seq ^ offset), :], target)
    move.finish()


def input_back(
    layer, blocks_h, inputs_h, grad_after_h, windows_h, qkv_h,
    grad_in_h, grad_gain_h,
    blocks, inputs, grad_after, gains, weights, grad_in, grad_gain, sides, sems,
):
    core, seq = place()
    move = Mover(sems, core)
    copies_blocks = move.fetch_all(blocks_h, blocks)
    copies = move.fetch_all((inputs_h, grad_after_h), (inputs, grad_after))
    copies.append(move.fetch_gains(layer, windows_h, gains))
    copies_qkv = [
        move.fetch_layer(layer, own.at[0], other.at[0], target) for (own, other), target in zip(qkv_h, weights)
    ]
    wait(copies_blocks)
    for here in range(PARTS):

        @pl.when(seq == here)
        def _():
            for kind in range(3):
                span = slice(kind * SHARE, (kind + 1) * SHARE)
                sides[kind] = jnp.concatenate(
                    [blocks[here ^ part][:, span] for part in range(PARTS)], axis=1
                )

    wait(copies)
    gain = gain_row(gains, 0)
    wide_inputs = inputs[...].astype(f32)
    scale = rms_scale(wide_inputs)
    normed = wide_inputs * scale
    grad_normed = jnp.zeros((ROWS, DIM), f32)
    for kind, weight in enumerate(weights):
        copies_qkv[kind].wait()
        grad_normed = grad_normed + nt(sides[kind], weight[...])
    grad_in[...] = (grad_after[...] + norm_back(grad_normed, gain, normed, scale)).astype(bf16)
    move.send(grad_in, grad_in_h)
    grad_gain[...] = jnp.sum(grad_normed * normed, axis=0, keepdims=True)
    move.send(grad_gain, grad_gain_h)
    move.finish()


def attention_weights_grad(
    normed_h, blocks_h, mixed_h, grads_h,
    result_h,
    normed, blocks, mixed, grads, packed, whole, branch, output_grad, sems,
):
    _, seq = place()
    move = Mover(sems)
    copies = move.fetch_all(mixed_h, mixed)
    copies += move.fetch_all(grads_h, grads)
    copies_qkv = move.fetch_all(blocks_h, blocks) + [move.fetch(normed_h, normed)]
    wait(copies)
    for offset, grad in enumerate(grads):
        branch[block_rows(seq ^ offset), :] = grad[:, SHARE:]
    for offset, block in enumerate(mixed):
        output_grad[block_rows(seq ^ offset, SHARE), :] = tn(unpack(block[...], SLOTS), branch[...])
    wait(copies_qkv)
    for offset, block in enumerate(blocks):
        whole[block_rows(seq ^ offset), :] = block[...]
    result = tn(normed[...], whole[...])
    last = jnp.concatenate([result[:, 2 * SHARE :], output_grad[...]], axis=1)
    rows = DIM // packed.shape[0]
    for group in range(packed.shape[0]):
        span = slice(group * rows, (group + 1) * rows)
        for tile in range(6):
            source = columns_of((result, last)[tile // 3], tile % 3, span)
            packed[group, tile * rows : (tile + 1) * rows, :] = source.astype(bf16)
    move.send(packed, result_h)
    move.finish()


def ffn_weights_grad(
    layer, left_h, y_h, ffn_h,
    result_h,
    packed, w_g, w_u, w_d, normed_two, hidden, grad_out, grad_gate, grad_up, down, sems,
):
    core, seq = place()
    move = Mover(sems, core)
    (g_own, g_other), (u_own, u_other), (d_own, d_other) = ffn_h
    span = pl.ds(pl.multiple_of(seq * FF_SHARE, FF_SHARE), FF_SHARE)
    if layer == 0:
        copies = move.fetch_all(left_h, (normed_two, hidden))
        copies += [move.fetch(block, grad_out.at[block_rows(seq ^ offset), :]) for offset, block in enumerate(y_h)]
    else:
        copies = [move.fetch(block, normed_two.at[block_rows(seq ^ offset), :]) for offset, block in enumerate(left_h)]
        copies += [
            move.fetch(y_h.at[part, core], grad_out.at[part * ROWS : (part + 1) * ROWS, :]) for part in range(PARTS)
        ]
    copies += [
        move.fetch_layer(layer, g_own.at[0, :, span], g_other.at[0, :, span], w_g.at[PARTS]),
        move.fetch_layer(layer, u_own.at[0, :, span], u_other.at[0, :, span], w_u.at[PARTS]),
        move.fetch_layer(layer, d_own.at[0, span, :], d_other.at[0, span, :], w_d),
    ]
    copies_ffn = []
    if layer == 1:
        for part in range(PARTS):
            part_span = slice(part * FF_SHARE, (part + 1) * FF_SHARE)
            copies_ffn.append(
                (
                    move.fetch_layer(layer, g_own.at[0, :, part_span], g_other.at[0, :, part_span], w_g.at[part]),
                    move.fetch_layer(layer, u_own.at[0, :, part_span], u_other.at[0, :, part_span], w_u.at[part]),
                )
            )
    wait(copies)
    for first, count in HALVES:
        rows = slice(first, first + count)
        block = normed_two[rows, :]
        grad_gate[rows, :], grad_up[rows, :] = ffn_back_chunk(
            nn(block, w_g[PARTS]), nn(block, w_u[PARTS]), nt(grad_out[rows, :], w_d[...])
        )
    groups = packed.shape[0]
    tile_rows = DIM // groups
    for index, grads in enumerate((grad_gate, grad_up)):
        result = tn(normed_two[...], grads[...])
        for group in range(groups):
            span = slice(group * tile_rows, (group + 1) * tile_rows)
            for tile in range(4):
                packed[group, index, tile * tile_rows : (tile + 1) * tile_rows, :] = columns_of(result, tile, span).astype(bf16)

    window = grad_out[:, pl.ds(window_start(seq), WINDOW)].astype(f32)
    columns = jnp.where(seq % 2 == 1, pltpu.roll(window, WINDOW - HEAD_DIM, 1), window)
    columns = columns[:, :SHARE].astype(bf16)
    for part in range(PARTS):
        part_span = slice(part * FF_SHARE, (part + 1) * FF_SHARE)
        if layer == 1:
            wait(copies_ffn[part])
            for first, count in HALVES:
                rows = slice(first, first + count)
                gate = nn(normed_two[rows, :], w_g[part])
                up = nn(normed_two[rows, :], w_u[part])
                hidden[rows, part_span] = (gate * jax.nn.sigmoid(gate) * up).astype(bf16)
        down[part_span, :] = tn(hidden[:, part_span], columns)
    quarter = FF // groups // 4
    for index in range(2):
        for group in range(groups):
            begin = (group * 4 + index * 2) * quarter
            both = jnp.concatenate(
                [down[begin : begin + quarter, :], down[begin + quarter : begin + 2 * quarter, :]], axis=1
            ).astype(bf16)
            for tile in range(3):
                place_at = 4 * tile_rows + tile * quarter
                packed[group, index, place_at : place_at + quarter, :] = columns_of(both, tile)
    move.send(packed, result_h)
    move.finish()


def join_attention(parts_h, gains_h, result_h, gains, result, sems):
    move = Mover(sems)
    rows = result.shape[2] - GAIN_ROWS
    copies = [move.fetch(part, result.at[:, layer, :rows, :]) for layer, part in enumerate(parts_h)]
    move.fetch(gains_h, gains).wait()
    result[:, :, rows:, :] = gains[...].astype(bf16)
    wait(copies)
    move.send(result, result_h)
    move.finish()


def write_weights(
    ffn_0, ffn_1, attn_h, ffn_other_0, ffn_other_1,
    q_h, k_h, v_h, o_h, g_h, u_h, d_h, gain_h,
    ffn_low, ffn_high, attn, q, k, v, o, g, u, d, gain, sems,
):
    core, _ = place()
    move = Mover(sems, core)
    copies = [
        move.fetch_layer(0, ffn_0, ffn_other_1, ffn_low),
        move.fetch_layer(0, ffn_other_0, ffn_1, ffn_high),
        move.fetch(attn_h, attn),
    ]
    wait(copies)
    rows = q.shape[1]
    quarter = d.shape[2] // 4
    for index, (ffn, wide_out, pair) in enumerate(((ffn_low, g, (q, k)), (ffn_high, u, (v, o)))):
        for tile in range(4):
            wide_out[0, :, tile * 128 : (tile + 1) * 128] = ffn[tile * rows : (tile + 1) * rows, :].astype(f32)
        place_at = 4 * rows
        both = jnp.concatenate(
            [ffn[place_at + tile * quarter : place_at + (tile + 1) * quarter, :].astype(f32) for tile in range(3)],
            axis=1,
        )
        begin = index * 2 * quarter
        turned = jnp.transpose(both)
        d[0, :, begin : begin + quarter] = turned[:SHARE]
        d[0, :, begin + quarter : begin + 2 * quarter] = turned[SHARE:]
        both = jnp.concatenate(
            [
                attn[(index * 3 + tile) * rows : (index * 3 + tile + 1) * rows, :].astype(f32)
                for tile in range(3)
            ],
            axis=1,
        )
        pair[0][0] = both[:, :SHARE]
        pair[1][0] = both[:, SHARE:]
    for source, target in zip((q, k, v, o, g, u, d), (q_h, k_h, v_h, o_h, g_h, u_h, d_h)):
        move.send(source, target)
    gain[...] = attn[6 * rows :, :].astype(f32)
    move.send(gain, gain_h)
    move.finish()


def shape(*dims, dtype=bf16):
    return jax.ShapeDtypeStruct(dims, dtype)


def vm(*dims, dtype=bf16):
    return pltpu.VMEM(dims, dtype)


def call(body, args, outs, scratch, micros, name, after=()):
    leaves, tree = jax.tree.flatten(args)
    out_leaves, out_tree = jax.tree.flatten(outs)
    scratch_leaves, scratch_tree = jax.tree.flatten(scratch)
    count_in, count_all = len(leaves), len(leaves) + len(after)

    def kernel(*refs):
        ins = jax.tree.unflatten(tree, refs[:count_in])
        results = jax.tree.unflatten(out_tree, refs[count_all : count_all + len(out_leaves)])
        temps = jax.tree.unflatten(scratch_tree, refs[count_all + len(out_leaves) :])
        body(*ins, *results, *temps)

    def spec(leaf):
        small = leaf.dtype == jnp.int32
        return pl.BlockSpec(memory_space=pltpu.SMEM if small else pltpu.HBM)

    results = pl.pallas_call(
        kernel,
        out_shape=out_leaves,
        in_specs=[spec(leaf) for leaf in leaves] + [pl.BlockSpec(memory_space=pltpu.HBM)] * len(after),
        out_specs=[pl.BlockSpec(memory_space=pltpu.HBM)] * len(out_leaves),
        scratch_shapes=scratch_leaves,
        compiler_params=pltpu.CompilerParams(vmem_limit_bytes=VMEM_MIB * MIB),
        cost_estimate=pl.CostEstimate(flops=micros * COST, bytes_accessed=10**4, transcendentals=0),
        name=name,
    )(*leaves, *after)
    return jax.tree.unflatten(out_tree, results)


def sems(count):
    return pltpu.SemaphoreType.DMA((count,))


GAINS = vm(GAIN_ROWS, WINDOW)
TABLES = [vm(SLOTS, 128, dtype=f32)] * 2
HEADS = (3, SHARE_HEADS, SLOTS, HEAD_DIM)
WEIGHTS = [vm(DIM, DIM), vm(PARTS, DIM, FF_SHARE), vm(PARTS, DIM, FF_SHARE), vm(FF, DIM)]
ATTEND = [
    vm(SHARE_HEADS, HEAD_DIM, SLOTS),
    vm(SHARE_HEADS, HEAD_DIM, SLOTS, dtype=f32),
    vm(SLOTS, 128),
    vm(SLOTS, 128),
]
WINDOWS = [vm(DIM, WINDOW)] * 3
ROW = (ROWS, DIM)
BRANCH = (ROWS, 2 * SHARE)
QKV = (ROWS, 3 * SHARE)


def call_pack_windows(weights, gains):
    rows = 3 * DIM + GAIN_ROWS
    return call(
        pack_windows,
        (weights, gains),
        [shape(rows, WINDOW)],
        [vm(rows, WINDOW), [vm(1, DIM)] * 2, sems(8)],
        3,
        "pack_windows",
    )[0]


def call_first_attention(*args):
    return call(
        first_attention,
        args,
        [shape(SLOTS, DIM), shape(*HEADS), shape(PACKED, 128)],
        [[vm(*ROW)] * 4, GAINS, *TABLES, WINDOWS, vm(SLOTS, DIM), vm(*HEADS), vm(PACKED, 128), *ATTEND, sems(16)],
        10,
        "first_attention",
    )


def call_middle(*args):
    return call(
        middle,
        args,
        [
            shape(*ROW, dtype=f32), shape(SLOTS, DIM), shape(SLOTS, FF), shape(*ROW), shape(SLOTS, DIM),
            shape(*HEADS), shape(PACKED, 128), [shape(PACKED_ROWS, 128)] * 4,
        ],
        [
            [vm(*ROW)] * 4, [vm(PACKED, 128)] * 4, GAINS, GAINS, *TABLES, *WEIGHTS, WINDOWS,
            vm(SLOTS, DIM, dtype=f32), vm(SLOTS, DIM), vm(SLOTS, FF), vm(SLOTS, DIM), vm(SLOTS, DIM),
            vm(*HEADS), vm(PACKED, 128), [vm(PACKED_ROWS, 128)] * 4, vm(SLOTS, DIM, dtype=f32), *ATTEND, sems(48),
        ],
        20,
        "middle",
    )


def call_last_rows(*args, after=()):
    return call(
        last_rows,
        args,
        [shape(*ROW), shape(*ROW), shape(*ROW, dtype=f32), shape(1, DIM, dtype=f32), [shape(*BRANCH)] * 4],
        [
            vm(*ROW), vm(*ROW), [vm(PACKED_ROWS, 128)] * 4, GAINS, *WEIGHTS,
            vm(*ROW), vm(*ROW), vm(*ROW, dtype=f32), vm(1, DIM, dtype=f32), [vm(*BRANCH)] * 4,
            vm(*ROW), vm(ROWS, FF), sems(32),
        ],
        11,
        "last_rows",
        after,
    )


def call_first_rows_back(*args, after=()):
    return call(
        first_rows_back,
        args,
        [shape(*ROW, dtype=f32), shape(1, DIM, dtype=f32), [shape(*BRANCH)] * 4],
        [
            vm(*ROW, dtype=f32), vm(*ROW), GAINS, *WEIGHTS,
            vm(*ROW, dtype=f32), vm(1, DIM, dtype=f32), [vm(*BRANCH)] * 4, vm(*ROW), sems(32),
        ],
        10,
        "first_rows_back",
        after,
    )


def call_attention_back(*args, after=()):
    return call(
        attention_back,
        args,
        [[shape(*QKV)] * 4],
        [
            [vm(*BRANCH)] * 4, *TABLES, vm(*HEADS), vm(SHARE_HEADS, SLOTS, HEAD_DIM), vm(HEAD_DIM, SLOTS),
            vm(SHARE_HEADS, HEAD_DIM, SLOTS, dtype=f32), vm(SHARE_HEADS, SLOTS, HEAD_DIM, dtype=f32),
            vm(SHARE_HEADS, SLOTS, HEAD_DIM, dtype=f32), vm(SLOTS, 3 * SHARE), sems(12),
        ],
        11,
        "attention_back",
        after,
    )[0]


def call_input_back(layer, *args, after=()):
    return call(
        functools.partial(input_back, layer),
        args,
        [shape(*ROW), shape(1, DIM, dtype=f32)],
        [
            [vm(*QKV)] * 4, vm(*ROW), vm(*ROW, dtype=f32), GAINS, [vm(DIM, DIM)] * 3,
            vm(*ROW), vm(1, DIM, dtype=f32), vm(3, *ROW), sems(16),
        ],
        10,
        "input_back",
        after,
    )


def call_attention_weights_grad(groups, *args, after=()):
    out = (groups, 6 * DIM // groups, 128)
    return call(
        attention_weights_grad,
        args,
        [shape(*out)],
        [
            vm(SLOTS, DIM), [vm(*QKV)] * 4, [vm(PACKED, 128)] * 4, [vm(*BRANCH)] * 4, vm(*out),
            vm(SLOTS, 3 * SHARE), vm(SLOTS, SHARE), vm(DIM, SHARE, dtype=f32), sems(16),
        ],
        8,
        "attention_weights_grad",
        after,
    )[0]


def call_ffn_weights_grad(layer, groups, *args, after=()):
    out = (groups, 2, (4 * DIM + 3 * FF // 4) // groups, 128)
    return call(
        functools.partial(ffn_weights_grad, layer),
        args,
        [shape(*out)],
        [
            vm(*out), vm(PARTS + 1, DIM, FF_SHARE), vm(PARTS + 1, DIM, FF_SHARE), vm(FF_SHARE, DIM),
            vm(SLOTS, DIM), vm(SLOTS, FF), vm(SLOTS, DIM), vm(SLOTS, FF_SHARE), vm(SLOTS, FF_SHARE),
            vm(FF, SHARE, dtype=f32), sems(48),
        ],
        15,
        "ffn_weights_grad",
        after,
    )[0]


def call_join_attention(parts, gains):
    groups, rows, _ = parts[0].shape
    out = (groups, len(parts), rows + GAIN_ROWS, 128)
    return call(
        join_attention,
        (parts, gains),
        [shape(*out)],
        [vm(*gains.shape, dtype=f32), vm(*out), sems(8)],
        3,
        "join_attention",
    )[0]


def call_write_weights(groups, *args):
    rows = DIM // groups
    dims = [(1, rows, SHARE)] * 4 + [(1, rows, FF_SHARE)] * 2 + [(1, SHARE, FF // groups), (GAIN_ROWS, 128)]
    ffn, _, attn = args[:3]
    return call(
        write_weights,
        args,
        [shape(*dim, dtype=f32) for dim in dims],
        [vm(*ffn.shape), vm(*ffn.shape), vm(*attn.shape)] + [vm(*dim, dtype=f32) for dim in dims] + [sems(16)],
        3,
        "write_weights",
    )


def rotary_tables():
    lanes = np.arange(128)
    frequency = (10000.0 ** (-2.0 * (lanes % 32) / HEAD_DIM)).astype(np.float32)
    angles = np.arange(SLOTS, dtype=np.float32)[:, None] * frequency[None, :]
    sign = np.where(lanes % HEAD_DIM < 32, -1.0, 1.0).astype(np.float32)
    return np.cos(angles).astype(np.float32), (np.sin(angles) * sign).astype(np.float32)


def swap(value):
    return lax.ppermute(value, "section", [(0, 1), (1, 0)])


def to_partner(value, offset):
    return lax.ppermute(value, "seq", [(part, part ^ offset) for part in range(PARTS)])


def gathered(value):
    return [value] + [to_partner(value, offset) for offset in range(1, PARTS)]


def exchanged(blocks):
    return [blocks[0]] + [to_partner(blocks[offset], offset) for offset in range(1, PARTS)]


def later(values, *earlier):
    return lax.optimization_barrier((values, earlier))[0]


def sum_over_items(parts):
    parts = parts.reshape(-1, *parts.shape[2:])
    return lax.psum_scatter(parts, ("dp", "section"), scatter_dimension=0)


def give(value, giver):
    return lax.ppermute(value, "section", [(giver, 1 - giver)])


def on_device(
    section_input, out_cotangent, lengths, attn_gain, w_query, w_key, w_value, w_output,
    ffn_gain, w_gate, w_up, w_down,
):
    groups = lax.axis_size("dp")
    core = lax.axis_index("section")
    is_first = core == 0
    inputs = lax.dynamic_index_in_dim(section_input, core, 0, keepdims=False)
    cos, sin = (jnp.asarray(table) for table in rotary_tables())
    x_blocks = gathered(inputs)
    windows = call_pack_windows((w_query, w_key, w_value), (attn_gain, ffn_gain))
    windows = (windows, swap(windows))
    o_pair, g_pair, u_pair, d_pair = (
        (weight, swap(later(weight, *earlier)))
        for weight, *earlier in (
            (w_output, windows[1]),
            (w_gate, windows[1]),
            (w_up, windows[1], x_blocks),
            (w_down, windows[1], x_blocks),
        )
    )
    ffn = (g_pair, u_pair, d_pair)

    normed_0, heads_0, packed_0 = call_first_attention(x_blocks, lengths, cos, sin, windows)
    mixed_0 = gathered(later(packed_0, o_pair[1], g_pair[1]))
    after_0, normed_two_0, hidden_0, mid, normed_1, heads_1, packed_1, mixed_blocks = call_middle(
        x_blocks, mixed_0, lengths, cos, sin, o_pair, ffn, windows
    )
    cotangent_all = lax.all_gather(later(out_cotangent, mixed_0), "seq", axis=0)
    qkv = tuple((weight, swap(later(weight, mixed_0))) for weight in (w_query, w_key, w_value))
    mixed_rows = exchanged(mixed_blocks)
    mixed_1 = gathered(later(packed_1, mixed_rows[1]))
    output, normed_two_1, grad_after_1, gain_ffn_1, grad_blocks_1 = call_last_rows(
        mid, out_cotangent, mixed_rows, windows, o_pair, ffn, after=[pair[1] for pair in qkv]
    )
    grad_mixed_1 = exchanged(grad_blocks_1)
    normed_two_all = gathered(later(normed_two_1, grad_mixed_1[1], mixed_1))
    grad_qkv_1 = call_attention_back(grad_mixed_1, lengths, cos, sin, heads_1)
    grad_rows_1 = exchanged(grad_qkv_1)
    parts_f1 = call_ffn_weights_grad(1, groups, normed_two_all, cotangent_all, ffn, after=(grad_qkv_1[0],))
    grad_rows_1, parts_f1 = lax.optimization_barrier((grad_rows_1, parts_f1))
    sum_f1 = sum_over_items(parts_f1)
    grad_mid, gain_attn_1 = call_input_back(1, grad_rows_1, mid, grad_after_1, windows, qkv)
    grad_mid_all = gathered(grad_mid)
    grad_after_0, gain_ffn_0, grad_blocks_0 = call_first_rows_back(after_0, grad_mid, windows, o_pair, ffn)
    grad_mixed_0 = exchanged(grad_blocks_0)
    parts_f0 = call_ffn_weights_grad(
        0, groups, (normed_two_0, hidden_0), grad_mid_all, ffn, after=(grad_after_0,)
    )
    grad_mixed_0, parts_f0 = lax.optimization_barrier((grad_mixed_0, parts_f0))
    sum_f0 = sum_over_items(parts_f0)
    grad_qkv_0 = call_attention_back(grad_mixed_0, lengths, cos, sin, heads_0)
    grad_rows_0 = exchanged(grad_qkv_0)
    parts_a1 = call_attention_weights_grad(
        groups, normed_1, grad_qkv_1, mixed_1, grad_mixed_1, after=(grad_qkv_0[0],)
    )
    parts_a0 = call_attention_weights_grad(
        groups, normed_0, grad_qkv_0, mixed_0, grad_mixed_0, after=(parts_a1,)
    )
    grad_first, gain_attn_0 = call_input_back(
        0, grad_rows_0, inputs, grad_after_0, windows, qkv, after=(parts_a0,)
    )

    share = DIM // (groups * PARTS)
    gain_grads = jnp.concatenate([gain_attn_0, gain_ffn_0, gain_attn_1, gain_ffn_1], axis=0)
    gain_grads = gain_grads.reshape(2, 2, groups, PARTS, share).transpose(3, 2, 0, 1, 4)
    seq = lax.axis_index("seq")
    gain_parts = exchanged(
        [lax.dynamic_index_in_dim(gain_grads, seq ^ offset, 0, keepdims=False) for offset in range(PARTS)]
    )
    gain_rows = jnp.pad(sum(gain_parts), ((0, 0), (0, 0), (0, GAIN_ROWS - 2), (0, 128 - share)))
    sum_attn = sum_over_items(call_join_attention((parts_a0, parts_a1), gain_rows))

    def sort(of_first, of_second):
        mine = jnp.where(is_first, of_first, of_second)
        other = swap(jnp.where(is_first, of_second, of_first))
        return jnp.where(is_first, mine, other), jnp.where(is_first, other, mine)

    section_outputs = jnp.stack(sort(mid, output))[None]
    input_grads = jnp.stack(sort(grad_first, grad_mid))[None]
    g_query, g_key, g_value, g_output, g_gate, g_up, g_down, gain_sums = call_write_weights(
        groups, sum_f0, sum_f1, sum_attn, give(sum_f0, 1), give(sum_f1, 0)
    )
    gain_sums = gain_sums[:2, :share]
    return (
        section_outputs, input_grads, gain_sums[0:1], g_query, g_key, g_value, g_output, gain_sums[1:2],
        g_gate, g_up, g_down.transpose(0, 2, 1),
    )


def solution(mesh):
    return jax.shard_map(
        on_device,
        mesh=mesh,
        in_specs=(
            P("dp", "seq", None),
            P("dp", "seq", None),
            P("dp"),
            P("section", None),
            P("section", None, None),
            P("section", None, None),
            P("section", None, None),
            P("section", None, None),
            P("section", None),
            P("section", None, None),
            P("section", None, None),
            P("section", None, None),
        ),
        out_specs=(
            P("section", "dp", "seq", None),
            P("section", "dp", "seq", None),
            P("section", ("dp", "seq")),
            P("section", "dp", "seq"),
            P("section", "dp", "seq"),
            P("section", "dp", "seq"),
            P("section", "dp", "seq"),
            P("section", ("dp", "seq")),
            P("section", "dp", "seq"),
            P("section", "dp", "seq"),
            P("section", "dp", "seq"),
        ),
        check_vma=False,
    )
```

time: 504 us -> 265 us (0.53)
  waiting for transfers between devices: 268 us -> 73 us
  local copies, waits for them, and re-layouts: 50.2 us -> 9.87 us
  Pallas kernels: 98.8 us -> 114 us
  other arithmetic: 16.5 us -> 2.52 us
    reduce_scatter x6 -> x3, waiting for transfers between devices: 129 us -> 32.7 us  [sum_over_items(): return lax.psum_scatter(parts, ('dp', 'section'), scatter_dimension=0)]
    unnamed x8 -> x4, waiting for transfers between devices: 78.4 us -> 0.07 us
    unnamed x256 -> x95, local copies, waits for them, and re-layouts: 46.3 us -> 7.81 us
    pallas_call x12 -> x15, Pallas kernels: 98.8 us -> 114 us  [call(): pl.pallas_call(kernel, out_shape=out_leaves, in_specs=[spec(leaf) for lea...]
    ppermute x33, waiting for transfers between devices: 50.5 us -> 35.9 us  [to_partner(): lax.ppermute(value, 'seq', [(part, part ^ offset) for part in range(PARTS)])]
    convert_element_type x10 -> x0, other arithmetic: 11.7 us -> none  [the longest x6 9.11 us: scatter_sum(): total = (keep.astype(f32) + received.astype(f32)).astype(bf16)]
    ppermute x20 -> x10, waiting for transfers between devices: 9.92 us -> 4.35 us  [swap(): return lax.ppermute(value, 'section', [(0, 1), (1, 0)])]
  transfers between devices with their start and end apart: 60 -> 49, of which waited for: 33 -> 16; matrix products, arithmetic and copies ran while one was open for 4% -> 1% of each run, Pallas kernels for 12% -> 42%
where the time goes in v2:
time: 265 us; the launch traced here: 260 us
  Pallas kernels  114 us (43%)
  waiting for transfers between devices  73 us (28%)
  starting transfers between devices  46 us (17%)
  between operations  14.7 us (6%)
  local copies, waits for them, and re-layouts  9.87 us (4%)
    pallas_call x15, Pallas kernels, call(): pl.pallas_call(kernel, out_shape=out_leaves, in_specs=[spec(leaf) for lea...  114 us
    ppermute x33, starting transfers between devices, to_partner(): lax.ppermute(value, 'seq', [(part, part ^ offset) for part in range(PARTS)])  39.5 us
    ppermute x33, waiting for transfers between devices, to_partner(): lax.ppermute(value, 'seq', [(part, part ^ offset) for part in range(PARTS)])  35.9 us
    reduce_scatter x3, waiting for transfers between devices, sum_over_items(): return lax.psum_scatter(parts, ('dp', 'section'), scatter_dimension=0)  32.7 us
    unnamed x95, local copies, waits for them, and re-layouts  7.81 us
  transfers between devices with their start and end apart: 49, of which 16 were waited for; matrix products, arithmetic and copies ran while one was open for 1% of the time, Pallas kernels for 42%

profile of v2, /device:TPU:0, one launch (start us, length us, event | category | flops | bytes accessed | tf_op | source)
XLA Modules:
  0.0 259.9 jit_solution(623328096890381934)
XLA Ops:
  7.3 2.5 pack_windows.1.refs_7_.refs_19_.refs_6_.refs_2_
  10.3 2.7 %collective-permute-done.3.refs_8_.refs_20_.refs_7_.refs_3_ = bf16[2320,256]{1,0:T(8,128)(2,1)S(1)} collective-permute-done((bf16[2320,256]{1,0:T(8,128)(2,1)}, bf16[2320,256]{1,0:T(8,128)(2,1)S(1)}, u32[]{:S(2)}, u32[]{:S(2)}) %collective-permute-start.3) | collective-permute-done | bytes 1187872 | tf_op jit(solution)/shard_map/ppermute | solution.py:931
  13.4 2.7 %collective-permute-start = (bf16[160,768]{1,0:T(8,128)(2,1)S(1)}, bf16[160,768]{1,0:T(8,128)(2,1)S(1)}, u32[]{:S(2)}, u32[]{:S(2)}) collective-permute-start(bf16[160,768]{1,0:T(8,128)(2,1)S(1)} %dynamic-slice_bitcast_fusion.refs_0_.refs_4_), channel_id=1, source_target_pairs={{0,1},{1,0},{2,3},{3,2},{4,5},{5,4},{6,7},{7,6},{8,9},{9,8},{10,11... | collective-permute-start | bytes 737288 | tf_op jit(solution)/shard_map/ppermute | solution.py:935
  17.6 5.2 %collective-permute-done.refs_1_ = bf16[160,768]{1,0:T(8,128)(2,1)S(1)} collective-permute-done((bf16[160,768]{1,0:T(8,128)(2,1)S(1)}, bf16[160,768]{1,0:T(8,128)(2,1)S(1)}, u32[]{:S(2)}, u32[]{:S(2)}) %collective-permute-start) | collective-permute-done | bytes 245792 | tf_op jit(solution)/shard_map/ppermute | solution.py:935
  22.9 6.4 %collective-permute-done.1.refs_2_ = bf16[160,768]{1,0:T(8,128)(2,1)S(1)} collective-permute-done((bf16[160,768]{1,0:T(8,128)(2,1)S(1)}, bf16[160,768]{1,0:T(8,128)(2,1)S(1)}, u32[]{:S(2)}, u32[]{:S(2)}) %collective-permute-start.1) | collective-permute-done | bytes 245792 | tf_op jit(solution)/shard_map/ppermute | solution.py:935
  30.1 7.7 %first_attention.1 = (bf16[640,768]{1,0:T(8,128)(2,1)}, bf16[3,3,640,64]{3,2,1,0:T(8,128)(2,1)}, bf16[960,128]{1,0:T(8,128)(2,1)}) custom-call(bf16[160,768]{1,0:T(8,128)(2,1)} %copy-done.6, bf16[160,768]{1,0:T(8,128)(2,1)} %copy-done.22, bf16[160,768]{1,0:T(8,128)(2,1)} %copy-done.23, bf16[160,768]{1,0:T(8,128)(2,1)} %copy-done.24, s32[2]{0:T(128)} %refs_4_.9, ...), custom_call_target="tpu_custom_call" | custom-call | flops 10000000000 | bytes 10000 | tf_op jit(solution)/shard_map/first_attention/pallas_call | solution.py:726
  42.0 5.5 %collective-permute-done.6.refs_5_.refs_6_ = bf16[960,128]{1,0:T(8,128)(2,1)S(1)} collective-permute-done((bf16[960,128]{1,0:T(8,128)(2,1)}, bf16[960,128]{1,0:T(8,128)(2,1)S(1)}, u32[]{:S(2)}, u32[]{:S(2)}) %collective-permute-start.6) | collective-permute-done | bytes 245792 | tf_op jit(solution)/shard_map/ppermute | solution.py:935
  47.5 3.9 %collective-permute-done.7.refs_6_.refs_7_ = bf16[960,128]{1,0:T(8,128)(2,1)S(1)} collective-permute-done((bf16[960,128]{1,0:T(8,128)(2,1)}, bf16[960,128]{1,0:T(8,128)(2,1)S(1)}, u32[]{:S(2)}, u32[]{:S(2)}) %collective-permute-start.7) | collective-permute-done | bytes 245792 | tf_op jit(solution)/shard_map/ppermute | solution.py:935
  53.9 17.5 %middle.1 = (f32[160,768]{1,0:T(8,128)}, bf16[640,768]{1,0:T(8,128)(2,1)}, bf16[640,2048]{1,0:T(8,128)(2,1)}, bf16[160,768]{1,0:T(8,128)(2,1)}, bf16[640,768]{1,...) custom-call(bf16[160,768]{1,0:T(8,128)(2,1)} %copy-done.6, ...), custom_call_target="tpu_custom_call" | custom-call | flops 20000000000 | bytes 10000 | tf_op jit(solution)/shard_map/middle/pallas_call | solution.py:726
  78.4 5.0 %collective-permute-done.13.refs_5_ = bf16[240,128]{1,0:T(8,128)(2,1)S(1)} collective-permute-done((bf16[240,128]{1,0:T(8,128)(2,1)}, bf16[240,128]{1,0:T(8,128)(2,1)S(1)}, u32[]{:S(2)}, u32[]{:S(2)}) %collective-permute-start.13) | collective-permute-done | bytes 61472 | tf_op jit(solution)/shard_map/ppermute | solution.py:935
  86.6 10.3 %last_rows.1 = (bf16[160,768]{1,0:T(8,128)(2,1)}, bf16[160,768]{1,0:T(8,128)(2,1)}, f32[160,768]{1,0:T(8,128)}, f32[1,768]{1,0:T(1,128)}, bf16[160,384]{1,0:T(8,...) custom-call(bf16[160,768]{1,0:T(8,128)(2,1)} %get-tuple-element.86.refs_0_.refs_4_, ...), custom_call_target="tpu_custom_call" | custom-call | flops 11000000512 | bytes 10000 | tf_op jit(solution)/shard_map/last_rows/pallas_call | solution.py:726
  100.9 2.5 collective-permute-done.18.refs_1_.refs_10_
  107.6 9.5 %attention_back.2 = (bf16[160,576]{1,0:T(8,128)(2,1)}, bf16[160,576]{1,0:T(8,128)(2,1)}, bf16[160,576]{1,0:T(8,128)(2,1)}, bf16[160,576]{1,0:T(8,128)(2,1)}) custom-call(bf16[160,384]{1,0:T(8,128)(2,1)} %get-tuple-element.96.refs_0_.refs_9_, bf16[160,384]{1,0:T(8,128)(2,1)} %copy-done.37, bf16[160,384]{1,0:T(8,128)(2,1)} %copy-done.38, ...), custom_call_target="tpu_custom_call" | custom-call | flops 11000000512 | bytes 10000 | tf_op jit(solution)/shard_map/attention_back/pallas_call | solution.py:726
  121.5 14.4 %ffn_weights_grad.2 = bf16[4,2,1152,128]{3,2,1,0:T(8,128)(2,1)} custom-call(bf16[160,768]{1,0:T(8,128)(2,1)} %get-tuple-element.108.refs_0_, bf16[160,768]{1,0:T(8,128)(2,1)} %copy-done.25, bf16[160,768]{1,0:T(8,128)(2,1)} %copy-done.26, bf16[160,768]{1,0:T(8,128)(2,1)} %copy-done.27, bf16[4,2,160,768]{3,2,1,0:T(8,128)(2,1)} %bitcast.53, ...), custom_call_target="tpu_custom_call" | custom-call | flops 15000000512 | bytes 10000 | tf_op jit(solution)/shard_map/ffn_weights_grad/pallas_call | solution.py:726
  136.7 4.6 %input_back.2 = (bf16[160,768]{1,0:T(8,128)(2,1)}, f32[1,768]{1,0:T(1,128)}) custom-call(bf16[160,576]{1,0:T(8,128)(2,1)} %get-tuple-element.110.refs_11_.refs_0_.refs_1_, bf16[160,576]{1,0:T(8,128)(2,1)} %copy-done.34, bf16[160,576]{1,0:T(8,128)(2,1)} %copy-done.35, bf16[160,576]{1,0:T(8,128)(2,1)} %copy-done.36, ...), custom_call_target="tpu_custom_call" | custom-call | flops 10000000000 | bytes 10000 | tf_op jit(solution)/shard_map/input_back/pallas_call | solution.py:726
  144.9 9.0 %first_rows_back.1 = (f32[160,768]{1,0:T(8,128)}, f32[1,768]{1,0:T(1,128)}, bf16[160,384]{1,0:T(8,128)(2,1)}, bf16[160,384]{1,0:T(8,128)(2,1)}, bf16[160,384]{1,0:T(8,128)(2,1)}, /*index=5*/bf16[160,384]{1,0:T(8,128)(2,1)}) custom-call(f32[160,768]{1,0:T(8,128)} %get-tuple-element.95.refs_0_, bf16[160,768]{1,0:T(8,128)(2,1)} %get-tuple-element.115.refs_1_.refs_2_, ...), custom_call_target="tpu_custom_call" | custom-call | flops 10000000000 | bytes 10000 | tf_op jit(solution)/shard_map/first_rows_back/pallas_call | solution.py:726
  158.3 9.0 %ffn_weights_grad.3 = bf16[4,2,1152,128]{3,2,1,0:T(8,128)(2,1)} custom-call(bf16[640,768]{1,0:T(8,128)(2,1)} %get-tuple-element.120.refs_0_, bf16[640,2048]{1,0:T(8,128)(2,1)} %get-tuple-element.121.refs_1_, bf16[160,768]{1,0:T(8,128)(2,1)} %get-tuple-element.115.refs_1_.refs_2_, bf16[160,768]{1,0:T(8,128)(2,1)} %copy-done.28, bf16[160,768]{1,0:T(8,128)(2,1)} %copy-done.29, ...), custom_call_target="tpu_custom_call" | custom-call | flops 15000000512 | bytes 10000 | tf_op jit(solution)/shard_map/ffn_weights_grad/pallas_call | solution.py:726
  168.0 9.5 %attention_back.3 = (bf16[160,576]{1,0:T(8,128)(2,1)}, bf16[160,576]{1,0:T(8,128)(2,1)}, bf16[160,576]{1,0:T(8,128)(2,1)}, bf16[160,576]{1,0:T(8,128)(2,1)}) custom-call(bf16[160,384]{1,0:T(8,128)(2,1)} %get-tuple-element.123.refs_0_.refs_9_, bf16[160,384]{1,0:T(8,128)(2,1)} %copy-done.40, bf16[160,384]{1,0:T(8,128)(2,1)} %copy-done.41, ...), custom_call_target="tpu_custom_call" | custom-call | flops 11000000512 | bytes 10000 | tf_op jit(solution)/shard_map/attention_back/pallas_call | solution.py:726
  181.1 4.6 %attention_weights_grad.2.refs_13_.refs_1_ = bf16[4,1152,128]{2,1,0:T(8,128)(2,1)} custom-call(bf16[640,768]{1,0:T(8,128)(2,1)} %get-tuple-element.133.refs_0_, bf16[160,576]{1,0:T(8,128)(2,1)} %get-tuple-element.110.refs_11_.refs_0_.refs_1_, bf16[160,576]{1,0:T(8,128)(2,1)} %get-tuple-element.102.refs_2_, bf16[160,576]{1,0:T(8,128)(2,1)} %get-tuple-element.103.refs_3_, ...), custom_call_target="tpu_custom_call" | custom-call | flops 8000000000 | bytes 10000 | tf_op jit(solution)/shard_map/attention_weights_grad/pallas_call | solution.py:726
  185.7 4.6 %attention_weights_grad.3.refs_14_.refs_0_ = bf16[4,1152,128]{2,1,0:T(8,128)(2,1)} custom-call(bf16[640,768]{1,0:T(8,128)(2,1)} %get-tuple-element.132.refs_0_, bf16[160,576]{1,0:T(8,128)(2,1)} %get-tuple-element.128.refs_13_.refs_1_.refs_0_, bf16[160,576]{1,0:T(8,128)(2,1)} %get-tuple-element.129.refs_2_, bf16[160,576]{1,0:T(8,128)(2,1)} %get-tuple-element.130.refs_3_, ...), custom_call_target="tpu_custom_call" | custom-call | flops 8000000000 | bytes 10000 | tf_op jit(solution)/shard_map/attention_weights_grad/pallas_call | solution.py:726
  191.8 4.6 %input_back.3 = (bf16[160,768]{1,0:T(8,128)(2,1)}, f32[1,768]{1,0:T(1,128)}) custom-call(bf16[160,576]{1,0:T(8,128)(2,1)} %get-tuple-element.128.refs_13_.refs_1_.refs_0_, bf16[160,576]{1,0:T(8,128)(2,1)} %copy-done.31, bf16[160,576]{1,0:T(8,128)(2,1)} %copy-done.32, bf16[160,576]{1,0:T(8,128)(2,1)} %copy-done.33, bf16[160,768]{1,0:T(8,128)(2,1)} %copy-done.6, ...), custom_call_target="tpu_custom_call" | custom-call | flops 10000000000 | bytes 10000 | tf_op jit(solution)/shard_map/input_back/pallas_call | solution.py:726
  204.7 3.1 %join_attention.1 = bf16[4,2,1168,128]{3,2,1,0:T(8,128)(2,1)} custom-call(bf16[4,1152,128]{2,1,0:T(8,128)(2,1)} %attention_weights_grad.3.refs_14_.refs_0_, bf16[4,1152,128]{2,1,0:T(8,128)(2,1)} %attention_weights_grad.2.refs_13_.refs_1_, f32[4,2,16,128]{3,2,1,0:T(8,128)} %pad.4.refs_2_), custom_call_target="tpu_custom_call" | custom-call | flops 3000000000 | bytes 10000 | tf_op jit(solution)/shard_map/join_attention/pallas_call | solution.py:726
  215.6 32.7 %reduce-scatter.8.cloned.1.call-done = bf16[1,1168,128]{2,1,0:T(8,128)(2,1)} async-done(((bf16[8,1168,128]{2,1,0:T(8,128)(2,1)}), bf16[1,1168,128]{2,1,0:T(8,128)(2,1)}) %reduce-scatter.8.cloned.1.call-update) | async-done | bytes 299024 | tf_op jit(solution)/shard_map/reduce_scatter | solution.py:952
  249.1 2.7 %write_weights.1 = (f32[1,192,192]{2,1,0:T(8,128)}, f32[1,192,192]{2,1,0:T(8,128)}, f32[1,192,192]{2,1,0:T(8,128)}, f32[1,192,192]{2,1,0:T(8,128)}, f32[1,192,51...) custom-call(bf16[1152,128]{1,0:T(8,128)(2,1)} %bitcast.58, ...), custom_call_target="tpu_custom_call" | custom-call | flops 3000000000 | bytes 10000 | tf_op jit(solution)/shard_map/write_weights/pallas_call | solution.py:726
  (201 shorter events, 64.8 us)
Async XLA Ops:
  7.2 113.5 %all-gather.3.cloned.1.call-start = ((), (), s32[]{:S(2)}) async-start(), calls=%async_computation.6 | async-start | bytes 2457600 | tf_op jit(solution)/shard_map/all_gather | solution.py:987
  13.0 25.6 %collective-permute-start.5 = (bf16[1,768,2048]{2,1,0:T(8,128)(2,1)}, bf16[1,768,2048]{2,1,0:T(8,128)(2,1)}, u32[]{:S(2)}, u32[]{:S(2)}) collective-permute-start(bf16[1,768,2048]{2,1,0:T(8,128)(2,1)} %refs_6_.6), channel_id=1, source_target_pairs={{0,16},{16,0},{1,17},{17,1},{2,18},{18,2},{3,19},{19,3},{4,20},{20... | collective-permute-start | bytes 9437192 | tf_op jit(solution)/shard_map/ppermute | solution.py:931
  29.3 24.6 %collective-permute-start.10 = (bf16[1,2048,768]{2,1,0:T(8,128)(2,1)}, bf16[1,2048,768]{2,1,0:T(8,128)(2,1)}, u32[]{:S(2)}, u32[]{:S(2)}) collective-permute-start(bf16[1,2048,768]{2,1,0:T(8,128)(2,1)} %refs_10_.9), channel_id=1, source_target_pairs={{0,16},{16,0},{1,17},{17,1},{2,18},{18,2},{3,19},{19,3},{4,20},{20... | collective-permute-start | bytes 9437192 | tf_op jit(solution)/shard_map/ppermute | solution.py:931
  29.4 24.5 %collective-permute-start.9 = (bf16[1,768,2048]{2,1,0:T(8,128)(2,1)}, bf16[1,768,2048]{2,1,0:T(8,128)(2,1)}, u32[]{:S(2)}, u32[]{:S(2)}) collective-permute-start(bf16[1,768,2048]{2,1,0:T(8,128)(2,1)} %refs_8_.10), channel_id=1, source_target_pairs={{0,16},{16,0},{1,17},{17,1},{2,18},{18,2},{3,19},{19,3},{4,20},{20... | collective-permute-start | bytes 9437192 | tf_op jit(solution)/shard_map/ppermute | solution.py:931
  53.0 158.4 %reduce-scatter.6.cloned.1.call-start = ((), (), s32[]{:S(2)}) async-start(), calls=%async_computation.4 | async-start | bytes 2654208 | tf_op jit(solution)/shard_map/reduce_scatter | solution.py:952
  53.2 30.9 %collective-permute-start.16 = (bf16[1,768,768]{2,1,0:T(8,128)(2,1)}, bf16[1,768,768]{2,1,0:T(8,128)(2,1)S(1)}, u32[]{:S(2)}, u32[]{:S(2)}) collective-permute-start(bf16[1,768,768]{2,1,0:T(8,128)(2,1)} %refs_12_.5), channel_id=1, source_target_pairs={{0,16},{16,0},{1,17},{17,1},{2,18},{18,2},{3,19},{19,3},{4,20},{20... | collective-permute-start | bytes 3538952 | tf_op jit(solution)/shard_map/ppermute | solution.py:931
  53.3 32.3 %collective-permute-start.15 = (bf16[1,768,768]{2,1,0:T(8,128)(2,1)}, bf16[1,768,768]{2,1,0:T(8,128)(2,1)S(1)}, u32[]{:S(2)}, u32[]{:S(2)}) collective-permute-start(bf16[1,768,768]{2,1,0:T(8,128)(2,1)} %refs_10_.10), channel_id=1, source_target_pairs={{0,16},{16,0},{1,17},{17,1},{2,18},{18,2},{3,19},{19,3},{4,20},{20... | collective-permute-start | bytes 3538952 | tf_op jit(solution)/shard_map/ppermute | solution.py:931
  53.8 31.8 %collective-permute-start.14 = (bf16[1,768,768]{2,1,0:T(8,128)(2,1)}, bf16[1,768,768]{2,1,0:T(8,128)(2,1)}, u32[]{:S(2)}, u32[]{:S(2)}) collective-permute-start(bf16[1,768,768]{2,1,0:T(8,128)(2,1)} %refs_8_.11), channel_id=1, source_target_pairs={{0,16},{16,0},{1,17},{17,1},{2,18},{18,2},{3,19},{19,3},{4,20},{20... | collective-permute-start | bytes 3538952 | tf_op jit(solution)/shard_map/ppermute | solution.py:931
  77.8 21.2 %collective-permute-start.24 = (bf16[960,128]{1,0:T(8,128)(2,1)}, bf16[960,128]{1,0:T(8,128)(2,1)S(1)}, u32[]{:S(2)}, u32[]{:S(2)}) collective-permute-start(bf16[960,128]{1,0:T(8,128)(2,1)} %get-tuple-element.107.refs_5_), channel_id=1, source_target_pairs={{0,1},{1,0},{2,3},{3,2},{4,5},{5,4},{6,7},{7,6},{8,9},{9,8},{10,11... | collective-permute-start | bytes 737288 | tf_op jit(solution)/shard_map/ppermute | solution.py:935
  83.3 17.1 %collective-permute-start.25 = (bf16[960,128]{1,0:T(8,128)(2,1)}, bf16[960,128]{1,0:T(8,128)(2,1)S(1)}, u32[]{:S(2)}, u32[]{:S(2)}) collective-permute-start(bf16[960,128]{1,0:T(8,128)(2,1)} %get-tuple-element.107.refs_5_), channel_id=1, source_target_pairs={{0,2},{1,3},{2,0},{3,1},{4,6},{5,7},{6,4},{7,5},{8,10},{9,11},{10,... | collective-permute-start | bytes 737288 | tf_op jit(solution)/shard_map/ppermute | solution.py:935
  84.2 16.7 %collective-permute-start.26 = (bf16[960,128]{1,0:T(8,128)(2,1)}, bf16[960,128]{1,0:T(8,128)(2,1)S(1)}, u32[]{:S(2)}, u32[]{:S(2)}) collective-permute-start(bf16[960,128]{1,0:T(8,128)(2,1)} %get-tuple-element.107.refs_5_), channel_id=1, source_target_pairs={{0,3},{1,2},{2,1},{3,0},{4,7},{5,6},{6,5},{7,4},{8,11},{9,10},{10,... | collective-permute-start | bytes 737288 | tf_op jit(solution)/shard_map/ppermute | solution.py:935
  103.4 15.8 %collective-permute-start.27 = (bf16[160,768]{1,0:T(8,128)(2,1)}, bf16[160,768]{1,0:T(8,128)(2,1)S(1)}, u32[]{:S(2)}, u32[]{:S(2)}) collective-permute-start(bf16[160,768]{1,0:T(8,128)(2,1)} %get-tuple-element.108.refs_0_), channel_id=1, source_target_pairs={{0,1},{1,0},{2,3},{3,2},{4,5},{5,4},{6,7},{7,6},{8,9},{9,8},{10,11... | collective-permute-start | bytes 737288 | tf_op jit(solution)/shard_map/ppermute | solution.py:935
  103.7 16.9 %collective-permute-start.28 = (bf16[160,768]{1,0:T(8,128)(2,1)}, bf16[160,768]{1,0:T(8,128)(2,1)S(1)}, u32[]{:S(2)}, u32[]{:S(2)}) collective-permute-start(bf16[160,768]{1,0:T(8,128)(2,1)} %get-tuple-element.108.refs_0_), channel_id=1, source_target_pairs={{0,2},{1,3},{2,0},{3,1},{4,6},{5,7},{6,4},{7,5},{8,10},{9,11},{10,... | collective-permute-start | bytes 737288 | tf_op jit(solution)/shard_map/ppermute | solution.py:935
  105.4 15.2 %collective-permute-start.29 = (bf16[160,768]{1,0:T(8,128)(2,1)}, bf16[160,768]{1,0:T(8,128)(2,1)S(1)}, u32[]{:S(2)}, u32[]{:S(2)}) collective-permute-start(bf16[160,768]{1,0:T(8,128)(2,1)} %get-tuple-element.108.refs_0_), channel_id=1, source_target_pairs={{0,3},{1,2},{2,1},{3,0},{4,7},{5,6},{6,5},{7,4},{8,11},{9,10},{10,... | collective-permute-start | bytes 737288 | tf_op jit(solution)/shard_map/ppermute | solution.py:935
  117.1 18.8 %collective-permute-start.21 = (bf16[160,576]{1,0:T(8,128)(2,1)}, bf16[160,576]{1,0:T(8,128)(2,1)S(1)}, u32[]{:S(2)}, u32[]{:S(2)}) collective-permute-start(bf16[160,576]{1,0:T(8,128)(2,1)} %get-tuple-element.102.refs_2_), channel_id=1, source_target_pairs={{0,1},{1,0},{2,3},{3,2},{4,5},{5,4},{6,7},{7,6},{8,9},{9,8},{10,11... | collective-permute-start | bytes 552968 | tf_op jit(solution)/shard_map/ppermute | solution.py:935
  118.0 17.9 %collective-permute-start.22 = (bf16[160,576]{1,0:T(8,128)(2,1)}, bf16[160,576]{1,0:T(8,128)(2,1)S(1)}, u32[]{:S(2)}, u32[]{:S(2)}) collective-permute-start(bf16[160,576]{1,0:T(8,128)(2,1)} %get-tuple-element.103.refs_3_), channel_id=1, source_target_pairs={{0,2},{1,3},{2,0},{3,1},{4,6},{5,7},{6,4},{7,5},{8,10},{9,11},{10,... | collective-permute-start | bytes 552968 | tf_op jit(solution)/shard_map/ppermute | solution.py:935
  119.2 16.8 %collective-permute-start.23 = (bf16[160,576]{1,0:T(8,128)(2,1)}, bf16[160,576]{1,0:T(8,128)(2,1)S(1)}, u32[]{:S(2)}, u32[]{:S(2)}) collective-permute-start(bf16[160,576]{1,0:T(8,128)(2,1)} %get-tuple-element.104.refs_4_), channel_id=1, source_target_pairs={{0,3},{1,2},{2,1},{3,0},{4,7},{5,6},{6,5},{7,4},{8,11},{9,10},{10,... | collective-permute-start | bytes 552968 | tf_op jit(solution)/shard_map/ppermute | solution.py:935
  136.0 77.4 %reduce-scatter.4.cloned.1.call-start = ((), (), s32[]{:S(2)}) async-start(), calls=%async_computation.3 | async-start | bytes 2654208 | tf_op jit(solution)/shard_map/reduce_scatter | solution.py:952
  141.3 14.7 %collective-permute-start.33 = (bf16[160,768]{1,0:T(8,128)(2,1)}, bf16[160,768]{1,0:T(8,128)(2,1)S(1)}, u32[]{:S(2)}, u32[]{:S(2)}) collective-permute-start(bf16[160,768]{1,0:T(8,128)(2,1)} %get-tuple-element.115.refs_1_.refs_2_), channel_id=1, source_target_pairs={{0,1},{1,0},{2,3},{3,2},{4,5},{5,4},{6,7},{7,6},{8,9},{9,8},{10,11... | collective-permute-start | bytes 737288 | tf_op jit(solution)/shard_map/ppermute | solution.py:935
  142.3 15.2 %collective-permute-start.34 = (bf16[160,768]{1,0:T(8,128)(2,1)}, bf16[160,768]{1,0:T(8,128)(2,1)S(1)}, u32[]{:S(2)}, u32[]{:S(2)}) collective-permute-start(bf16[160,768]{1,0:T(8,128)(2,1)} %get-tuple-element.115.refs_1_.refs_2_), channel_id=1, source_target_pairs={{0,2},{1,3},{2,0},{3,1},{4,6},{5,7},{6,4},{7,5},{8,10},{9,11},{10,... | collective-permute-start | bytes 737288 | tf_op jit(solution)/shard_map/ppermute | solution.py:935
  143.4 14.0 %collective-permute-start.35 = (bf16[160,768]{1,0:T(8,128)(2,1)}, bf16[160,768]{1,0:T(8,128)(2,1)S(1)}, u32[]{:S(2)}, u32[]{:S(2)}) collective-permute-start(bf16[160,768]{1,0:T(8,128)(2,1)} %get-tuple-element.115.refs_1_.refs_2_), channel_id=1, source_target_pairs={{0,3},{1,2},{2,1},{3,0},{4,7},{5,6},{6,5},{7,4},{8,11},{9,10},{10,... | collective-permute-start | bytes 737288 | tf_op jit(solution)/shard_map/ppermute | solution.py:935
  153.9 13.4 %collective-permute-start.30 = (bf16[160,384]{1,0:T(8,128)(2,1)}, bf16[160,384]{1,0:T(8,128)(2,1)S(1)}, u32[]{:S(2)}, u32[]{:S(2)}) collective-permute-start(bf16[160,384]{1,0:T(8,128)(2,1)} %get-tuple-element.117), channel_id=1, source_target_pairs={{0,1},{1,0},{2,3},{3,2},{4,5},{5,4},{6,7},{7,6},{8,9},{9,8},{10,11... | collective-permute-start | bytes 368648 | tf_op jit(solution)/shard_map/ppermute | solution.py:935
  167.4 80.9 %reduce-scatter.8.cloned.1.call-start = ((), (), s32[]{:S(2)}) async-start(), calls=%async_computation.5 | async-start | bytes 2691072 | tf_op jit(solution)/shard_map/reduce_scatter | solution.py:952
  213.4 34.9 %collective-permute-start.43 = (bf16[1152,128]{1,0:T(8,128)(2,1)}, bf16[1152,128]{1,0:T(8,128)(2,1)S(1)}, u32[]{:S(2)}, u32[]{:S(2)}) collective-permute-start(bf16[1152,128]{1,0:T(8,128)(2,1)} %bitcast.57), channel_id=1, source_target_pairs={{16,0},{17,1},{18,2},{19,3},{20,4},{21,5},{22,6},{23,7},{24,8},{25... | collective-permute-start | bytes 884744 | tf_op jit(solution)/shard_map/ppermute | solution.py:956
  (71 other events, 433.9 us)
Sparse Core Ops, SparseCore 0:
  53.1 43.4 all-gather.2
  136.1 36.2 reduce-scatter.5
  174.8 35.3 reduce-scatter.3
  212.3 35.9 reduce-scatter.7

commit v3 on v2

--- a/solution.py
+++ b/solution.py
@@ -20,7 +20,7 @@
 PACKED = SLOTS * 3 // 2
 PACKED_ROWS = ROWS * 3 // 2
 WINDOW = 256
-QUERY_BLOCKS = ((0, 256), (256, 256), (512, 128))
+QUERY_BLOCKS = ((0, 384), (384, 256))
 HALVES = ((0, 320), (320, 320))
 
 epsilon = 1e-05
@@ -255,20 +255,21 @@
 def first_attention(
     x_h, lengths, cos_h, sin_h, windows_h,
     normed_h, heads_h, packed_h,
-    x_blocks, gains, cos, sin, windows, normed, heads, packed, value_t, mixed_t, pair, single, sems,
+    x, gains, cos, sin, windows, normed, heads, packed, value_t, mixed_t, pair, single, sems,
 ):
     core, seq = place()
     move = Mover(sems, core)
-    copies_x = move.fetch_all(x_h, x_blocks)
+    copy_x = move.fetch(x_h, x)
     copy_gains = move.fetch_gains(0, windows_h, gains)
     copies_qkv = move.fetch_windows(0, windows_h, windows)
     copies_table = move.fetch_all((cos_h, sin_h), (cos, sin))
     copy_gains.wait()
     gain = gain_row(gains, 0)
-    for offset, block in enumerate(x_blocks):
-        copies_x[offset].wait()
-        wide_block = block[...].astype(f32)
-        normed[block_rows(seq ^ offset), :] = (wide_block * rms_scale(wide_block) * gain).astype(bf16)
+    copy_x.wait()
+    for first, count in HALVES:
+        rows = slice(first, first + count)
+        block = x[rows, :].astype(f32)
+        normed[rows, :] = (block * rms_scale(block) * gain).astype(bf16)
     move.send(normed, normed_h)
     wait(copies_table + copies_qkv)
     project(normed, windows, seq % 2 == 1, cos, sin, heads, value_t)
@@ -283,25 +284,24 @@
 def middle(
     x_h, mixed_h, lengths, cos_h, sin_h, o_h, ffn_h, windows_h,
     after_h, normed_two_h, hidden_h, mid_h, normed_h, heads_h, packed_h, blocks_h,
-    x_blocks, mixed, gains, gains_next, cos, sin, w_o, w_g, w_u, w_d, windows,
+    x, mixed, gains, gains_next, cos, sin, w_o, w_g, w_u, w_d, windows,
     after, normed_two, hidden, mid, normed, heads, packed, blocks, total, value_t, mixed_t, pair, single, sems,
 ):
     core, seq = place()
     move = Mover(sems, core)
-    copies_x = move.fetch_all(x_h, x_blocks)
+    copy_x = move.fetch(x_h, x)
     copy_o = move.fetch_layer(0, o_h[0].at[0], o_h[1].at[0], w_o)
     copies_gain = [move.fetch_gains(0, windows_h, gains), move.fetch_gains(1, windows_h, gains_next)]
-    copies_mixed = move.fetch_all(mixed_h, mixed)
+    copies_mixed = [move.fetch(mixed_h.at[part], target) for part, target in enumerate(mixed)]
     copies_ffn = move.fetch_ffn(0, ffn_h, (w_g, w_u, w_d))
     copies_qkv = move.fetch_windows(1, windows_h, windows)
     copies_table = move.fetch_all((cos_h, sin_h), (cos, sin))
-    for offset, block in enumerate(x_blocks):
-        copies_x[offset].wait()
-        after[block_rows(seq ^ offset), :] = block[...].astype(f32)
+    copy_x.wait()
+    after[...] = x[...].astype(f32)
     copy_o.wait()
-    for offset, block in enumerate(mixed):
-        share = w_o[block_rows(seq ^ offset, SHARE), :]
-        copies_mixed[offset].wait()
+    for part, block in enumerate(mixed):
+        share = w_o[part * SHARE : (part + 1) * SHARE, :]
+        copies_mixed[part].wait()
         whole = unpack(block[...], SLOTS)
         for first, count in HALVES:
             rows = slice(first, first + count)
@@ -541,15 +541,26 @@
 
 
 def attention_weights_grad(
-    normed_h, blocks_h, mixed_h, grads_h,
+    own, first_h, second_h,
     result_h,
     normed, blocks, mixed, grads, packed, whole, branch, output_grad, sems,
 ):
-    _, seq = place()
-    move = Mover(sems)
-    copies = move.fetch_all(mixed_h, mixed)
-    copies += move.fetch_all(grads_h, grads)
-    copies_qkv = move.fetch_all(blocks_h, blocks) + [move.fetch(normed_h, normed)]
+    core, seq = place()
+    move = Mover(sems, core)
+    layer = 0 if own else 1
+    normed_h, blocks_h, mixed_h, grads_h = (
+        list(zip(one, two)) if isinstance(one, (list, tuple)) else (one, two) for one, two in zip(first_h, second_h)
+    )
+
+    def fetch(pairs, targets):
+        return [move.fetch_layer(layer, *pair, target) for pair, target in zip(pairs, targets)]
+
+    copies = [
+        move.fetch_layer(layer, gathered_h.at[seq ^ offset], block_h, mixed[offset])
+        for offset, (gathered_h, block_h) in enumerate(mixed_h)
+    ]
+    copies += fetch(grads_h, grads)
+    copies_qkv = fetch(blocks_h, blocks) + fetch((normed_h,), (normed,))
     wait(copies)
     for offset, grad in enumerate(grads):
         branch[block_rows(seq ^ offset), :] = grad[:, SHARE:]
@@ -573,46 +584,49 @@
 def ffn_weights_grad(
     layer, left_h, y_h, ffn_h,
     result_h,
-    packed, w_g, w_u, w_d, normed_two, hidden, grad_out, grad_gate, grad_up, down, sems,
+    packed, w_g, w_u, w_d, normed_two, normed_t, hidden, grad_out, grad_gate, grad_up, down, sems,
 ):
     core, seq = place()
     move = Mover(sems, core)
     (g_own, g_other), (u_own, u_other), (d_own, d_other) = ffn_h
-    span = pl.ds(pl.multiple_of(seq * FF_SHARE, FF_SHARE), FF_SHARE)
+    spans = [pl.ds(pl.multiple_of(((seq + part) & 3) * FF_SHARE, FF_SHARE), FF_SHARE) for part in range(PARTS)]
+    span = spans[0]
     if layer == 0:
         copies = move.fetch_all(left_h, (normed_two, hidden))
-        copies += [move.fetch(block, grad_out.at[block_rows(seq ^ offset), :]) for offset, block in enumerate(y_h)]
     else:
         copies = [move.fetch(block, normed_two.at[block_rows(seq ^ offset), :]) for offset, block in enumerate(left_h)]
-        copies += [
-            move.fetch(y_h.at[part, core], grad_out.at[part * ROWS : (part + 1) * ROWS, :]) for part in range(PARTS)
-        ]
+    copies += [move.fetch(block, grad_out.at[block_rows(seq ^ offset), :]) for offset, block in enumerate(y_h)]
     copies += [
-        move.fetch_layer(layer, g_own.at[0, :, span], g_other.at[0, :, span], w_g.at[PARTS]),
-        move.fetch_layer(layer, u_own.at[0, :, span], u_other.at[0, :, span], w_u.at[PARTS]),
+        move.fetch_layer(layer, g_own.at[0, :, span], g_other.at[0, :, span], w_g.at[0]),
+        move.fetch_layer(layer, u_own.at[0, :, span], u_other.at[0, :, span], w_u.at[0]),
         move.fetch_layer(layer, d_own.at[0, span, :], d_other.at[0, span, :], w_d),
     ]
     copies_ffn = []
     if layer == 1:
-        for part in range(PARTS):
-            part_span = slice(part * FF_SHARE, (part + 1) * FF_SHARE)
+        for part in range(1, PARTS):
             copies_ffn.append(
                 (
-                    move.fetch_layer(layer, g_own.at[0, :, part_span], g_other.at[0, :, part_span], w_g.at[part]),
-                    move.fetch_layer(layer, u_own.at[0, :, part_span], u_other.at[0, :, part_span], w_u.at[part]),
+                    move.fetch_layer(
+                        layer, g_own.at[0, :, spans[part]], g_other.at[0, :, spans[part]], w_g.at[part]
+                    ),
+                    move.fetch_layer(
+                        layer, u_own.at[0, :, spans[part]], u_other.at[0, :, spans[part]], w_u.at[part]
+                    ),
                 )
             )
     wait(copies)
     for first, count in HALVES:
         rows = slice(first, first + count)
         block = normed_two[rows, :]
-        grad_gate[rows, :], grad_up[rows, :] = ffn_back_chunk(
-            nn(block, w_g[PARTS]), nn(block, w_u[PARTS]), nt(grad_out[rows, :], w_d[...])
-        )
+        gate, up = nn(block, w_g[0]), nn(block, w_u[0])
+        grad_gate[rows, :], grad_up[rows, :] = ffn_back_chunk(gate, up, nt(grad_out[rows, :], w_d[...]))
+        if layer == 1:
+            hidden[rows, span] = (gate * jax.nn.sigmoid(gate) * up).astype(bf16)
     groups = packed.shape[0]
     tile_rows = DIM // groups
+    normed_t[...] = jnp.transpose(normed_two[...])
     for index, grads in enumerate((grad_gate, grad_up)):
-        result = tn(normed_two[...], grads[...])
+        result = nn(normed_t[...], grads[...])
         for group in range(groups):
             span = slice(group * tile_rows, (group + 1) * tile_rows)
             for tile in range(4):
@@ -620,46 +634,67 @@
 
     window = grad_out[:, pl.ds(window_start(seq), WINDOW)].astype(f32)
     columns = jnp.where(seq % 2 == 1, pltpu.roll(window, WINDOW - HEAD_DIM, 1), window)
-    columns = columns[:, :SHARE].astype(bf16)
+    columns_t = jnp.transpose(columns)[:SHARE].astype(bf16)
     for part in range(PARTS):
-        part_span = slice(part * FF_SHARE, (part + 1) * FF_SHARE)
-        if layer == 1:
-            wait(copies_ffn[part])
+        if layer == 1 and part > 0:
+            wait(copies_ffn[part - 1])
             for first, count in HALVES:
                 rows = slice(first, first + count)
                 gate = nn(normed_two[rows, :], w_g[part])
                 up = nn(normed_two[rows, :], w_u[part])
-                hidden[rows, part_span] = (gate * jax.nn.sigmoid(gate) * up).astype(bf16)
-        down[part_span, :] = tn(hidden[:, part_span], columns)
-    quarter = FF // groups // 4
+                hidden[rows, spans[part]] = (gate * jax.nn.sigmoid(gate) * up).astype(bf16)
+        down[:, spans[part]] = nn(columns_t, hidden[:, spans[part]])
+    width = FF // groups // 2
     for index in range(2):
         for group in range(groups):
-            begin = (group * 4 + index * 2) * quarter
-            both = jnp.concatenate(
-                [down[begin : begin + quarter, :], down[begin + quarter : begin + 2 * quarter, :]], axis=1
-            ).astype(bf16)
-            for tile in range(3):
-                place_at = 4 * tile_rows + tile * quarter
-                packed[group, index, place_at : place_at + quarter, :] = columns_of(both, tile)
+            begin = (group * 2 + index) * width
+            pack_down(down, begin, width, packed.at[group, index, 4 * tile_rows :, :])
     move.send(packed, result_h)
     move.finish()
 
 
-def join_attention(parts_h, gains_h, result_h, gains, result, sems):
+def pack_down(down, begin, width, target):
+    if width >= 128:
+        for tile in range(width // 128):
+            source = down[:, begin + tile * 128 : begin + (tile + 1) * 128]
+            target[tile * SHARE : (tile + 1) * SHARE, :] = source.astype(bf16)
+    else:
+        rows = SHARE * width // 128
+        piece = down[:, begin : begin + width]
+        target[...] = jnp.concatenate(
+            [piece[part * rows : (part + 1) * rows] for part in range(128 // width)], axis=1
+        ).astype(bf16)
+
+
+def unpack_down(source, target, begin, width):
+    if width >= 128:
+        for tile in range(width // 128):
+            piece = source[tile * SHARE : (tile + 1) * SHARE, :]
+            target[0, :, begin + tile * 128 : begin + (tile + 1) * 128] = piece.astype(f32)
+    else:
+        rows = SHARE * width // 128
+        for part in range(128 // width):
+            piece = source[:, part * width : (part + 1) * width]
+            target[0, part * rows : (part + 1) * rows, begin : begin + width] = piece.astype(f32)
+
+
+def add_parts(keep_h, received_h, total_h, keep, received, total, sems):
     move = Mover(sems)
-    rows = result.shape[2] - GAIN_ROWS
-    copies = [move.fetch(part, result.at[:, layer, :rows, :]) for layer, part in enumerate(parts_h)]
-    move.fetch(gains_h, gains).wait()
-    result[:, :, rows:, :] = gains[...].astype(bf16)
-    wait(copies)
-    move.send(result, result_h)
+    copies = [
+        move.fetch_all((keep_h.at[group], received_h.at[group]), (keep.at[group], received.at[group]))
+        for group in range(keep.shape[0])
+    ]
+    for group, pair in enumerate(copies):
+        wait(pair)
+        total[group] = (keep[group].astype(f32) + received[group].astype(f32)).astype(bf16)
+        move.send(total.at[group], total_h.at[group])
     move.finish()
 
 
 def write_weights(
     ffn_0, ffn_1, attn_h, ffn_other_0, ffn_other_1,
-    q_h, k_h, v_h, o_h, g_h, u_h, d_h, gain_h,
-    ffn_low, ffn_high, attn, q, k, v, o, g, u, d, gain, sems,
+    q_h, k_h, v_h, o_h, g_h, u_h, d_h,
+    ffn_low, ffn_high, attn, q, k, v, o, g, u, d, sems,
 ):
     core, _ = place()
     move = Mover(sems, core)
@@ -668,34 +703,28 @@
         move.fetch_layer(0, ffn_other_0, ffn_1, ffn_high),
         move.fetch(attn_h, attn),
     ]
-    wait(copies)
+    wait(copies[:2])
     rows = q.shape[1]
-    quarter = d.shape[2] // 4
-    for index, (ffn, wide_out, pair) in enumerate(((ffn_low, g, (q, k)), (ffn_high, u, (v, o)))):
+    for index, (ffn, wide_out) in enumerate(((ffn_low, g), (ffn_high, u))):
         for tile in range(4):
             wide_out[0, :, tile * 128 : (tile + 1) * 128] = ffn[tile * rows : (tile + 1) * rows, :].astype(f32)
-        place_at = 4 * rows
-        both = jnp.concatenate(
-            [ffn[place_at + tile * quarter : place_at + (tile + 1) * quarter, :].astype(f32) for tile in range(3)],
-            axis=1,
-        )
-        begin = index * 2 * quarter
-        turned = jnp.transpose(both)
-        d[0, :, begin : begin + quarter] = turned[:SHARE]
-        d[0, :, begin + quarter : begin + 2 * quarter] = turned[SHARE:]
+        width = d.shape[2] // 2
+        unpack_down(ffn.at[4 * rows :, :], d, index * width, width)
+    for source, target in zip((g, u, d), (g_h, u_h, d_h)):
+        move.send(source, target)
+    copies[2].wait()
+    for index, pair in enumerate(((q, k), (v, o))):
         both = jnp.concatenate(
             [
-                attn[(index * 3 + tile) * rows : (index * 3 + tile + 1) * rows, :].astype(f32)
+                jnp.sum(attn[:, (index * 3 + tile) * rows : (index * 3 + tile + 1) * rows, :].astype(f32), axis=0)
                 for tile in range(3)
             ],
             axis=1,
         )
         pair[0][0] = both[:, :SHARE]
         pair[1][0] = both[:, SHARE:]
-    for source, target in zip((q, k, v, o, g, u, d), (q_h, k_h, v_h, o_h, g_h, u_h, d_h)):
+    for source, target in zip((q, k, v, o), (q_h, k_h, v_h, o_h)):
         move.send(source, target)
-    gain[...] = attn[6 * rows :, :].astype(f32)
-    move.send(gain, gain_h)
     move.finish()
 
 
@@ -707,7 +736,7 @@
     return pltpu.VMEM(dims, dtype)
 
 
-def call(body, args, outs, scratch, micros, name, after=()):
+def call(body, args, outs, scratch, micros, name, after=(), vmem=VMEM_MIB):
     leaves, tree = jax.tree.flatten(args)
     out_leaves, out_tree = jax.tree.flatten(outs)
     scratch_leaves, scratch_tree = jax.tree.flatten(scratch)
@@ -729,7 +758,7 @@
         in_specs=[spec(leaf) for leaf in leaves] + [pl.BlockSpec(memory_space=pltpu.HBM)] * len(after),
         out_specs=[pl.BlockSpec(memory_space=pltpu.HBM)] * len(out_leaves),
         scratch_shapes=scratch_leaves,
-        compiler_params=pltpu.CompilerParams(vmem_limit_bytes=VMEM_MIB * MIB),
+        compiler_params=pltpu.CompilerParams(vmem_limit_bytes=vmem * MIB),
         cost_estimate=pl.CostEstimate(flops=micros * COST, bytes_accessed=10**4, transcendentals=0),
         name=name,
     )(*leaves, *after)
@@ -768,14 +797,15 @@
     )[0]
 
 
-def call_first_attention(*args):
+def call_first_attention(*args, after=()):
     return call(
         first_attention,
         args,
         [shape(SLOTS, DIM), shape(*HEADS), shape(PACKED, 128)],
-        [[vm(*ROW)] * 4, GAINS, *TABLES, WINDOWS, vm(SLOTS, DIM), vm(*HEADS), vm(PACKED, 128), *ATTEND, sems(16)],
+        [vm(SLOTS, DIM), GAINS, *TABLES, WINDOWS, vm(SLOTS, DIM), vm(*HEADS), vm(PACKED, 128), *ATTEND, sems(16)],
         10,
         "first_attention",
+        after,
     )
 
 
@@ -788,7 +818,7 @@
             shape(*HEADS), shape(PACKED, 128), [shape(PACKED_ROWS, 128)] * 4,
         ],
         [
-            [vm(*ROW)] * 4, [vm(PACKED, 128)] * 4, GAINS, GAINS, *TABLES, *WEIGHTS, WINDOWS,
+            vm(SLOTS, DIM), [vm(PACKED, 128)] * 4, GAINS, GAINS, *TABLES, *WEIGHTS, WINDOWS,
             vm(SLOTS, DIM, dtype=f32), vm(SLOTS, DIM), vm(SLOTS, FF), vm(SLOTS, DIM), vm(SLOTS, DIM),
             vm(*HEADS), vm(PACKED, 128), [vm(PACKED_ROWS, 128)] * 4, vm(SLOTS, DIM, dtype=f32), *ATTEND, sems(48),
         ],
@@ -859,10 +889,10 @@
     )
 
 
-def call_attention_weights_grad(groups, *args, after=()):
+def call_attention_weights_grad(own, groups, *args, after=()):
     out = (groups, 6 * DIM // groups, 128)
     return call(
-        attention_weights_grad,
+        functools.partial(attention_weights_grad, own),
         args,
         [shape(*out)],
         [
@@ -882,9 +912,9 @@
         args,
         [shape(*out)],
         [
-            vm(*out), vm(PARTS + 1, DIM, FF_SHARE), vm(PARTS + 1, DIM, FF_SHARE), vm(FF_SHARE, DIM),
-            vm(SLOTS, DIM), vm(SLOTS, FF), vm(SLOTS, DIM), vm(SLOTS, FF_SHARE), vm(SLOTS, FF_SHARE),
-            vm(FF, SHARE, dtype=f32), sems(48),
+            vm(*out), vm(PARTS, DIM, FF_SHARE), vm(PARTS, DIM, FF_SHARE), vm(FF_SHARE, DIM),
+            vm(SLOTS, DIM), vm(DIM, SLOTS), vm(SLOTS, FF), vm(SLOTS, DIM), vm(SLOTS, FF_SHARE), vm(SLOTS, FF_SHARE),
+            vm(SHARE, FF, dtype=f32), sems(48),
         ],
         15,
         "ffn_weights_grad",
@@ -892,22 +922,22 @@
     )[0]
 
 
-def call_join_attention(parts, gains):
-    groups, rows, _ = parts[0].shape
-    out = (groups, len(parts), rows + GAIN_ROWS, 128)
+def call_add_parts(keep, received, after):
+    dims = keep.shape
     return call(
-        join_attention,
-        (parts, gains),
-        [shape(*out)],
-        [vm(*gains.shape, dtype=f32), vm(*out), sems(8)],
+        add_parts,
+        (keep, received),
+        [shape(*dims)],
+        [vm(*dims), vm(*dims), vm(*dims), sems(3 * dims[0])],
         3,
-        "join_attention",
+        "add_parts",
+        after,
     )[0]
 
 
 def call_write_weights(groups, *args):
     rows = DIM // groups
-    dims = [(1, rows, SHARE)] * 4 + [(1, rows, FF_SHARE)] * 2 + [(1, SHARE, FF // groups), (GAIN_ROWS, 128)]
+    dims = [(1, rows, SHARE)] * 4 + [(1, rows, FF_SHARE)] * 2 + [(1, SHARE, FF // groups)]
     ffn, _, attn = args[:3]
     return call(
         write_weights,
@@ -916,6 +946,7 @@
         [vm(*ffn.shape), vm(*ffn.shape), vm(*attn.shape)] + [vm(*dim, dtype=f32) for dim in dims] + [sems(16)],
         3,
         "write_weights",
+        vmem=24,
     )
 
 
@@ -964,34 +995,28 @@
     core = lax.axis_index("section")
     is_first = core == 0
     inputs = lax.dynamic_index_in_dim(section_input, core, 0, keepdims=False)
+    cotangent = lax.dynamic_index_in_dim(out_cotangent, core, 0, keepdims=False)
     cos, sin = (jnp.asarray(table) for table in rotary_tables())
-    x_blocks = gathered(inputs)
     windows = call_pack_windows((w_query, w_key, w_value), (attn_gain, ffn_gain))
     windows = (windows, swap(windows))
-    o_pair, g_pair, u_pair, d_pair = (
-        (weight, swap(later(weight, *earlier)))
-        for weight, *earlier in (
-            (w_output, windows[1]),
-            (w_gate, windows[1]),
-            (w_up, windows[1], x_blocks),
-            (w_down, windows[1], x_blocks),
-        )
-    )
-    ffn = (g_pair, u_pair, d_pair)
-
-    normed_0, heads_0, packed_0 = call_first_attention(x_blocks, lengths, cos, sin, windows)
-    mixed_0 = gathered(later(packed_0, o_pair[1], g_pair[1]))
+    x_all = lax.all_gather(later(inputs, windows[0]), "seq", axis=0, tiled=True)
+    o_pair, *ffn = ((weight, swap(later(weight, x_all, windows[1]))) for weight in (w_output, w_gate, w_up, w_down))
+
+    normed_0, heads_0, packed_0 = call_first_attention(x_all, lengths, cos, sin, windows)
+    mixed_0 = lax.all_gather(packed_0, "seq", axis=0)
     after_0, normed_two_0, hidden_0, mid, normed_1, heads_1, packed_1, mixed_blocks = call_middle(
-        x_blocks, mixed_0, lengths, cos, sin, o_pair, ffn, windows
-    )
-    cotangent_all = lax.all_gather(later(out_cotangent, mixed_0), "seq", axis=0)
-    qkv = tuple((weight, swap(later(weight, mixed_0))) for weight in (w_query, w_key, w_value))
-    mixed_rows = exchanged(mixed_blocks)
+        x_all, mixed_0, lengths, cos, sin, o_pair, ffn, windows
+    )
+    others = [pair[1] for pair in (o_pair, *ffn)]
+    cotangent_all = gathered(later(cotangent, mixed_0, others))
+    q_pair, k_pair = ((weight, swap(later(weight, mixed_0, others))) for weight in (w_query, w_key))
+    qkv = (q_pair, k_pair, (w_value, swap(later(w_value, cotangent_all, q_pair[1]))))
+    mixed_rows = exchanged(later(mixed_blocks, cotangent_all[1:], q_pair[1], k_pair[1]))
     mixed_1 = gathered(later(packed_1, mixed_rows[1]))
     output, normed_two_1, grad_after_1, gain_ffn_1, grad_blocks_1 = call_last_rows(
-        mid, out_cotangent, mixed_rows, windows, o_pair, ffn, after=[pair[1] for pair in qkv]
-    )
-    grad_mixed_1 = exchanged(grad_blocks_1)
+        mid, out_cotangent, mixed_rows, windows, o_pair, ffn
+    )
+    grad_mixed_1 = exchanged(later(grad_blocks_1, mixed_1))
     normed_two_all = gathered(later(normed_two_1, grad_mixed_1[1], mixed_1))
     grad_qkv_1 = call_attention_back(grad_mixed_1, lengths, cos, sin, heads_1)
     grad_rows_1 = exchanged(grad_qkv_1)
@@ -1006,40 +1031,48 @@
         0, groups, (normed_two_0, hidden_0), grad_mid_all, ffn, after=(grad_after_0,)
     )
     grad_mixed_0, parts_f0 = lax.optimization_barrier((grad_mixed_0, parts_f0))
-    sum_f0 = sum_over_items(parts_f0)
+    sum_f0 = sum_over_items(later(parts_f0, sum_f1))
     grad_qkv_0 = call_attention_back(grad_mixed_0, lengths, cos, sin, heads_0)
     grad_rows_0 = exchanged(grad_qkv_0)
-    parts_a1 = call_attention_weights_grad(
-        groups, normed_1, grad_qkv_1, mixed_1, grad_mixed_1, after=(grad_qkv_0[0],)
-    )
-    parts_a0 = call_attention_weights_grad(
-        groups, normed_0, grad_qkv_0, mixed_0, grad_mixed_0, after=(parts_a1,)
-    )
-    grad_first, gain_attn_0 = call_input_back(
-        0, grad_rows_0, inputs, grad_after_0, windows, qkv, after=(parts_a0,)
-    )
+    of_layers = (
+        (normed_0, grad_qkv_0, [mixed_0] * PARTS, grad_mixed_0),
+        (normed_1, grad_qkv_1, mixed_1, grad_mixed_1),
+    )
+    send_a = call_attention_weights_grad(False, groups, *of_layers, after=(grad_qkv_0[0],))
+    keep_a = call_attention_weights_grad(True, groups, *of_layers, after=(send_a,))
+    send_a, keep_a = lax.optimization_barrier((send_a, keep_a))
+    received_a = swap(send_a)
+    grad_first, gain_attn_0 = call_input_back(0, grad_rows_0, inputs, grad_after_0, windows, qkv, after=(keep_a,))
+    added_a = call_add_parts(keep_a, received_a, after=(grad_first,))
+    sums_a = lax.all_to_all(added_a, "dp", split_axis=0, concat_axis=0, tiled=True)
 
     share = DIM // (groups * PARTS)
     gain_grads = jnp.concatenate([gain_attn_0, gain_ffn_0, gain_attn_1, gain_ffn_1], axis=0)
-    gain_grads = gain_grads.reshape(2, 2, groups, PARTS, share).transpose(3, 2, 0, 1, 4)
-    seq = lax.axis_index("seq")
-    gain_parts = exchanged(
-        [lax.dynamic_index_in_dim(gain_grads, seq ^ offset, 0, keepdims=False) for offset in range(PARTS)]
-    )
-    gain_rows = jnp.pad(sum(gain_parts), ((0, 0), (0, 0), (0, GAIN_ROWS - 2), (0, 128 - share)))
-    sum_attn = sum_over_items(call_join_attention((parts_a0, parts_a1), gain_rows))
+    gain_grads = later(gain_grads, added_a).reshape(2, 2, groups, PARTS, share)
+    seq, here = lax.axis_index("seq"), lax.axis_index("dp")
+    gain_grads = sum(
+        exchanged([lax.dynamic_index_in_dim(gain_grads, seq ^ offset, 3, keepdims=False) for offset in range(PARTS)])
+    )
+    gain_grads = jnp.where(is_first, gain_grads[0], gain_grads[1]) + swap(
+        jnp.where(is_first, gain_grads[1], gain_grads[0])
+    )
+    gain_sums = lax.dynamic_index_in_dim(gain_grads, here, 1, keepdims=False)
+    for offset in range(1, groups):
+        part = lax.dynamic_index_in_dim(gain_grads, lax.rem(here + offset, groups), 1, keepdims=False)
+        gain_sums = gain_sums + lax.ppermute(
+            part, "dp", [(group, (group + offset) % groups) for group in range(groups)]
+        )
 
     def sort(of_first, of_second):
         mine = jnp.where(is_first, of_first, of_second)
         other = swap(jnp.where(is_first, of_second, of_first))
         return jnp.where(is_first, mine, other), jnp.where(is_first, other, mine)
 
-    section_outputs = jnp.stack(sort(mid, output))[None]
+    section_outputs = jnp.stack(sort(*later((mid, output), grad_qkv_0[0])))[None]
     input_grads = jnp.stack(sort(grad_first, grad_mid))[None]
-    g_query, g_key, g_value, g_output, g_gate, g_up, g_down, gain_sums = call_write_weights(
-        groups, sum_f0, sum_f1, sum_attn, give(sum_f0, 1), give(sum_f1, 0)
-    )
-    gain_sums = gain_sums[:2, :share]
+    g_query, g_key, g_value, g_output, g_gate, g_up, g_down = call_write_weights(
+        groups, sum_f0, sum_f1, sums_a, give(sum_f0, 1), give(sum_f1, 0)
+    )
     return (
         section_outputs, input_grads, gain_sums[0:1], g_query, g_key, g_value, g_output, gain_sums[1:2],
         g_gate, g_up, g_down.transpose(0, 2, 1),

time: 265 us -> 245 us (0.925)
  waiting for transfers between devices: 73 us -> 22.2 us
  blocking collectives: 0 us -> 31.7 us
  starting transfers between devices: 46 us -> 52.6 us
  Pallas kernels: 114 us -> 109 us
    reduce_scatter x3 -> x2, waiting for transfers between devices: 32.7 us -> 0.02 us  [sum_over_items(): return lax.psum_scatter(parts, ('dp', 'section'), scatter_dimension=0)]
    all_gather x0 -> x2, blocking collectives: none -> 31.7 us  [the longest x1 16.6 us: on_device(): x_all = lax.all_gather(later(inputs, windows[0]), 'seq', axis=0, tiled=True)]
    ppermute x33 -> x30, waiting for transfers between devices: 35.9 us -> 5.42 us  [to_partner(): lax.ppermute(value, 'seq', [(part, part ^ offset) for part in range(PARTS)])]
    ppermute x0 -> x3, waiting for transfers between devices: none -> 15.6 us  [on_device(): lax.ppermute(part, 'dp', [(group, (group + offset) % groups) for group in...]
    ppermute x0 -> x3, starting transfers between devices: none -> 5.9 us  [on_device(): lax.ppermute(part, 'dp', [(group, (group + offset) % groups) for group in...]
    pallas_call x15, Pallas kernels: 114 us -> 109 us  [call(): pl.pallas_call(kernel, out_shape=out_leaves, in_specs=[spec(leaf) for lea...]
    all_to_all x0 -> x1, starting transfers between devices: none -> 4.88 us  [on_device(): lax.all_to_all(added_a, 'dp', split_axis=0, concat_axis=0, tiled=True)]
    ppermute x33 -> x30, starting transfers between devices: 39.5 us -> 35.4 us  [to_partner(): lax.ppermute(value, 'seq', [(part, part ^ offset) for part in range(PARTS)])]
  transfers between devices with their start and end apart: 49 -> 50, of which waited for: 16 -> 8; matrix products, arithmetic and copies ran while one was open for 1% -> 1% of each run, Pallas kernels for 42% -> 43%
where the time goes in v3:
time: 245 us; the launch traced here: 241 us
  Pallas kernels  109 us (44%)
  starting transfers between devices  52.6 us (21%)
  blocking collectives  31.7 us (13%)
  waiting for transfers between devices  22.2 us (9%)
  between operations  15.2 us (6%)
  local copies, waits for them, and re-layouts  7.71 us (3%)
  other arithmetic  2.53 us (1%)
    pallas_call x15, Pallas kernels, call(): pl.pallas_call(kernel, out_shape=out_leaves, in_specs=[spec(leaf) for lea...  109 us
    ppermute x30, starting transfers between devices, to_partner(): lax.ppermute(value, 'seq', [(part, part ^ offset) for part in range(PARTS)])  35.4 us
    all_gather x1, blocking collectives, on_device(): x_all = lax.all_gather(later(inputs, windows[0]), 'seq', axis=0, tiled=True)  16.6 us
    ppermute x3, waiting for transfers between devices, on_device(): lax.ppermute(part, 'dp', [(group, (group + offset) % groups) for group in...  15.6 us
    all_gather x1, blocking collectives, on_device(): mixed_0 = lax.all_gather(packed_0, 'seq', axis=0)  15.2 us
    unnamed x92, local copies, waits for them, and re-layouts  7.01 us
    ppermute x3, starting transfers between devices, on_device(): lax.ppermute(part, 'dp', [(group, (group + offset) % groups) for group in...  5.9 us
    ppermute x30, waiting for transfers between devices, to_partner(): lax.ppermute(value, 'seq', [(part, part ^ offset) for part in range(PARTS)])  5.42 us
  transfers between devices with their start and end apart: 50, of which 8 were waited for; matrix products, arithmetic and copies ran while one was open for 1% of the time, Pallas kernels for 43%

profile of v3, /device:TPU:0, one launch (start us, length us, event | category | flops | bytes accessed | tf_op | source)
XLA Modules:
  0.0 240.6 jit_solution(1681634708659047397)
XLA Ops:
  7.2 2.5 %pack_windows.1.refs_4_.refs_13_.refs_6_.refs_2_ = bf16[2320,256]{1,0:T(8,128)(2,1)} custom-call(bf16[1,768,768]{2,1,0:T(8,128)(2,1)} %refs_8_.11, bf16[1,768,768]{2,1,0:T(8,128)(2,1)} %refs_10_.11, bf16[1,768,768]{2,1,0:T(8,128)(2,1)} %refs_12_.7, bf16[1,768]{1,0:T(2,128)(2,1)} %refs_3_.3, bf16[1,768]{1,0:T(2,128)(2,1)} %refs_4_.5), custom_call_target="tpu_custom_call" | custom-call | flops 3000000000 | bytes 10000 | tf_op jit(solution)/shard_map/pack_windows/pallas_call | solution.py:755
  10.3 16.6 %all_gather.9.refs_0_ = bf16[640,768]{1,0:T(8,128)(2,1)} all-gather(bf16[160,768]{1,0:T(8,128)(2,1)S(1)} %dynamic-slice_bitcast_fusion.1.refs_4_), channel_id=1, replica_groups=mesh['section'=2,'dp'=4,'seq'=4] {'seq'}, dimensions={0}, use_global_device_ids=true | all-gather | bytes 1228800 | tf_op jit(solution)/shard_map/all_gather | solution.py:1002
  28.0 7.4 %first_attention.1 = (bf16[640,768]{1,0:T(8,128)(2,1)}, bf16[3,3,640,64]{3,2,1,0:T(8,128)(2,1)}, bf16[960,128]{1,0:T(8,128)(2,1)}) custom-call(bf16[640,768]{1,0:T(8,128)(2,1)} %all_gather.9.refs_0_, s32[2]{0:T(128)} %refs_4_.8, f32[640,128]{1,0:T(8,128)} %constant.59.clone.refs_2_.refs_3_.refs_5_, f32[640,128]{1,0:T(8,128)} %constant.60.clone.refs_3_.refs_4_.refs_6_, ...), custom_call_target="tpu_custom_call" | custom-call | flops 10000000000 | bytes 10000 | tf_op jit(solution)/shard_map/first_attention/pallas_call | solution.py:755
  35.5 15.2 %all-gather = bf16[3840,128]{1,0:T(8,128)(2,1)} all-gather(bf16[960,128]{1,0:T(8,128)(2,1)} %get-tuple-element.94), channel_id=2, replica_groups=mesh['section'=2,'dp'=4,'seq'=4] {'seq'}, dimensions={0}, use_global_device_ids=true | all-gather | bytes 1228800 | tf_op jit(solution)/shard_map/all_gather | solution.py:1006
  54.8 17.0 %middle.1 = (f32[160,768]{1,0:T(8,128)}, bf16[640,768]{1,0:T(8,128)(2,1)}, bf16[640,2048]{1,0:T(8,128)(2,1)}, bf16[160,768]{1,0:T(8,128)(2,1)}, bf16[640,768]{1,...) custom-call(bf16[640,768]{1,0:T(8,128)(2,1)} %all_gather.9.refs_0_, ...), custom_call_target="tpu_custom_call" | custom-call | flops 20000000000 | bytes 10000 | tf_op jit(solution)/shard_map/middle/pallas_call | solution.py:755
  80.5 10.3 %last_rows.1 = (bf16[160,768]{1,0:T(8,128)(2,1)}, bf16[160,768]{1,0:T(8,128)(2,1)}, f32[160,768]{1,0:T(8,128)}, f32[1,768]{1,0:T(1,128)}, bf16[160,384]{1,0:T(8,...) custom-call(bf16[160,768]{1,0:T(8,128)(2,1)} %get-tuple-element.150.refs_0_.refs_4_, ...), custom_call_target="tpu_custom_call" | custom-call | flops 11000000512 | bytes 10000 | tf_op jit(solution)/shard_map/last_rows/pallas_call | solution.py:755
  94.4 1.6 collective-permute-done.16.refs_1_.refs_23_
  100.0 9.0 %attention_back.2 = (bf16[160,576]{1,0:T(8,128)(2,1)}, bf16[160,576]{1,0:T(8,128)(2,1)}, bf16[160,576]{1,0:T(8,128)(2,1)}, bf16[160,576]{1,0:T(8,128)(2,1)}) custom-call(bf16[160,384]{1,0:T(8,128)(2,1)} %get-tuple-element.119.refs_0_.refs_22_, bf16[160,384]{1,0:T(8,128)(2,1)} %copy-done.39, bf16[160,384]{1,0:T(8,128)(2,1)} %collective-permute-done.17.refs_2_.refs_24_, ...), custom_call_target="tpu_custom_call" | custom-call | flops 11000000512 | bytes 10000 | tf_op jit(solution)/shard_map/attention_back/pallas_call | solution.py:755
  113.4 12.0 %ffn_weights_grad.2 = bf16[4,2,1152,128]{3,2,1,0:T(8,128)(2,1)} custom-call(bf16[160,768]{1,0:T(8,128)(2,1)} %get-tuple-element.129.refs_0_, bf16[160,768]{1,0:T(8,128)(2,1)} %copy-done.27, bf16[160,768]{1,0:T(8,128)(2,1)} %copy-done.28, bf16[160,768]{1,0:T(8,128)(2,1)} %copy-done.31, bf16[160,768]{1,0:T(8,128)(2,1)} %copy-done.9, ...), custom_call_target="tpu_custom_call" | custom-call | flops 15000000512 | bytes 10000 | tf_op jit(solution)/shard_map/ffn_weights_grad/pallas_call | solution.py:755
  127.3 4.6 %input_back.2 = (bf16[160,768]{1,0:T(8,128)(2,1)}, f32[1,768]{1,0:T(1,128)}) custom-call(bf16[160,576]{1,0:T(8,128)(2,1)} %get-tuple-element.130.refs_14_.refs_0_, bf16[160,576]{1,0:T(8,128)(2,1)} %copy-done.33, bf16[160,576]{1,0:T(8,128)(2,1)} %copy-done.34, bf16[160,576]{1,0:T(8,128)(2,1)} %copy-done.35, ...), custom_call_target="tpu_custom_call" | custom-call | flops 10000000000 | bytes 10000 | tf_op jit(solution)/shard_map/input_back/pallas_call | solution.py:755
  135.5 9.2 %first_rows_back.1 = (f32[160,768]{1,0:T(8,128)}, f32[1,768]{1,0:T(1,128)}, bf16[160,384]{1,0:T(8,128)(2,1)}, bf16[160,384]{1,0:T(8,128)(2,1)}, bf16[160,384]{1,0:T(8,128)(2,1)}, /*index=5*/bf16[160,384]{1,0:T(8,128)(2,1)}) custom-call(f32[160,768]{1,0:T(8,128)} %get-tuple-element.112.refs_0_, bf16[160,768]{1,0:T(8,128)(2,1)} %get-tuple-element.136.refs_1_.refs_2_, ...), custom_call_target="tpu_custom_call" | custom-call | flops 10000000000 | bytes 10000 | tf_op jit(solution)/shard_map/first_rows_back/pallas_call | solution.py:755
  149.1 8.8 %ffn_weights_grad.3 = bf16[4,2,1152,128]{3,2,1,0:T(8,128)(2,1)} custom-call(bf16[640,768]{1,0:T(8,128)(2,1)} %get-tuple-element.141.refs_0_, bf16[640,2048]{1,0:T(8,128)(2,1)} %get-tuple-element.142.refs_1_, bf16[160,768]{1,0:T(8,128)(2,1)} %get-tuple-element.136.refs_1_.refs_2_, bf16[160,768]{1,0:T(8,128)(2,1)} %copy-done.29, bf16[160,768]{1,0:T(8,128)(2,1)} %copy-done.30, ...), custom_call_target="tpu_custom_call" | custom-call | flops 15000000512 | bytes 10000 | tf_op jit(solution)/shard_map/ffn_weights_grad/pallas_call | solution.py:755
  158.6 9.0 %attention_back.3 = (bf16[160,576]{1,0:T(8,128)(2,1)}, bf16[160,576]{1,0:T(8,128)(2,1)}, bf16[160,576]{1,0:T(8,128)(2,1)}, bf16[160,576]{1,0:T(8,128)(2,1)}) custom-call(bf16[160,384]{1,0:T(8,128)(2,1)} %get-tuple-element.144.refs_0_.refs_9_, bf16[160,384]{1,0:T(8,128)(2,1)} %copy-done.40, bf16[160,384]{1,0:T(8,128)(2,1)} %copy-done.41, ...), custom_call_target="tpu_custom_call" | custom-call | flops 11000000512 | bytes 10000 | tf_op jit(solution)/shard_map/attention_back/pallas_call | solution.py:755
  171.2 4.6 %attention_weights_grad.2.refs_26_ = bf16[4,1152,128]{2,1,0:T(8,128)(2,1)} custom-call(bf16[640,768]{1,0:T(8,128)(2,1)} %get-tuple-element.155.refs_0_, bf16[160,576]{1,0:T(8,128)(2,1)} %get-tuple-element.149.refs_1_.refs_26_.refs_0_, bf16[160,576]{1,0:T(8,128)(2,1)} %get-tuple-element.152.refs_2_, bf16[160,576]{1,0:T(8,128)(2,1)} %get-tuple-element.153.refs_3_, ...), custom_call_target="tpu_custom_call" | custom-call | flops 8000000000 | bytes 10000 | tf_op jit(solution)/shard_map/attention_weights_grad/pallas_call | solution.py:755
  175.9 5.1 %attention_weights_grad.3.refs_14_.refs_0_ = bf16[4,1152,128]{2,1,0:T(8,128)(2,1)} custom-call(bf16[640,768]{1,0:T(8,128)(2,1)} %get-tuple-element.155.refs_0_, bf16[160,576]{1,0:T(8,128)(2,1)} %get-tuple-element.149.refs_1_.refs_26_.refs_0_, bf16[160,576]{1,0:T(8,128)(2,1)} %get-tuple-element.152.refs_2_, bf16[160,576]{1,0:T(8,128)(2,1)} %get-tuple-element.153.refs_3_, ...), custom_call_target="tpu_custom_call" | custom-call | flops 8000000000 | bytes 10000 | tf_op jit(solution)/shard_map/attention_weights_grad/pallas_call | solution.py:755
  183.2 4.6 %input_back.3 = (bf16[160,768]{1,0:T(8,128)(2,1)}, f32[1,768]{1,0:T(1,128)}) custom-call(bf16[160,576]{1,0:T(8,128)(2,1)} %get-tuple-element.149.refs_1_.refs_26_.refs_0_, bf16[160,576]{1,0:T(8,128)(2,1)} %copy-done.36, bf16[160,576]{1,0:T(8,128)(2,1)} %copy-done.37, bf16[160,576]{1,0:T(8,128)(2,1)} %copy-done.38, bf16[160,768]{1,0:T(8,128)(2,1)} %copy-done.4, ...), custom_call_target="tpu_custom_call" | custom-call | flops 10000000000 | bytes 10000 | tf_op jit(solution)/shard_map/input_back/pallas_call | solution.py:755
  189.7 2.5 %add_parts.1 = bf16[4,1152,128]{2,1,0:T(8,128)(2,1)} custom-call(bf16[4,1152,128]{2,1,0:T(8,128)(2,1)} %attention_weights_grad.3.refs_14_.refs_0_, bf16[4,1152,128]{2,1,0:T(8,128)(2,1)} %collective-permute-done.37.refs_1_, bf16[160,768]{1,0:T(8,128)(2,1)} %get-tuple-element.158.refs_2_), custom_call_target="tpu_custom_call" | custom-call | flops 3000000000 | bytes 10000 | tf_op jit(solution)/shard_map/add_parts/pallas_call | solution.py:755
  192.2 4.9 %all-to-all-start = ((bf16[4,1152,128]{2,1,0:T(8,128)(2,1)}), bf16[4,1152,128]{2,1,0:T(8,128)(2,1)S(1)}, u32[]{:S(2)}, u32[]{:S(2)}) async-start(bf16[4,1152,128]{2,1,0:T(8,128)(2,1)} %add_parts.1), calls=%async_computation.2 | async-start | bytes 2359296 | tf_op jit(solution)/shard_map/all_to_all | solution.py:1047
  201.7 2.2 collective-permute-done.40
  205.2 2.1 collective-permute-start.42
  207.3 2.4 collective-permute-start.43
  214.6 10.2 %collective-permute-done.42 = f32[2,48]{1,0:T(2,128)S(1)} collective-permute-done((f32[2,48]{1,0:T(2,128)S(1)}, f32[2,48]{1,0:T(2,128)S(1)}, u32[]{:S(2)}, u32[]{:S(2)}) %collective-permute-start.42) | collective-permute-done | bytes 416 | tf_op jit(solution)/shard_map/ppermute | solution.py:1062
  224.7 5.4 %collective-permute-done.43 = f32[2,48]{1,0:T(2,128)S(1)} collective-permute-done((f32[2,48]{1,0:T(2,128)S(1)}, f32[2,48]{1,0:T(2,128)S(1)}, u32[]{:S(2)}, u32[]{:S(2)}) %collective-permute-start.43) | collective-permute-done | bytes 416 | tf_op jit(solution)/shard_map/ppermute | solution.py:1062
  231.7 1.8 write_weights.1
  (207 shorter events, 56.4 us)
Async XLA Ops:
  7.2 164.0 %reduce-scatter.3.cloned.1.call-start = ((), (), s32[]{:S(2)}) async-start(), calls=%async_computation.3 | async-start | bytes 2654208 | tf_op jit(solution)/shard_map/reduce_scatter | solution.py:983
  9.7 17.1 %collective-permute-start = (bf16[2320,256]{1,0:T(8,128)(2,1)}, bf16[2320,256]{1,0:T(8,128)(2,1)S(1)}, u32[]{:S(2)}, u32[]{:S(2)}) collective-permute-start(bf16[2320,256]{1,0:T(8,128)(2,1)} %pack_windows.1.refs_4_.refs_13_.refs_6_.refs_2_), channel_id=1, source_target_pairs={{0,16},{16,0},{1,17},{17,1},{2,18},{18,2},{3,19},{19,3},{4,20},{20... | collective-permute-start | bytes 3563528 | tf_op jit(solution)/shard_map/ppermute | solution.py:962
  26.9 23.8 %collective-permute-start.2 = (bf16[1,768,2048]{2,1,0:T(8,128)(2,1)}, bf16[1,768,2048]{2,1,0:T(8,128)(2,1)}, u32[]{:S(2)}, u32[]{:S(2)}) collective-permute-start(bf16[1,768,2048]{2,1,0:T(8,128)(2,1)} %refs_6_.5), channel_id=1, source_target_pairs={{0,16},{16,0},{1,17},{17,1},{2,18},{18,2},{3,19},{19,3},{4,20},{20... | collective-permute-start | bytes 9437192 | tf_op jit(solution)/shard_map/ppermute | solution.py:962
  27.0 23.7 %collective-permute-start.3 = (bf16[1,768,2048]{2,1,0:T(8,128)(2,1)}, bf16[1,768,2048]{2,1,0:T(8,128)(2,1)}, u32[]{:S(2)}, u32[]{:S(2)}) collective-permute-start(bf16[1,768,2048]{2,1,0:T(8,128)(2,1)} %refs_8_.10), channel_id=1, source_target_pairs={{0,16},{16,0},{1,17},{17,1},{2,18},{18,2},{3,19},{19,3},{4,20},{20... | collective-permute-start | bytes 9437192 | tf_op jit(solution)/shard_map/ppermute | solution.py:962
  27.5 23.2 %collective-permute-start.4 = (bf16[1,2048,768]{2,1,0:T(8,128)(2,1)}, bf16[1,2048,768]{2,1,0:T(8,128)(2,1)}, u32[]{:S(2)}, u32[]{:S(2)}) collective-permute-start(bf16[1,2048,768]{2,1,0:T(8,128)(2,1)} %refs_10_.10), channel_id=1, source_target_pairs={{0,16},{16,0},{1,17},{17,1},{2,18},{18,2},{3,19},{19,3},{4,20},{20... | collective-permute-start | bytes 9437192 | tf_op jit(solution)/shard_map/ppermute | solution.py:962
  27.6 23.1 %collective-permute-start.1 = (bf16[1,768,768]{2,1,0:T(8,128)(2,1)S(1)}, bf16[1,768,768]{2,1,0:T(8,128)(2,1)}, u32[]{:S(2)}, u32[]{:S(2)}) collective-permute-start(bf16[1,768,768]{2,1,0:T(8,128)(2,1)S(1)} %copy-done.15), channel_id=1, source_target_pairs={{0,16},{16,0},{1,17},{17,1},{2,18},{18,2},{3,19},{19,3},{4,20},{20... | collective-permute-start | bytes 3538952 | tf_op jit(solution)/shard_map/ppermute | solution.py:962
  50.7 21.1 %collective-permute-start.5 = (bf16[160,768]{1,0:T(8,128)(2,1)S(1)}, bf16[160,768]{1,0:T(8,128)(2,1)S(1)}, u32[]{:S(2)}, u32[]{:S(2)}) collective-permute-start(bf16[160,768]{1,0:T(8,128)(2,1)S(1)} %dynamic-slice_bitcast_fusion.refs_4_), channel_id=1, source_target_pairs={{0,1},{1,0},{2,3},{3,2},{4,5},{5,4},{6,7},{7,6},{8,9},{9,8},{10,11... | collective-permute-start | bytes 737288 | tf_op jit(solution)/shard_map/ppermute | solution.py:966
  51.5 20.2 %collective-permute-start.6 = (bf16[160,768]{1,0:T(8,128)(2,1)S(1)}, bf16[160,768]{1,0:T(8,128)(2,1)S(1)}, u32[]{:S(2)}, u32[]{:S(2)}) collective-permute-start(bf16[160,768]{1,0:T(8,128)(2,1)S(1)} %dynamic-slice_bitcast_fusion.refs_4_), channel_id=1, source_target_pairs={{0,2},{1,3},{2,0},{3,1},{4,6},{5,7},{6,4},{7,5},{8,10},{9,11},{10,... | collective-permute-start | bytes 737288 | tf_op jit(solution)/shard_map/ppermute | solution.py:966
  52.8 19.0 %collective-permute-start.7 = (bf16[160,768]{1,0:T(8,128)(2,1)S(1)}, bf16[160,768]{1,0:T(8,128)(2,1)S(1)}, u32[]{:S(2)}, u32[]{:S(2)}) collective-permute-start(bf16[160,768]{1,0:T(8,128)(2,1)S(1)} %dynamic-slice_bitcast_fusion.refs_4_), channel_id=1, source_target_pairs={{0,3},{1,2},{2,1},{3,0},{4,7},{5,6},{6,5},{7,4},{8,11},{9,10},{10,... | collective-permute-start | bytes 737288 | tf_op jit(solution)/shard_map/ppermute | solution.py:966
  54.2 17.6 %collective-permute-start.8 = (bf16[1,768,768]{2,1,0:T(8,128)(2,1)S(1)}, bf16[1,768,768]{2,1,0:T(8,128)(2,1)S(1)}, u32[]{:S(2)}, u32[]{:S(2)}) collective-permute-start(bf16[1,768,768]{2,1,0:T(8,128)(2,1)S(1)} %copy-done.16), channel_id=1, source_target_pairs={{0,16},{16,0},{1,17},{17,1},{2,18},{18,2},{3,19},{19,3},{4,20},{20... | collective-permute-start | bytes 3538952 | tf_op jit(solution)/shard_map/ppermute | solution.py:962
  54.3 17.6 %collective-permute-start.9 = (bf16[1,768,768]{2,1,0:T(8,128)(2,1)}, bf16[1,768,768]{2,1,0:T(8,128)(2,1)}, u32[]{:S(2)}, u32[]{:S(2)}) collective-permute-start(bf16[1,768,768]{2,1,0:T(8,128)(2,1)} %refs_10_.11), channel_id=1, source_target_pairs={{0,16},{16,0},{1,17},{17,1},{2,18},{18,2},{3,19},{19,3},{4,20},{20... | collective-permute-start | bytes 3538952 | tf_op jit(solution)/shard_map/ppermute | solution.py:962
  94.4 31.9 %collective-permute-start.25 = (bf16[1,768,768]{2,1,0:T(8,128)(2,1)S(1)}, bf16[1,768,768]{2,1,0:T(8,128)(2,1)S(1)}, u32[]{:S(2)}, u32[]{:S(2)}) collective-permute-start(bf16[1,768,768]{2,1,0:T(8,128)(2,1)S(1)} %copy-done.17), channel_id=1, source_target_pairs={{0,16},{16,0},{1,17},{17,1},{2,18},{18,2},{3,19},{19,3},{4,20},{20... | collective-permute-start | bytes 3538952 | tf_op jit(solution)/shard_map/ppermute | solution.py:962
  109.1 16.3 %collective-permute-start.19 = (bf16[160,576]{1,0:T(8,128)(2,1)}, bf16[160,576]{1,0:T(8,128)(2,1)S(1)}, u32[]{:S(2)}, u32[]{:S(2)}) collective-permute-start(bf16[160,576]{1,0:T(8,128)(2,1)} %get-tuple-element.125.refs_15_), channel_id=1, source_target_pairs={{0,1},{1,0},{2,3},{3,2},{4,5},{5,4},{6,7},{7,6},{8,9},{9,8},{10,11... | collective-permute-start | bytes 552968 | tf_op jit(solution)/shard_map/ppermute | solution.py:966
  110.0 15.5 %collective-permute-start.20 = (bf16[160,576]{1,0:T(8,128)(2,1)}, bf16[160,576]{1,0:T(8,128)(2,1)S(1)}, u32[]{:S(2)}, u32[]{:S(2)}) collective-permute-start(bf16[160,576]{1,0:T(8,128)(2,1)} %get-tuple-element.126.refs_16_), channel_id=1, source_target_pairs={{0,2},{1,3},{2,0},{3,1},{4,6},{5,7},{6,4},{7,5},{8,10},{9,11},{10,... | collective-permute-start | bytes 552968 | tf_op jit(solution)/shard_map/ppermute | solution.py:966
  125.5 87.7 %reduce-scatter.5.cloned.1.call-start = ((), (), s32[]{:S(2)}) async-start(), calls=%async_computation.4 | async-start | bytes 2654208 | tf_op jit(solution)/shard_map/reduce_scatter | solution.py:983
  131.9 15.0 %collective-permute-start.29 = (bf16[160,768]{1,0:T(8,128)(2,1)}, bf16[160,768]{1,0:T(8,128)(2,1)S(1)}, u32[]{:S(2)}, u32[]{:S(2)}) collective-permute-start(bf16[160,768]{1,0:T(8,128)(2,1)} %get-tuple-element.136.refs_1_.refs_2_), channel_id=1, source_target_pairs={{0,1},{1,0},{2,3},{3,2},{4,5},{5,4},{6,7},{7,6},{8,9},{9,8},{10,11... | collective-permute-start | bytes 737288 | tf_op jit(solution)/shard_map/ppermute | solution.py:966
  132.8 15.5 %collective-permute-start.30 = (bf16[160,768]{1,0:T(8,128)(2,1)}, bf16[160,768]{1,0:T(8,128)(2,1)S(1)}, u32[]{:S(2)}, u32[]{:S(2)}) collective-permute-start(bf16[160,768]{1,0:T(8,128)(2,1)} %get-tuple-element.136.refs_1_.refs_2_), channel_id=1, source_target_pairs={{0,2},{1,3},{2,0},{3,1},{4,6},{5,7},{6,4},{7,5},{8,10},{9,11},{10,... | collective-permute-start | bytes 737288 | tf_op jit(solution)/shard_map/ppermute | solution.py:966
  187.9 16.2 %collective-permute-start.36 = (bf16[160,768]{1,0:T(8,128)(2,1)S(1)}, bf16[160,768]{1,0:T(8,128)(2,1)S(1)}, u32[]{:S(2)}, u32[]{:S(2)}) collective-permute-start(bf16[160,768]{1,0:T(8,128)(2,1)S(1)} %broadcast_select_fusion), channel_id=1, source_target_pairs={{0,16},{16,0},{1,17},{17,1},{2,18},{18,2},{3,19},{19,3},{4,20},{20... | collective-permute-start | bytes 737288 | tf_op jit(solution)/shard_map/ppermute | solution.py:962
  192.2 38.5 %all-to-all-start = ((bf16[4,1152,128]{2,1,0:T(8,128)(2,1)}), bf16[4,1152,128]{2,1,0:T(8,128)(2,1)S(1)}, u32[]{:S(2)}, u32[]{:S(2)}) async-start(bf16[4,1152,128]{2,1,0:T(8,128)(2,1)} %add_parts.1), calls=%async_computation.2 | async-start | bytes 2359296 | tf_op jit(solution)/shard_map/all_to_all | solution.py:1047
  205.2 19.5 %collective-permute-start.42 = (f32[2,48]{1,0:T(2,128)S(1)}, f32[2,48]{1,0:T(2,128)S(1)}, u32[]{:S(2)}, u32[]{:S(2)}) collective-permute-start(f32[2,48]{1,0:T(2,128)S(1)} %get-tuple-element.183), channel_id=1, source_target_pairs={{0,4},{4,8},{8,12},{12,0},{1,5},{5,9},{9,13},{13,1},{2,6},{6,10},{... | collective-permute-start | bytes 1160 | tf_op jit(solution)/shard_map/ppermute | solution.py:1062
  207.3 22.9 %collective-permute-start.43 = (f32[2,48]{1,0:T(2,128)S(1)}, f32[2,48]{1,0:T(2,128)S(1)}, u32[]{:S(2)}, u32[]{:S(2)}) collective-permute-start(f32[2,48]{1,0:T(2,128)S(1)} %get-tuple-element.185), channel_id=1, source_target_pairs={{0,8},{4,12},{8,0},{12,4},{1,9},{5,13},{9,1},{13,5},{2,10},{6,14},... | collective-permute-start | bytes 1160 | tf_op jit(solution)/shard_map/ppermute | solution.py:1062
  209.6 20.5 %collective-permute-start.44 = (f32[2,48]{1,0:T(2,128)S(1)}, f32[2,48]{1,0:T(2,128)S(1)}, u32[]{:S(2)}, u32[]{:S(2)}) collective-permute-start(f32[2,48]{1,0:T(2,128)S(1)} %get-tuple-element.184), channel_id=1, source_target_pairs={{0,12},{4,0},{8,4},{12,8},{1,13},{5,1},{9,5},{13,9},{2,14},{6,2},{... | collective-permute-start | bytes 1160 | tf_op jit(solution)/shard_map/ppermute | solution.py:1062
  211.9 18.8 %collective-permute-start.46 = (bf16[1152,128]{1,0:T(8,128)(2,1)S(1)}, bf16[1152,128]{1,0:T(8,128)(2,1)S(1)}, u32[]{:S(2)}, u32[]{:S(2)}) collective-permute-start(bf16[1152,128]{1,0:T(8,128)(2,1)S(1)} %bitcast.55), channel_id=1, source_target_pairs={{0,16},{1,17},{2,18},{3,19},{4,20},{5,21},{6,22},{7,23},{8,24},{9,... | collective-permute-start | bytes 884744 | tf_op jit(solution)/shard_map/ppermute | solution.py:987
  213.3 17.4 %collective-permute-start.45 = (bf16[1152,128]{1,0:T(8,128)(2,1)}, bf16[1152,128]{1,0:T(8,128)(2,1)S(1)}, u32[]{:S(2)}, u32[]{:S(2)}) collective-permute-start(bf16[1152,128]{1,0:T(8,128)(2,1)} %bitcast.57), channel_id=1, source_target_pairs={{16,0},{17,1},{18,2},{19,3},{20,4},{21,5},{22,6},{23,7},{24,8},{25... | collective-permute-start | bytes 884744 | tf_op jit(solution)/shard_map/ppermute | solution.py:987
  (72 other events, 558.5 us)
Sparse Core Ops, SparseCore 0:
  125.6 36.6 reduce-scatter.2
  171.4 40.6 reduce-scatter.4

commit v4 on v3

--- a/solution.py
+++ b/solution.py
@@ -366,9 +366,9 @@
 
 def last_rows(
     mid_h, cotangent_h, mixed_h, windows_h, o_h, ffn_h,
-    output_h, normed_two_h, grad_after_h, grad_gain_h, blocks_h,
+    after_h, hidden_h, normed_two_h, grad_after_h, grad_gain_h, blocks_h,
     mid, cotangent, mixed, gains, w_o, w_g, w_u, w_d,
-    output, normed_two, grad_after, grad_gain, blocks, branch, hidden, sems,
+    after_out, normed_two, grad_after, grad_gain, blocks, branch, hidden, sems,
 ):
     core, seq = place()
     move = Mover(sems, core)
@@ -387,6 +387,8 @@
     scale = rms_scale(after)
     normed = after * scale
     low = (normed * gain).astype(bf16)
+    after_out[...] = after
+    move.send(after_out, after_h)
     normed_two[...] = low
     move.send(normed_two, normed_two_h)
     grad_low = cotangent[...]
@@ -399,6 +401,7 @@
         hidden[:, span] = (gate * jax.nn.sigmoid(gate) * up).astype(bf16)
         grad_gate, grad_up = ffn_back_chunk(gate, up, nt(grad_low, w_d[span, :]))
         grad_normed = grad_normed + nt(grad_gate, w_g[part]) + nt(grad_up, w_u[part])
+    move.send(hidden, hidden_h)
     grad_gain[...] = jnp.sum(grad_normed * normed, axis=0, keepdims=True)
     move.send(grad_gain, grad_gain_h)
     total = grad_low.astype(f32) + norm_back(grad_normed, gain, normed, scale)
@@ -406,7 +409,14 @@
     move.send(grad_after, grad_after_h)
     branch[...] = total.astype(bf16)
     send_blocks(move, seq, branch, w_o, blocks, blocks_h)
-    output[...] = (after + nn(hidden[...], w_d[...])).astype(bf16)
+    move.finish()
+
+
+def last_output(after_h, hidden_h, d_h, output_h, after, hidden, w_d, output, sems):
+    core, _ = place()
+    move = Mover(sems, core)
+    wait(move.fetch_all((after_h, hidden_h), (after, hidden)) + [move.fetch_layer(1, d_h[0].at[0], d_h[1].at[0], w_d)])
+    output[...] = (after[...] + nn(hidden[...], w_d[...])).astype(bf16)
     move.send(output, output_h)
     move.finish()
 
@@ -831,16 +841,31 @@
     return call(
         last_rows,
         args,
-        [shape(*ROW), shape(*ROW), shape(*ROW, dtype=f32), shape(1, DIM, dtype=f32), [shape(*BRANCH)] * 4],
+        [
+            shape(*ROW, dtype=f32), shape(ROWS, FF), shape(*ROW), shape(*ROW, dtype=f32),
+            shape(1, DIM, dtype=f32), [shape(*BRANCH)] * 4,
+        ],
         [
             vm(*ROW), vm(*ROW), [vm(PACKED_ROWS, 128)] * 4, GAINS, *WEIGHTS,
-            vm(*ROW), vm(*ROW), vm(*ROW, dtype=f32), vm(1, DIM, dtype=f32), [vm(*BRANCH)] * 4,
+            vm(*ROW, dtype=f32), vm(*ROW), vm(*ROW, dtype=f32), vm(1, DIM, dtype=f32), [vm(*BRANCH)] * 4,
             vm(*ROW), vm(ROWS, FF), sems(32),
         ],
         11,
         "last_rows",
         after,
     )
+
+
+def call_last_output(*args, after=()):
+    return call(
+        last_output,
+        args,
+        [shape(*ROW)],
+        [vm(*ROW, dtype=f32), vm(ROWS, FF), vm(FF, DIM), vm(*ROW), sems(4)],
+        4,
+        "last_output",
+        after,
+    )[0]
 
 
 def call_first_rows_back(*args, after=()):
@@ -1013,7 +1038,7 @@
     qkv = (q_pair, k_pair, (w_value, swap(later(w_value, cotangent_all, q_pair[1]))))
     mixed_rows = exchanged(later(mixed_blocks, cotangent_all[1:], q_pair[1], k_pair[1]))
     mixed_1 = gathered(later(packed_1, mixed_rows[1]))
-    output, normed_two_1, grad_after_1, gain_ffn_1, grad_blocks_1 = call_last_rows(
+    after_1, hidden_1, normed_two_1, grad_after_1, gain_ffn_1, grad_blocks_1 = call_last_rows(
         mid, out_cotangent, mixed_rows, windows, o_pair, ffn
     )
     grad_mixed_1 = exchanged(later(grad_blocks_1, mixed_1))
@@ -1068,7 +1093,8 @@
         other = swap(jnp.where(is_first, of_second, of_first))
         return jnp.where(is_first, mine, other), jnp.where(is_first, other, mine)
 
-    section_outputs = jnp.stack(sort(*later((mid, output), grad_qkv_0[0])))[None]
+    output = call_last_output(after_1, hidden_1, ffn[2], after=(added_a,))
+    section_outputs = jnp.stack(sort(mid, output))[None]
     input_grads = jnp.stack(sort(grad_first, grad_mid))[None]
     g_query, g_key, g_value, g_output, g_gate, g_up, g_down = call_write_weights(
         groups, sum_f0, sum_f1, sums_a, give(sum_f0, 1), give(sum_f1, 0)

time: 245 us -> 253 us (1.033)
  Pallas kernels: 109 us -> 112 us
  waiting for transfers between devices: 22.2 us -> 25.2 us
    ppermute x3, waiting for transfers between devices: 15.6 us -> 20 us  [on_device(): lax.ppermute(part, 'dp', [(group, (group + offset) % groups) for group in...]
    pallas_call x15 -> x16, Pallas kernels: 109 us -> 112 us  [call(): pl.pallas_call(kernel, out_shape=out_leaves, in_specs=[spec(leaf) for lea...]
    unnamed x92 -> x90, local copies, waits for them, and re-layouts: 7.01 us -> 6.47 us
  transfers between devices with their start and end apart: 50 -> 50, of which waited for: 8 -> 7; matrix products, arithmetic and copies ran while one was open for 1% -> 2% of each run, Pallas kernels for 43% -> 43%
where the time goes in v4:
time: 253 us; the launch traced here: 248 us
  Pallas kernels  112 us (44%)
  starting transfers between devices  53 us (21%)
  blocking collectives  31.8 us (13%)
  waiting for transfers between devices  25.2 us (10%)
  between operations  15.2 us (6%)
  local copies, waits for them, and re-layouts  7.19 us (3%)
  other arithmetic  4.45 us (2%)
    pallas_call x16, Pallas kernels, call(): pl.pallas_call(kernel, out_shape=out_leaves, in_specs=[spec(leaf) for lea...  112 us
    ppermute x30, starting transfers between devices, to_partner(): lax.ppermute(value, 'seq', [(part, part ^ offset) for part in range(PARTS)])  35.4 us
    ppermute x3, waiting for transfers between devices, on_device(): lax.ppermute(part, 'dp', [(group, (group + offset) % groups) for group in...  20 us
    all_gather x1, blocking collectives, on_device(): x_all = lax.all_gather(later(inputs, windows[0]), 'seq', axis=0, tiled=True)  16.6 us
    all_gather x1, blocking collectives, on_device(): mixed_0 = lax.all_gather(packed_0, 'seq', axis=0)  15.2 us
    unnamed x90, local copies, waits for them, and re-layouts  6.47 us
    ppermute x3, starting transfers between devices, on_device(): lax.ppermute(part, 'dp', [(group, (group + offset) % groups) for group in...  5.89 us
  transfers between devices with their start and end apart: 50, of which 7 were waited for; matrix products, arithmetic and copies ran while one was open for 2% of the time, Pallas kernels for 43%

profile of v4, /device:TPU:0, one launch (start us, length us, event | category | flops | bytes accessed | tf_op | source)
XLA Modules:
  0.0 248.4 jit_solution(8061699473485047258)
XLA Ops:
  7.2 2.5 pack_windows.1.refs_4_.refs_13_.refs_6_.refs_2_
  10.3 16.6 %all_gather.9.refs_0_ = bf16[640,768]{1,0:T(8,128)(2,1)} all-gather(bf16[160,768]{1,0:T(8,128)(2,1)S(1)} %dynamic-slice_bitcast_fusion.1.refs_4_), channel_id=1, replica_groups=mesh['section'=2,'dp'=4,'seq'=4] {'seq'}, dimensions={0}, use_global_device_ids=true | all-gather | bytes 1228800 | tf_op jit(solution)/shard_map/all_gather | solution.py:1027
  28.0 7.5 %first_attention.1 = (bf16[640,768]{1,0:T(8,128)(2,1)}, bf16[3,3,640,64]{3,2,1,0:T(8,128)(2,1)}, bf16[960,128]{1,0:T(8,128)(2,1)}) custom-call(bf16[640,768]{1,0:T(8,128)(2,1)} %all_gather.9.refs_0_, s32[2]{0:T(128)} %refs_4_.8, f32[640,128]{1,0:T(8,128)} %constant.59.clone.refs_2_.refs_3_.refs_5_, f32[640,128]{1,0:T(8,128)} %constant.60.clone.refs_3_.refs_4_.refs_6_, ...), custom_call_target="tpu_custom_call" | custom-call | flops 10000000000 | bytes 10000 | tf_op jit(solution)/shard_map/first_attention/pallas_call | solution.py:765
  35.5 15.2 %all-gather = bf16[3840,128]{1,0:T(8,128)(2,1)} all-gather(bf16[960,128]{1,0:T(8,128)(2,1)} %get-tuple-element.93), channel_id=2, replica_groups=mesh['section'=2,'dp'=4,'seq'=4] {'seq'}, dimensions={0}, use_global_device_ids=true | all-gather | bytes 1228800 | tf_op jit(solution)/shard_map/all_gather | solution.py:1031
  54.8 17.0 %middle.1 = (f32[160,768]{1,0:T(8,128)}, bf16[640,768]{1,0:T(8,128)(2,1)}, bf16[640,2048]{1,0:T(8,128)(2,1)}, bf16[160,768]{1,0:T(8,128)(2,1)}, bf16[640,768]{1,...) custom-call(bf16[640,768]{1,0:T(8,128)(2,1)} %all_gather.9.refs_0_, ...), custom_call_target="tpu_custom_call" | custom-call | flops 20000000000 | bytes 10000 | tf_op jit(solution)/shard_map/middle/pallas_call | solution.py:765
  80.5 9.7 %last_rows.1 = (f32[160,768]{1,0:T(8,128)}, bf16[160,2048]{1,0:T(8,128)(2,1)}, bf16[160,768]{1,0:T(8,128)(2,1)}, f32[160,768]{1,0:T(8,128)}, f32[1,768]{1,0:T(1,...) custom-call(bf16[160,768]{1,0:T(8,128)(2,1)} %get-tuple-element.98.r, ...), custom_call_target="tpu_custom_call" | custom-call | flops 11000000512 | bytes 10000 | tf_op jit(solution)/shard_map/last_rows/pallas_call | solution.py:765
  93.9 1.6 collective-permute-done.16.refs_1_.refs_23_
  99.6 9.1 %attention_back.2 = (bf16[160,576]{1,0:T(8,128)(2,1)}, bf16[160,576]{1,0:T(8,128)(2,1)}, bf16[160,576]{1,0:T(8,128)(2,1)}, bf16[160,576]{1,0:T(8,128)(2,1)}) custom-call(bf16[160,384]{1,0:T(8,128)(2,1)} %get-tuple-element.120.refs_0_.refs_22_, bf16[160,384]{1,0:T(8,128)(2,1)} %copy-done.38, bf16[160,384]{1,0:T(8,128)(2,1)} %collective-permute-done.17.refs_2_.refs_24_, ...), custom_call_target="tpu_custom_call" | custom-call | flops 11000000512 | bytes 10000 | tf_op jit(solution)/shard_map/attention_back/pallas_call | solution.py:765
  113.0 11.9 %ffn_weights_grad.2 = bf16[4,2,1152,128]{3,2,1,0:T(8,128)(2,1)} custom-call(bf16[160,768]{1,0:T(8,128)(2,1)} %get-tuple-element.130.refs_0_, bf16[160,768]{1,0:T(8,128)(2,1)} %copy-done.26, bf16[160,768]{1,0:T(8,128)(2,1)} %copy-done.27, bf16[160,768]{1,0:T(8,128)(2,1)} %copy-done.29, bf16[160,768]{1,0:T(8,128)(2,1)} %copy-done.7, ...), custom_call_target="tpu_custom_call" | custom-call | flops 15000000512 | bytes 10000 | tf_op jit(solution)/shard_map/ffn_weights_grad/pallas_call | solution.py:765
  126.3 4.6 %input_back.2 = (bf16[160,768]{1,0:T(8,128)(2,1)}, f32[1,768]{1,0:T(1,128)}) custom-call(bf16[160,576]{1,0:T(8,128)(2,1)} %get-tuple-element.131.refs_14_.refs_0_, bf16[160,576]{1,0:T(8,128)(2,1)} %copy-done.35, bf16[160,576]{1,0:T(8,128)(2,1)} %copy-done.36, bf16[160,576]{1,0:T(8,128)(2,1)} %copy-done.37, ...), custom_call_target="tpu_custom_call" | custom-call | flops 10000000000 | bytes 10000 | tf_op jit(solution)/shard_map/input_back/pallas_call | solution.py:765
  134.5 9.2 %first_rows_back.1 = (f32[160,768]{1,0:T(8,128)}, f32[1,768]{1,0:T(1,128)}, bf16[160,384]{1,0:T(8,128)(2,1)}, bf16[160,384]{1,0:T(8,128)(2,1)}, bf16[160,384]{1,0:T(8,128)(2,1)}, /*index=5*/bf16[160,384]{1,0:T(8,128)(2,1)}) custom-call(f32[160,768]{1,0:T(8,128)} %get-tuple-element.113.refs_0_, bf16[160,768]{1,0:T(8,128)(2,1)} %get-tuple-element.137.refs_1_.refs_2_, ...), custom_call_target="tpu_custom_call" | custom-call | flops 10000000000 | bytes 10000 | tf_op jit(solution)/shard_map/first_rows_back/pallas_call | solution.py:765
  148.1 8.8 %ffn_weights_grad.3 = bf16[4,2,1152,128]{3,2,1,0:T(8,128)(2,1)} custom-call(bf16[640,768]{1,0:T(8,128)(2,1)} %get-tuple-element.142.refs_0_, bf16[640,2048]{1,0:T(8,128)(2,1)} %get-tuple-element.143.refs_1_, bf16[160,768]{1,0:T(8,128)(2,1)} %get-tuple-element.137.refs_1_.refs_2_, bf16[160,768]{1,0:T(8,128)(2,1)} %copy-done.28, bf16[160,768]{1,0:T(8,128)(2,1)} %copy-done.30, ...), custom_call_target="tpu_custom_call" | custom-call | flops 15000000512 | bytes 10000 | tf_op jit(solution)/shard_map/ffn_weights_grad/pallas_call | solution.py:765
  157.6 9.1 %attention_back.3 = (bf16[160,576]{1,0:T(8,128)(2,1)}, bf16[160,576]{1,0:T(8,128)(2,1)}, bf16[160,576]{1,0:T(8,128)(2,1)}, bf16[160,576]{1,0:T(8,128)(2,1)}) custom-call(bf16[160,384]{1,0:T(8,128)(2,1)} %get-tuple-element.145.refs_0_.refs_9_, bf16[160,384]{1,0:T(8,128)(2,1)} %copy-done.39, bf16[160,384]{1,0:T(8,128)(2,1)} %copy-done.40, ...), custom_call_target="tpu_custom_call" | custom-call | flops 11000000512 | bytes 10000 | tf_op jit(solution)/shard_map/attention_back/pallas_call | solution.py:765
  170.2 4.6 %attention_weights_grad.2.refs_26_ = bf16[4,1152,128]{2,1,0:T(8,128)(2,1)} custom-call(bf16[640,768]{1,0:T(8,128)(2,1)} %get-tuple-element.112.refs_0_, bf16[160,576]{1,0:T(8,128)(2,1)} %get-tuple-element.150.refs_1_.refs_26_.refs_0_, bf16[160,576]{1,0:T(8,128)(2,1)} %get-tuple-element.151.refs_2_, bf16[160,576]{1,0:T(8,128)(2,1)} %get-tuple-element.152.refs_3_, ...), custom_call_target="tpu_custom_call" | custom-call | flops 8000000000 | bytes 10000 | tf_op jit(solution)/shard_map/attention_weights_grad/pallas_call | solution.py:765
  174.9 5.0 %attention_weights_grad.3.refs_14_.refs_0_ = bf16[4,1152,128]{2,1,0:T(8,128)(2,1)} custom-call(bf16[640,768]{1,0:T(8,128)(2,1)} %get-tuple-element.112.refs_0_, bf16[160,576]{1,0:T(8,128)(2,1)} %get-tuple-element.150.refs_1_.refs_26_.refs_0_, bf16[160,576]{1,0:T(8,128)(2,1)} %get-tuple-element.151.refs_2_, bf16[160,576]{1,0:T(8,128)(2,1)} %get-tuple-element.152.refs_3_, ...), custom_call_target="tpu_custom_call" | custom-call | flops 8000000000 | bytes 10000 | tf_op jit(solution)/shard_map/attention_weights_grad/pallas_call | solution.py:765
  181.6 4.6 %input_back.3 = (bf16[160,768]{1,0:T(8,128)(2,1)}, f32[1,768]{1,0:T(1,128)}) custom-call(bf16[160,576]{1,0:T(8,128)(2,1)} %get-tuple-element.150.refs_1_.refs_26_.refs_0_, bf16[160,576]{1,0:T(8,128)(2,1)} %copy-done.32, bf16[160,576]{1,0:T(8,128)(2,1)} %copy-done.33, bf16[160,576]{1,0:T(8,128)(2,1)} %copy-done.34, bf16[160,768]{1,0:T(8,128)(2,1)} %copy-done.4, ...), custom_call_target="tpu_custom_call" | custom-call | flops 10000000000 | bytes 10000 | tf_op jit(solution)/shard_map/input_back/pallas_call | solution.py:765
  190.9 2.5 %add_parts.1.refs_4_ = bf16[4,1152,128]{2,1,0:T(8,128)(2,1)} custom-call(bf16[4,1152,128]{2,1,0:T(8,128)(2,1)} %attention_weights_grad.3.refs_14_.refs_0_, bf16[4,1152,128]{2,1,0:T(8,128)(2,1)} %copy-done.19, bf16[160,768]{1,0:T(8,128)(2,1)} %get-tuple-element.157.refs_2_), custom_call_target="tpu_custom_call" | custom-call | flops 3000000000 | bytes 10000 | tf_op jit(solution)/shard_map/add_parts/pallas_call | solution.py:765
  198.0 4.9 %all-to-all-start = ((bf16[4,1152,128]{2,1,0:T(8,128)(2,1)}), bf16[4,1152,128]{2,1,0:T(8,128)(2,1)S(1)}, u32[]{:S(2)}, u32[]{:S(2)}) async-start(bf16[4,1152,128]{2,1,0:T(8,128)(2,1)} %add_parts.1.refs_4_), calls=%async_computation.2 | async-start | bytes 2359296 | tf_op jit(solution)/shard_map/all_to_all | solution.py:1072
  203.0 3.7 %last_output.1 = bf16[160,768]{1,0:T(8,128)(2,1)} custom-call(f32[160,768]{1,0:T(8,128)} %get-tuple-element.110.refs_0_, bf16[160,2048]{1,0:T(8,128)(2,1)} %get-tuple-element.111.refs_1_, bf16[1,2048,768]{2,1,0:T(8,128)(2,1)} %refs_2_.6, bf16[1,2048,768]{2,1,0:T(8,128)(2,1)} %collective-permute-done.4.refs_12_.refs_15_.refs_13_.refs_11_.refs_3_, ...), custom_call_target="tpu_custom_call" | custom-call | flops 4000000000 | bytes 10000 | tf_op jit(solution)/shard_map/last_output/pallas_call | solution.py:765
  206.8 2.0 collective-permute-start.42
  208.8 2.4 collective-permute-start.43
  213.7 14.7 %collective-permute-done.42 = f32[2,48]{1,0:T(2,128)S(1)} collective-permute-done((f32[2,48]{1,0:T(2,128)S(1)}, f32[2,48]{1,0:T(2,128)S(1)}, u32[]{:S(2)}, u32[]{:S(2)}) %collective-permute-start.42) | collective-permute-done | bytes 416 | tf_op jit(solution)/shard_map/ppermute | solution.py:1087
  228.4 5.3 %collective-permute-done.43 = f32[2,48]{1,0:T(2,128)S(1)} collective-permute-done((f32[2,48]{1,0:T(2,128)S(1)}, f32[2,48]{1,0:T(2,128)S(1)}, u32[]{:S(2)}, u32[]{:S(2)}) %collective-permute-start.43) | collective-permute-done | bytes 416 | tf_op jit(solution)/shard_map/ppermute | solution.py:1087
  239.5 1.8 write_weights.1
  (206 shorter events, 58.9 us)
Async XLA Ops:
  7.2 167.7 %reduce-scatter.3.cloned.1.call-start = ((), (), s32[]{:S(2)}) async-start(), calls=%async_computation.3 | async-start | bytes 2654208 | tf_op jit(solution)/shard_map/reduce_scatter | solution.py:1008
  9.7 17.2 %collective-permute-start = (bf16[2320,256]{1,0:T(8,128)(2,1)}, bf16[2320,256]{1,0:T(8,128)(2,1)S(1)}, u32[]{:S(2)}, u32[]{:S(2)}) collective-permute-start(bf16[2320,256]{1,0:T(8,128)(2,1)} %pack_windows.1.refs_4_.refs_13_.refs_6_.refs_2_), channel_id=1, source_target_pairs={{0,16},{16,0},{1,17},{17,1},{2,18},{18,2},{3,19},{19,3},{4,20},{20... | collective-permute-start | bytes 3563528 | tf_op jit(solution)/shard_map/ppermute | solution.py:987
  26.9 23.8 %collective-permute-start.4 = (bf16[1,2048,768]{2,1,0:T(8,128)(2,1)}, bf16[1,2048,768]{2,1,0:T(8,128)(2,1)}, u32[]{:S(2)}, u32[]{:S(2)}) collective-permute-start(bf16[1,2048,768]{2,1,0:T(8,128)(2,1)} %refs_2_.6), channel_id=1, source_target_pairs={{0,16},{16,0},{1,17},{17,1},{2,18},{18,2},{3,19},{19,3},{4,20},{20... | collective-permute-start | bytes 9437192 | tf_op jit(solution)/shard_map/ppermute | solution.py:987
  27.0 23.7 %collective-permute-start.2 = (bf16[1,768,2048]{2,1,0:T(8,128)(2,1)}, bf16[1,768,2048]{2,1,0:T(8,128)(2,1)}, u32[]{:S(2)}, u32[]{:S(2)}) collective-permute-start(bf16[1,768,2048]{2,1,0:T(8,128)(2,1)} %refs_6_.5), channel_id=1, source_target_pairs={{0,16},{16,0},{1,17},{17,1},{2,18},{18,2},{3,19},{19,3},{4,20},{20... | collective-permute-start | bytes 9437192 | tf_op jit(solution)/shard_map/ppermute | solution.py:987
  27.5 23.3 %collective-permute-start.3 = (bf16[1,768,2048]{2,1,0:T(8,128)(2,1)}, bf16[1,768,2048]{2,1,0:T(8,128)(2,1)}, u32[]{:S(2)}, u32[]{:S(2)}) collective-permute-start(bf16[1,768,2048]{2,1,0:T(8,128)(2,1)} %refs_8_.10), channel_id=1, source_target_pairs={{0,16},{16,0},{1,17},{17,1},{2,18},{18,2},{3,19},{19,3},{4,20},{20... | collective-permute-start | bytes 9437192 | tf_op jit(solution)/shard_map/ppermute | solution.py:987
  27.6 23.1 %collective-permute-start.1 = (bf16[1,768,768]{2,1,0:T(8,128)(2,1)S(1)}, bf16[1,768,768]{2,1,0:T(8,128)(2,1)}, u32[]{:S(2)}, u32[]{:S(2)}) collective-permute-start(bf16[1,768,768]{2,1,0:T(8,128)(2,1)S(1)} %copy-done.13), channel_id=1, source_target_pairs={{0,16},{16,0},{1,17},{17,1},{2,18},{18,2},{3,19},{19,3},{4,20},{20... | collective-permute-start | bytes 3538952 | tf_op jit(solution)/shard_map/ppermute | solution.py:987
  50.7 21.0 %collective-permute-start.5 = (bf16[160,768]{1,0:T(8,128)(2,1)S(1)}, bf16[160,768]{1,0:T(8,128)(2,1)S(1)}, u32[]{:S(2)}, u32[]{:S(2)}) collective-permute-start(bf16[160,768]{1,0:T(8,128)(2,1)S(1)} %dynamic-slice_bitcast_fusion.refs_4_), channel_id=1, source_target_pairs={{0,1},{1,0},{2,3},{3,2},{4,5},{5,4},{6,7},{7,6},{8,9},{9,8},{10,11... | collective-permute-start | bytes 737288 | tf_op jit(solution)/shard_map/ppermute | solution.py:991
  51.5 20.3 %collective-permute-start.6 = (bf16[160,768]{1,0:T(8,128)(2,1)S(1)}, bf16[160,768]{1,0:T(8,128)(2,1)S(1)}, u32[]{:S(2)}, u32[]{:S(2)}) collective-permute-start(bf16[160,768]{1,0:T(8,128)(2,1)S(1)} %dynamic-slice_bitcast_fusion.refs_4_), channel_id=1, source_target_pairs={{0,2},{1,3},{2,0},{3,1},{4,6},{5,7},{6,4},{7,5},{8,10},{9,11},{10,... | collective-permute-start | bytes 737288 | tf_op jit(solution)/shard_map/ppermute | solution.py:991
  52.8 19.0 %collective-permute-start.7 = (bf16[160,768]{1,0:T(8,128)(2,1)S(1)}, bf16[160,768]{1,0:T(8,128)(2,1)S(1)}, u32[]{:S(2)}, u32[]{:S(2)}) collective-permute-start(bf16[160,768]{1,0:T(8,128)(2,1)S(1)} %dynamic-slice_bitcast_fusion.refs_4_), channel_id=1, source_target_pairs={{0,3},{1,2},{2,1},{3,0},{4,7},{5,6},{6,5},{7,4},{8,11},{9,10},{10,... | collective-permute-start | bytes 737288 | tf_op jit(solution)/shard_map/ppermute | solution.py:991
  54.3 17.5 %collective-permute-start.8 = (bf16[1,768,768]{2,1,0:T(8,128)(2,1)S(1)}, bf16[1,768,768]{2,1,0:T(8,128)(2,1)S(1)}, u32[]{:S(2)}, u32[]{:S(2)}) collective-permute-start(bf16[1,768,768]{2,1,0:T(8,128)(2,1)S(1)} %copy-done.14), channel_id=1, source_target_pairs={{0,16},{16,0},{1,17},{17,1},{2,18},{18,2},{3,19},{19,3},{4,20},{20... | collective-permute-start | bytes 3538952 | tf_op jit(solution)/shard_map/ppermute | solution.py:987
  54.3 17.6 %collective-permute-start.9 = (bf16[1,768,768]{2,1,0:T(8,128)(2,1)}, bf16[1,768,768]{2,1,0:T(8,128)(2,1)}, u32[]{:S(2)}, u32[]{:S(2)}) collective-permute-start(bf16[1,768,768]{2,1,0:T(8,128)(2,1)} %refs_10_.11), channel_id=1, source_target_pairs={{0,16},{16,0},{1,17},{17,1},{2,18},{18,2},{3,19},{19,3},{4,20},{20... | collective-permute-start | bytes 3538952 | tf_op jit(solution)/shard_map/ppermute | solution.py:987
  93.9 31.3 %collective-permute-start.25 = (bf16[1,768,768]{2,1,0:T(8,128)(2,1)S(1)}, bf16[1,768,768]{2,1,0:T(8,128)(2,1)S(1)}, u32[]{:S(2)}, u32[]{:S(2)}) collective-permute-start(bf16[1,768,768]{2,1,0:T(8,128)(2,1)S(1)} %copy-done.15), channel_id=1, source_target_pairs={{0,16},{16,0},{1,17},{17,1},{2,18},{18,2},{3,19},{19,3},{4,20},{20... | collective-permute-start | bytes 3538952 | tf_op jit(solution)/shard_map/ppermute | solution.py:987
  97.5 14.8 %collective-permute-start.24 = (bf16[160,768]{1,0:T(8,128)(2,1)}, bf16[160,768]{1,0:T(8,128)(2,1)S(1)}, u32[]{:S(2)}, u32[]{:S(2)}) collective-permute-start(bf16[160,768]{1,0:T(8,128)(2,1)} %get-tuple-element.130.refs_0_), channel_id=1, source_target_pairs={{0,3},{1,2},{2,1},{3,0},{4,7},{5,6},{6,5},{7,4},{8,11},{9,10},{10,... | collective-permute-start | bytes 737288 | tf_op jit(solution)/shard_map/ppermute | solution.py:991
  108.7 16.1 %collective-permute-start.19 = (bf16[160,576]{1,0:T(8,128)(2,1)}, bf16[160,576]{1,0:T(8,128)(2,1)S(1)}, u32[]{:S(2)}, u32[]{:S(2)}) collective-permute-start(bf16[160,576]{1,0:T(8,128)(2,1)} %get-tuple-element.126.refs_15_), channel_id=1, source_target_pairs={{0,1},{1,0},{2,3},{3,2},{4,5},{5,4},{6,7},{7,6},{8,9},{9,8},{10,11... | collective-permute-start | bytes 552968 | tf_op jit(solution)/shard_map/ppermute | solution.py:991
  109.5 15.4 %collective-permute-start.20 = (bf16[160,576]{1,0:T(8,128)(2,1)}, bf16[160,576]{1,0:T(8,128)(2,1)S(1)}, u32[]{:S(2)}, u32[]{:S(2)}) collective-permute-start(bf16[160,576]{1,0:T(8,128)(2,1)} %get-tuple-element.127.refs_16_), channel_id=1, source_target_pairs={{0,2},{1,3},{2,0},{3,1},{4,6},{5,7},{6,4},{7,5},{8,10},{9,11},{10,... | collective-permute-start | bytes 552968 | tf_op jit(solution)/shard_map/ppermute | solution.py:991
  125.0 110.7 %reduce-scatter.5.cloned.1.call-start = ((), (), s32[]{:S(2)}) async-start(), calls=%async_computation.4 | async-start | bytes 2654208 | tf_op jit(solution)/shard_map/reduce_scatter | solution.py:1008
  130.9 14.9 %collective-permute-start.29 = (bf16[160,768]{1,0:T(8,128)(2,1)}, bf16[160,768]{1,0:T(8,128)(2,1)S(1)}, u32[]{:S(2)}, u32[]{:S(2)}) collective-permute-start(bf16[160,768]{1,0:T(8,128)(2,1)} %get-tuple-element.137.refs_1_.refs_2_), channel_id=1, source_target_pairs={{0,1},{1,0},{2,3},{3,2},{4,5},{5,4},{6,7},{7,6},{8,9},{9,8},{10,11... | collective-permute-start | bytes 737288 | tf_op jit(solution)/shard_map/ppermute | solution.py:991
  131.7 15.6 %collective-permute-start.30 = (bf16[160,768]{1,0:T(8,128)(2,1)}, bf16[160,768]{1,0:T(8,128)(2,1)S(1)}, u32[]{:S(2)}, u32[]{:S(2)}) collective-permute-start(bf16[160,768]{1,0:T(8,128)(2,1)} %get-tuple-element.137.refs_1_.refs_2_), channel_id=1, source_target_pairs={{0,2},{1,3},{2,0},{3,1},{4,6},{5,7},{6,4},{7,5},{8,10},{9,11},{10,... | collective-permute-start | bytes 737288 | tf_op jit(solution)/shard_map/ppermute | solution.py:991
  133.0 14.3 %collective-permute-start.31 = (bf16[160,768]{1,0:T(8,128)(2,1)}, bf16[160,768]{1,0:T(8,128)(2,1)S(1)}, u32[]{:S(2)}, u32[]{:S(2)}) collective-permute-start(bf16[160,768]{1,0:T(8,128)(2,1)} %get-tuple-element.137.refs_1_.refs_2_), channel_id=1, source_target_pairs={{0,3},{1,2},{2,1},{3,0},{4,7},{5,6},{6,5},{7,4},{8,11},{9,10},{10,... | collective-permute-start | bytes 737288 | tf_op jit(solution)/shard_map/ppermute | solution.py:991
  198.0 40.0 %all-to-all-start = ((bf16[4,1152,128]{2,1,0:T(8,128)(2,1)}), bf16[4,1152,128]{2,1,0:T(8,128)(2,1)S(1)}, u32[]{:S(2)}, u32[]{:S(2)}) async-start(bf16[4,1152,128]{2,1,0:T(8,128)(2,1)} %add_parts.1.refs_4_), calls=%async_computation.2 | async-start | bytes 2359296 | tf_op jit(solution)/shard_map/all_to_all | solution.py:1072
  206.8 21.7 %collective-permute-start.42 = (f32[2,48]{1,0:T(2,128)S(1)}, f32[2,48]{1,0:T(2,128)S(1)}, u32[]{:S(2)}, u32[]{:S(2)}) collective-permute-start(f32[2,48]{1,0:T(2,128)S(1)} %get-tuple-element.181), channel_id=1, source_target_pairs={{0,4},{4,8},{8,12},{12,0},{1,5},{5,9},{9,13},{13,1},{2,6},{6,10},{... | collective-permute-start | bytes 1160 | tf_op jit(solution)/shard_map/ppermute | solution.py:1087
  208.8 24.9 %collective-permute-start.43 = (f32[2,48]{1,0:T(2,128)S(1)}, f32[2,48]{1,0:T(2,128)S(1)}, u32[]{:S(2)}, u32[]{:S(2)}) collective-permute-start(f32[2,48]{1,0:T(2,128)S(1)} %get-tuple-element.183), channel_id=1, source_target_pairs={{0,8},{4,12},{8,0},{12,4},{1,9},{5,13},{9,1},{13,5},{2,10},{6,14},... | collective-permute-start | bytes 1160 | tf_op jit(solution)/shard_map/ppermute | solution.py:1087
  211.2 22.6 %collective-permute-start.44 = (f32[2,48]{1,0:T(2,128)S(1)}, f32[2,48]{1,0:T(2,128)S(1)}, u32[]{:S(2)}, u32[]{:S(2)}) collective-permute-start(f32[2,48]{1,0:T(2,128)S(1)} %get-tuple-element.182), channel_id=1, source_target_pairs={{0,12},{4,0},{8,4},{12,8},{1,13},{5,1},{9,5},{13,9},{2,14},{6,2},{... | collective-permute-start | bytes 1160 | tf_op jit(solution)/shard_map/ppermute | solution.py:1087
  213.6 23.4 %collective-permute-start.36 = (bf16[160,768]{1,0:T(8,128)(2,1)S(1)}, bf16[160,768]{1,0:T(8,128)(2,1)S(1)}, u32[]{:S(2)}, u32[]{:S(2)}) collective-permute-start(bf16[160,768]{1,0:T(8,128)(2,1)S(1)} %broadcast_select_fusion.2), channel_id=1, source_target_pairs={{0,16},{16,0},{1,17},{17,1},{2,18},{18,2},{3,19},{19,3},{4,20},{20... | collective-permute-start | bytes 737288 | tf_op jit(solution)/shard_map/ppermute | solution.py:987
  (71 other events, 560.8 us)
Sparse Core Ops, SparseCore 0:
  125.1 36.5 reduce-scatter.2
  175.1 39.9 reduce-scatter.4
